TPU v7x, 512 devices: a whole 4x8x8 slice. The times are simulated.
512 devices in a mesh: grp: 32 (over y, z_lo), tp: 16 (over x, z_hi, core).
Axes of the slice: x: 4, y: 8, z: 8 (z_hi: 2, z_lo: 4; z = z_hi * 4 + z_lo), core: 2. Of those that a mesh axis runs over, the one named last changes fastest.
Arguments:
- trainer_token_inputs: bfloat16 [8192, 16384], P('grp', 'tp'), may hold values from -6 to 6
- weighted_output_cotangents: bfloat16 [2, 512, 8192], P(None, 'tp', 'grp'), may hold values from -0.049804688 to 0.049804688
- adapter_down_master: float32 [2, 64, 16384], P(None, 'grp', 'tp'), may hold values from -0.046875 to 0.046875
- adapter_up_master: float32 [2, 512, 64], P(None, 'tp', 'grp'), may hold values from -0.4 to 0.4
- down_first_moment: float32 [2, 64, 16384], P(None, 'grp', 'tp'), may hold values from -0.3 to 0.3
- down_second_moment: float32 [2, 64, 16384], P(None, 'grp', 'tp'), may hold values from 0.01 to 0.2
- up_first_moment: float32 [2, 512, 64], P(None, 'tp', 'grp'), may hold values from -0.3 to 0.3
- up_second_moment: float32 [2, 512, 64], P(None, 'tp', 'grp'), may hold values from 0.01 to 0.2
- frozen_weights: bfloat16 [2, 16384, 512], P(None, 'tp'), may hold values from -0.046875 to 0.046875
- decode_step_inputs: bfloat16 [1024, 4, 16384], P('grp', None, 'tp'), may hold values from -6 to 6
- queries: bfloat16 [1024, 4, 8192], P(('grp', 'tp')), may hold values from -150 to 150
- rotated_key_cache: bfloat16 [1024, 4, 256, 128], P(('grp', 'tp')), may hold values from -5 to 5
- stored_value_cache: bfloat16 [1024, 4, 256, 128], P(('grp', 'tp')), may hold values from -6 to 6
- lengths: int32 [1024], P(('grp', 'tp')), may hold values from 64 to 256
Outputs:
- attended: float32 [1024, 4, 8192], P(('grp', 'tp'))
- new_keys: float32 [1024, 4, 512], P(('grp', 'tp'))
- new_values: float32 [1024, 4, 512], P(('grp', 'tp'))
- fresh_down_factors: float32 [2, 64, 16384], P(None, 'grp', 'tp')
- fresh_up_factors: float32 [2, 512, 64], P(None, 'tp', 'grp')
- fresh_down_first_moment: float32 [2, 64, 16384], P(None, 'grp', 'tp')
- fresh_down_second_moment: float32 [2, 64, 16384], P(None, 'grp', 'tp')
- fresh_up_first_moment: float32 [2, 512, 64], P(None, 'tp', 'grp')
- fresh_up_second_moment: float32 [2, 512, 64], P(None, 'tp', 'grp')
All inputs are finite; a program needn't handle non-finite values.
Results may differ from a plain program's by a relative error of at most 0.008.
Values may be sent and summed in bfloat16 or wider, within the bound.
No kernel may reach another device: no remote copies, remote signals or barrier semaphores. Data moves between devices by JAX's collectives and lax.ppermute only.
A program may use at most 64 MiB of HBM per device.

v0:
```python
import math

import jax
import jax.numpy as jnp
from jax import lax
from jax.sharding import PartitionSpec as P

OPT_STEP = 20


ADAPTER_SCALE = 2.0
LEARN_RATE = 0.001
WEIGHT_DECAY = 0.01
BETA_FIRST = 0.9
BETA_SECOND = 0.95
EPSILON = 1e-08
THETA = 500000.0
ROPE_FACTOR = 8.0
LOW_FACTOR = 1.0
HIGH_FACTOR = 4.0
INITIAL_CONTEXT = 8192.0
MASKED = -1e30


def rope_frequencies(head_size):
    half_head = head_size // 2
    exponent = jnp.arange(half_head, dtype=jnp.float32) * (2.0 / head_size)
    base_frequency = jnp.power(jnp.float32(THETA), -exponent)
    wavelength = 2.0 * math.pi / base_frequency
    smooth = (INITIAL_CONTEXT / wavelength - LOW_FACTOR) / (HIGH_FACTOR - LOW_FACTOR)
    blended = (1.0 - smooth) * base_frequency / ROPE_FACTOR + smooth * base_frequency
    scaled = jnp.where(
        wavelength > INITIAL_CONTEXT / LOW_FACTOR, base_frequency / ROPE_FACTOR, blended
    )
    return jnp.where(wavelength < INITIAL_CONTEXT / HIGH_FACTOR, base_frequency, scaled)


def rotate_keys(vectors, positions):
    half_head = vectors.shape[-1] // 2
    frequency = rope_frequencies(vectors.shape[-1])
    angles = positions.astype(jnp.float32)[..., None] * frequency
    cosine = jnp.cos(angles)[..., None, :]
    sine_part = jnp.sin(angles)[..., None, :]
    first_half = vectors[..., :half_head]
    second_half = vectors[..., half_head:]
    return jnp.concatenate(
        [
            first_half * cosine - second_half * sine_part,
            second_half * cosine + first_half * sine_part,
        ],
        axis=-1,
    )


def optimizer_update(current, gradient, moment_mean, moment_square):
    mean_next = BETA_FIRST * moment_mean + (1.0 - BETA_FIRST) * gradient
    square_next = BETA_SECOND * moment_square + (1.0 - BETA_SECOND) * gradient * gradient
    bias_first = 1.0 - BETA_FIRST**OPT_STEP
    bias_second = 1.0 - BETA_SECOND**OPT_STEP
    update = mean_next / bias_first / (jnp.sqrt(square_next / bias_second) + EPSILON)
    return (current - LEARN_RATE * (update + WEIGHT_DECAY * current), mean_next, square_next)


def project_step(inputs, merged_weight, step_index):
    piece = inputs[:, step_index]
    return jnp.einsum("rd,jdc->rjc", piece, merged_weight, preferred_element_type=jnp.float32)


def body(
    trainer_token_inputs,
    weighted_output_cotangents,
    adapter_down_master,
    adapter_up_master,
    down_first_moment,
    down_second_moment,
    up_first_moment,
    up_second_moment,
    frozen_weights,
    decode_step_inputs,
    queries,
    rotated_key_cache,
    stored_value_cache,
    lengths,
):
    row_count = queries.shape[0]
    steps_count = queries.shape[1]
    head_groups = rotated_key_cache.shape[1]
    cache_slots = rotated_key_cache.shape[2]
    head_size = rotated_key_cache.shape[3]
    scaling = 1.0 / math.sqrt(head_size)
    query_heads = queries.reshape(row_count, steps_count, head_groups, -1, head_size)
    cache_scores = (
        jnp.einsum(
            "rtghe,rgpe->rtghp", query_heads, rotated_key_cache, preferred_element_type=jnp.float32
        )
        * scaling
    )
    valid = jnp.arange(cache_slots, dtype=jnp.int32)[None, :] < lengths[:, None]
    cache_scores = jnp.where(valid[:, None, None, None, :], cache_scores, MASKED)
    local_down = adapter_down_master.astype(jnp.bfloat16)
    local_up = adapter_up_master.astype(jnp.bfloat16)
    bfloat_down_factors, bfloat_up_factors = (
        lax.all_gather(local_down, "grp", axis=1, tiled=True),
        lax.all_gather(local_up, "grp", axis=2, tiled=True),
    )
    projected_rows = jnp.einsum(
        "td,jrd->jtr", trainer_token_inputs, bfloat_down_factors, preferred_element_type=jnp.float32
    )
    gathered_rows = jnp.einsum(
        "jct,jcr->jtr",
        weighted_output_cotangents,
        bfloat_up_factors,
        preferred_element_type=jnp.float32,
    )
    projected_rows, gathered_rows = lax.psum((projected_rows, gathered_rows), "tp")
    projected_low = projected_rows.astype(jnp.bfloat16)
    pulled_low = gathered_rows.astype(jnp.bfloat16)
    down_gradient = ADAPTER_SCALE * jnp.einsum(
        "jtr,td->jrd", pulled_low, trainer_token_inputs, preferred_element_type=jnp.float32
    )
    up_gradient = ADAPTER_SCALE * jnp.einsum(
        "jct,jtr->jcr",
        weighted_output_cotangents,
        projected_low,
        preferred_element_type=jnp.float32,
    )
    owned_part = adapter_down_master.shape[1]
    total_down, total_up = lax.psum((down_gradient, up_gradient), "grp")
    offset = lax.axis_index("grp") * owned_part
    down_gradient = lax.dynamic_slice_in_dim(total_down, offset, owned_part, 1)
    up_gradient = lax.dynamic_slice_in_dim(total_up, offset, owned_part, 2)
    fresh_down_factors, fresh_down_first_moment, fresh_down_second_moment = optimizer_update(
        adapter_down_master, down_gradient, down_first_moment, down_second_moment
    )
    fresh_up_factors, fresh_up_first_moment, fresh_up_second_moment = optimizer_update(
        adapter_up_master, up_gradient, up_first_moment, up_second_moment
    )
    full_down, part_up = (
        lax.all_gather(fresh_down_factors, "grp", axis=1, tiled=True),
        lax.all_gather(fresh_up_factors, "grp", axis=2, tiled=True),
    )
    full_up = lax.all_gather(part_up, "tp", axis=1, tiled=True)
    weight_change = jnp.einsum("jrd,jcr->jdc", full_down, full_up, precision=lax.Precision.HIGHEST)
    merged_weight = (frozen_weights.astype(jnp.float32) + ADAPTER_SCALE * weight_change).astype(
        jnp.bfloat16
    )
    per_step = []
    for step_index in range(steps_count):
        per_step.append(
            lax.psum_scatter(
                project_step(
                    inputs=decode_step_inputs, merged_weight=merged_weight, step_index=step_index
                ),
                "tp",
                scatter_dimension=0,
                tiled=True,
            )
        )
    summed = jnp.stack(per_step, axis=1)
    positions = lengths[:, None] + jnp.arange(steps_count, dtype=jnp.int32)[None, :]
    key_raw = summed[:, :, 0].reshape(row_count, steps_count, head_groups, head_size)
    new_keys = rotate_keys(key_raw, positions).reshape(
        row_count, steps_count, head_groups * head_size
    )
    new_values = summed[:, :, 1]
    key_entries = new_keys.astype(jnp.bfloat16)
    value_entries = new_values.astype(jnp.bfloat16)
    fresh_heads = key_entries.reshape(row_count, steps_count, head_groups, head_size)
    fresh_scores = (
        jnp.einsum(
            "rtghe,rsge->rtghs", query_heads, fresh_heads, preferred_element_type=jnp.float32
        )
        * scaling
    )
    causal = jnp.arange(steps_count)[:, None] >= jnp.arange(steps_count)[None, :]
    fresh_scores = jnp.where(causal[None, :, None, None, :], fresh_scores, MASKED)
    scores = jnp.concatenate([cache_scores, fresh_scores], axis=-1)
    peak_score = jnp.max(scores, axis=-1, keepdims=True)
    exponent = jnp.exp(scores - peak_score)
    weights = (exponent / jnp.sum(exponent, axis=-1, keepdims=True)).astype(jnp.bfloat16)
    fresh_value_heads = value_entries.reshape(row_count, steps_count, head_groups, head_size)
    result = jnp.einsum(
        "rtghp,rgpe->rtghe",
        weights[..., :cache_slots],
        stored_value_cache,
        preferred_element_type=jnp.float32,
    )
    result = result + jnp.einsum(
        "rtghs,rsge->rtghe",
        weights[..., cache_slots:],
        fresh_value_heads,
        preferred_element_type=jnp.float32,
    )
    attended = result.reshape(row_count, steps_count, queries.shape[2])
    return (
        attended,
        new_keys,
        new_values,
        fresh_down_factors,
        fresh_up_factors,
        fresh_down_first_moment,
        fresh_down_second_moment,
        fresh_up_first_moment,
        fresh_up_second_moment,
    )


def solution(mesh):
    in_specs = (
        P("grp", "tp"),
        P(None, "tp", "grp"),
        P(None, "grp", "tp"),
        P(None, "tp", "grp"),
        P(None, "grp", "tp"),
        P(None, "grp", "tp"),
        P(None, "tp", "grp"),
        P(None, "tp", "grp"),
        P(None, "tp", None),
        P("grp", None, "tp"),
        P(("grp", "tp"), None, None),
        P(("grp", "tp"), None, None, None),
        P(("grp", "tp"), None, None, None),
        P(("grp", "tp")),
    )
    out_specs = (
        P(("grp", "tp"), None, None),
        P(("grp", "tp"), None, None),
        P(("grp", "tp"), None, None),
        P(None, "grp", "tp"),
        P(None, "tp", "grp"),
        P(None, "grp", "tp"),
        P(None, "grp", "tp"),
        P(None, "tp", "grp"),
        P(None, "tp", "grp"),
    )
    return jax.shard_map(body, mesh=mesh, in_specs=in_specs, out_specs=out_specs, check_vma=False)
```

profile of v0, /device:TPU:1, one launch (start us, length us, event | category | flops | bytes accessed | tf_op | source)
XLA Modules:
  0.0 841.4 jit_solution(17508402434133053982)
XLA Ops:
  7.2 0.0 all-reduce.10.cloned.1.call-start
  7.3 0.8 copy.222
  8.1 69.9 %all_gather.17 = bf16[2,64,1024]{2,0,1:T(2,128)(2,1)S(1)} all-gather(bf16[2,2,1024]{2,0,1:T(2,128)(2,1)S(1)} %copy.222), channel_id=1, replica_groups=mesh['grp'=32,'tp'=16] {'grp'}, dimensions={1}, use_global_device_ids=true | all-gather | bytes 270336 | tf_op jit(solution)/shard_map/all_gather | solution.py:103
  78.0 0.3 convolution_bitcast_fusion.2
  78.3 0.7 copy.223
  79.0 59.2 %all_gather.15 = bf16[2,32,64]{1,0,2:T(2,128)(2,1)S(1)} all-gather(bf16[2,32,2]{1,0,2:T(2,128)(2,1)S(1)} %copy.223), channel_id=1, replica_groups=mesh['grp'=32,'tp'=16] {'grp'}, dimensions={2}, use_global_device_ids=true | all-gather | bytes 8448 | tf_op jit(solution)/shard_map/all_gather | solution.py:104
  138.2 0.9 fusion.19
  139.1 107.5 %all-reduce.13 = (bf16[2,256,64]{1,2,0:T(8,128)(2,1)S(1)}, bf16[2,256,64]{1,2,0:T(8,128)(2,1)S(1)}) all-reduce(f32[2,256,64]{1,2,0:T(8,128)S(1)} %convolution_bitcast_fusion.2, f32[2,256,64]{1,2,0:T(8,128)S(1)} %fusion.19), channel_id=1, replica_groups=mesh['grp'=32,'tp'=16] {'tp'}, use_global_device_ids=true, to_apply=%region_2.3 | all-reduce | flops 65536 | bytes 393216 | tf_op jit(solution)/shard_map/psum | solution.py:115
  246.6 1.0 convolution_multiply_fusion
  247.7 0.0 all-reduce.10.cloned.1.call-update
  247.7 0.0 all-reduce.12.cloned.1.call-start
  247.7 0.1 fusion.3
  247.9 123.6 %psum.31 = f32[2,32,64]{1,2,0:T(8,128)S(1)} all-reduce(f32[2,32,64]{1,2,0:T(8,128)S(1)} %fusion.3), channel_id=1, replica_groups=mesh['grp'=32,'tp'=16] {'grp'}, use_global_device_ids=true, to_apply=%region_3.4 | all-reduce | flops 4096 | bytes 32768 | tf_op jit(solution)/shard_map/psum | solution.py:128
  371.5 0.6 multiply_subtract_fusion.2
  372.1 0.6 copy-done.13
  372.7 60.1 %all_gather.18 = f32[2,32,64]{1,0,2:T(2,128)S(1)} all-gather(f32[2,32,2]{1,0,2:T(2,128)S(1)} %copy.148), channel_id=1, replica_groups=mesh['grp'=32,'tp'=16] {'grp'}, dimensions={2}, use_global_device_ids=true | all-gather | bytes 16896 | tf_op jit(solution)/shard_map/all_gather | solution.py:140
  432.8 0.1 copy.149
  432.8 77.0 %all_gather.19 = f32[2,512,64]{2,1,0:T(8,128)S(1)} all-gather(f32[2,32,64]{2,1,0:T(8,128)S(1)} %copy.149), channel_id=1, replica_groups=mesh['grp'=32,'tp'=16] {'tp'}, dimensions={1}, use_global_device_ids=true | all-gather | bytes 278528 | tf_op jit(solution)/shard_map/all_gather | solution.py:142
  509.9 0.6 add_convert_fusion.1
  510.5 0.5 compare_select_fusion.1
  511.0 0.6 iota_compare_fusion.1
  511.6 1.1 fusion.31
  512.8 23.3 %all-reduce.10.cloned.1.call-done = f32[2,64,1024]{2,1,0:T(8,128)} async-done(((f32[2,64,1024]{2,1,0:T(8,128)}), f32[2,64,1024]{2,1,0:T(8,128)}) %all-reduce.10.cloned.1.call-update) | async-done | bytes 524304 | tf_op jit(solution)/shard_map/psum | solution.py:128
  536.1 1.5 multiply_subtract_fusion.1
  537.6 68.8 %all_gather.16 = f32[2,64,1024]{2,0,1:T(2,128)S(1)} all-gather(f32[2,2,1024]{2,0,1:T(2,128)S(1)} %copy.144), channel_id=1, replica_groups=mesh['grp'=32,'tp'=16] {'grp'}, dimensions={1}, use_global_device_ids=true | all-gather | bytes 540672 | tf_op jit(solution)/shard_map/all_gather | solution.py:139
  606.4 3.8 add_convert_fusion
  610.3 1.1 convolution_bitcast_fusion.3
  611.4 1.1 convolution_bitcast_fusion.4
  612.5 1.1 convolution_bitcast_fusion.5
  613.6 1.1 convolution_bitcast_fusion.6
  614.8 0.2 reshape.110
  615.0 1.3 dynamic-slice
  616.8 0.1 multiply_cosine_fusion
  616.9 0.4 fusion.33
  617.4 211.6 %all-reduce.12.cloned.1.call-done = (f32[32,2,512]{2,0,1:T(8,128)}, f32[32,2,512]{2,0,1:T(8,128)}, f32[32,2,512]{2,0,1:T(8,128)}, f32[32,2,512]{2,0,1:T(8,128)}) async-done(((f32[32,2,512]{2,0,1:T(8,128)}, f32[32,2,512]{2,0,1:T(8,128)}, f32[32,2,512]{2,0,1:T(8,128)}, f32[32,2,512]{2,0,1:T(8,128)}), (f32[32,2,512]{2,0,1:T(8,128)}, f32[32,2,512]{2,0,1:T(8,128)}, f32[32,2,512]{2,0,1:T(8,128)}, ...) | async-done | bytes 524304
  828.9 0.8 dynamic-slice_bitcast_fusion.2
  829.7 0.8 dynamic-slice_bitcast_fusion
  830.6 0.1 fusion.32
  830.7 0.7 fusion.25
  831.3 0.4 fusion.14
  831.8 0.1 fusion.28
  831.9 0.3 copy.160
  832.2 0.3 fusion.5
  832.5 0.2 divide_convert_fusion
  832.7 0.2 convolution_bitcast_fusion.1
  832.9 0.2 fusion.2
  833.1 0.8 reshape.111
  834.0 0.6 copy.165
  (51 shorter events, 0.2 us)
Async XLA Ops:
  7.2 70.8 %copy-start = (bf16[256,1024]{1,0:T(8,128)(2,1)S(1)}, bf16[256,1024]{1,0:T(8,128)(2,1)}, u32[]{:S(2)}) copy-start(bf16[256,1024]{1,0:T(8,128)(2,1)} %param.14) | copy-start | bytes 1572868
  7.2 364.3 %copy-start.12 = (f32[2,32,2]{1,2,0:T(2,128)S(1)}, f32[2,32,2]{1,2,0:T(2,128)}, u32[]{:S(2)}) copy-start(f32[2,32,2]{1,2,0:T(2,128)} %param.17) | copy-start | bytes 1540
  7.2 240.5 %copy-start.9 = (bf16[2,32,256]{2,1,0:T(8,128)(2,1)S(1)}, bf16[2,32,256]{2,1,0:T(8,128)(2,1)}, u32[]{:S(2)}) copy-start(bf16[2,32,256]{2,1,0:T(8,128)(2,1)} %param.15) | copy-start | bytes 98308
  7.2 364.3 %copy-start.14 = (f32[2,32,2]{1,2,0:T(2,128)S(1)}, f32[2,32,2]{1,2,0:T(2,128)}, u32[]{:S(2)}) copy-start(f32[2,32,2]{1,2,0:T(2,128)} %param.20) | copy-start | bytes 1540
  7.2 364.3 %copy-start.15 = (f32[2,32,2]{1,2,0:T(2,128)S(1)}, f32[2,32,2]{1,2,0:T(2,128)}, u32[]{:S(2)}) copy-start(f32[2,32,2]{1,2,0:T(2,128)} %param.21) | copy-start | bytes 1540
  7.2 528.8 %all-reduce.10.cloned.1.call-start = ((), (), s32[]{:S(2)}) async-start(), calls=%async_computation | async-start | bytes 1048576 | tf_op jit(solution)/shard_map/psum | solution.py:128
  78.0 431.9 %copy-start.19 = (s32[2]{0:T(128)S(1)}, s32[2]{0:T(128)}, u32[]{:S(2)}) copy-start(s32[2]{0:T(128)} %param.27) | copy-start | bytes 28
  78.0 433.7 %copy-start.2 = (bf16[32,4,1024]{2,1,0:T(4,128)(2,1)S(1)}, bf16[32,4,1024]{2,1,0:T(4,128)(2,1)}, u32[]{:S(2)}) copy-start(bf16[32,4,1024]{2,1,0:T(4,128)(2,1)} %param.23) | copy-start | bytes 786436
  138.2 397.8 %copy-start.10 = (f32[2,2,1024]{2,1,0:T(2,128)S(1)}, f32[2,2,1024]{2,1,0:T(2,128)}, u32[]{:S(2)}) copy-start(f32[2,2,1024]{2,1,0:T(2,128)} %param.16) | copy-start | bytes 49156
  246.6 359.8 %copy-start.1 = (bf16[2,1024,512]{2,1,0:T(8,128)(2,1)S(1)}, bf16[2,1024,512]{2,1,0:T(8,128)(2,1)}, u32[]{:S(2)}) copy-start(bf16[2,1024,512]{2,1,0:T(8,128)(2,1)} %param.22) | copy-start | bytes 6291460
  247.7 581.2 %all-reduce.12.cloned.1.call-start = ((), (), s32[]{:S(2)}) async-start(), calls=%async_computation.1 | async-start | bytes 1048576
  372.1 0.6 copy-start.13
  537.6 72.7 %copy-start.11 = (f32[2,2,1024]{2,1,0:T(2,128)}, f32[2,2,1024]{2,1,0:T(2,128)S(1)}, u32[]{:S(2)}) copy-start(f32[2,2,1024]{2,1,0:T(2,128)S(1)} %get-tuple-element.62) | copy-start | bytes 49156
  606.4 3.9 copy-start.7
  610.3 1.1 copy-start.6
  610.3 2.2 copy-start.5
  612.5 2.3 copy-start.8
  613.6 3.2 copy-start.16
  613.6 3.2 copy-start.18
  613.6 3.3 copy-start.3
  613.6 3.3 copy-start.17
  617.3 215.5 %copy-start.4 = (bf16[2,4,256,128]{3,2,1,0:T(8,128)(2,1)S(1)}, bf16[2,4,256,128]{3,2,1,0:T(8,128)(2,1)}, u32[]{:S(2)}) copy-start(bf16[2,4,256,128]{3,2,1,0:T(8,128)(2,1)} %param.26) | copy-start | bytes 1572868
Sparse Core Ops, SparseCore 0:
  247.8 288.2 all-reduce.9
  614.9 213.9 all-reduce.11
where the time goes:
time: 842 us; the launch traced here: 841 us
  blocking collectives  566 us (67%)
  waiting for transfers between devices  235 us (28%)
  between operations  15 us (2%)
  matrix products  11.8 us (1%)
    unnamed x3, waiting for transfers between devices  212 us
    psum x1, blocking collectives, body(): total_down, total_up = lax.psum((down_gradient, up_gradient), 'grp')  124 us
    psum x1, blocking collectives, body(): lax.psum((projected_rows, gathered_rows), 'tp')  107 us
    all_gather x1, blocking collectives, body(): full_up = lax.all_gather(part_up, 'tp', axis=1, tiled=True)  77 us
    all_gather x1, blocking collectives, body(): lax.all_gather(local_down, 'grp', axis=1, tiled=True)  69.9 us
    all_gather x1, blocking collectives, body(): lax.all_gather(fresh_down_factors, 'grp', axis=1, tiled=True)  68.8 us
    all_gather x1, blocking collectives, body(): lax.all_gather(fresh_up_factors, 'grp', axis=2, tiled=True)  60.1 us
    all_gather x1, blocking collectives, body(): lax.all_gather(local_up, 'grp', axis=2, tiled=True)  59.2 us
  transfers between devices with their start and end apart: 2, of which 2 were waited for; matrix products, arithmetic and copies ran while one was open for 1% of the time, Pallas kernels for 0%

commit v1 on v0

--- a/solution.py
+++ b/solution.py
@@ -1,3 +1,4 @@
+import functools
 import math
 
 import jax
@@ -61,12 +62,26 @@
     return (current - LEARN_RATE * (update + WEIGHT_DECAY * current), mean_next, square_next)
 
 
-def project_step(inputs, merged_weight, step_index):
-    piece = inputs[:, step_index]
-    return jnp.einsum("rd,jdc->rjc", piece, merged_weight, preferred_element_type=jnp.float32)
+def exchange(pieces, axis):
+    return lax.all_to_all(pieces, axis, 0, 0, tiled=True)
+
+
+def gather_over(block, axis, count):
+    return exchange(jnp.broadcast_to(block[None], (count,) + block.shape), axis)
+
+
+def two_terms(values):
+    high = lax.reduce_precision(values, 8, 7)
+    return high.astype(jnp.bfloat16), (values - high).astype(jnp.bfloat16)
+
+
+def product(spec, left, right):
+    return jnp.einsum(spec, left, right, preferred_element_type=jnp.float32)
 
 
 def body(
+    groups,
+    ranks,
     trainer_token_inputs,
     weighted_output_cotangents,
     adapter_down_master,
@@ -82,81 +97,114 @@
     stored_value_cache,
     lengths,
 ):
-    row_count = queries.shape[0]
-    steps_count = queries.shape[1]
-    head_groups = rotated_key_cache.shape[1]
-    cache_slots = rotated_key_cache.shape[2]
-    head_size = rotated_key_cache.shape[3]
+    row_count, steps_count, query_width = queries.shape
+    head_groups, cache_slots, head_size = rotated_key_cache.shape[1:]
+    kinds, own_rank, own_width = adapter_down_master.shape
+    own_columns, tokens = weighted_output_cotangents.shape[1:]
+    columns = own_columns * ranks
+    own_rows = kinds * own_rank
+    all_rows = own_rows * groups
+    own_lines = row_count * steps_count
+    lanes = 128
+    fill = -own_columns % lanes
+    is_value = (jnp.arange(all_rows) // own_rank) % kinds == 1
+
+    def own_down(values):
+        return values.reshape(own_rows, own_width)
+
+    def own_up(values):
+        return values.transpose(0, 2, 1).reshape(own_rows, own_columns)
+
+    def side_by_side(down, up):
+        parts = [down.astype(jnp.bfloat16), up.astype(jnp.bfloat16)]
+        return jnp.concatenate([parts[0], jnp.pad(parts[1], ((0, 0), (0, fill)))], axis=1)
+
+    def all_factors(down, up):
+        both = gather_over(side_by_side(down, up), "grp", groups).reshape(all_rows, -1)
+        return both[:, :own_width], both[:, own_width : own_width + own_columns]
+
+    flat_inputs = decode_step_inputs.reshape(-1, own_width)
+    frozen_part = [
+        product("rd,dc->rc", flat_inputs, frozen_weights[kind]).astype(jnp.bfloat16)
+        for kind in range(kinds)
+    ]
+
+    down, up = all_factors(own_down(adapter_down_master), own_up(adapter_up_master))
+    projected = product("td,nd->tn", trainer_token_inputs, down)
+    pulled = product("jct,nc->jtn", weighted_output_cotangents, up)
+    pulled = jnp.where(is_value[None, :], pulled[1], pulled[0])
+
+    width = 2 * all_rows
+    pieces = [
+        jnp.concatenate([projected, pulled], axis=1)
+        .astype(jnp.bfloat16)
+        .reshape(ranks, -1, width)
+    ] + [
+        part[:, at : at + width].reshape(ranks, own_lines, width)
+        for part in frozen_part
+        for at in range(0, columns, width)
+    ]
+    sums = exchange(jnp.concatenate(pieces, axis=1), "tp").astype(jnp.float32).sum(axis=0)
+    own_tokens = tokens // ranks
+    frozen_sum = jnp.concatenate(
+        [
+            sums[at : at + own_lines]
+            for at in range(own_tokens, sums.shape[0], own_lines)
+        ],
+        axis=1,
+    )
+    both = gather_over(sums[:own_tokens].astype(jnp.bfloat16), "tp", ranks).reshape(tokens, width)
+    projected, pulled = both[:, :all_rows], both[:, all_rows:]
+
+    down_gradient = ADAPTER_SCALE * product("tn,td->nd", pulled, trainer_token_inputs)
+    up_gradient = product("jct,tn->jnc", weighted_output_cotangents, projected)
+    up_gradient = ADAPTER_SCALE * jnp.where(is_value[:, None], up_gradient[1], up_gradient[0])
+
+    totals = (
+        exchange(
+            side_by_side(down_gradient, up_gradient).reshape(groups, own_rows, -1), "grp"
+        )
+        .astype(jnp.float32)
+        .sum(axis=0)
+    )
+    fresh_down = optimizer_update(
+        own_down(adapter_down_master),
+        totals[:, :own_width],
+        own_down(down_first_moment),
+        own_down(down_second_moment),
+    )
+    fresh_up = optimizer_update(
+        own_up(adapter_up_master),
+        totals[:, own_width : own_width + own_columns],
+        own_up(up_first_moment),
+        own_up(up_second_moment),
+    )
+    down, up = all_factors(fresh_down[0], fresh_up[0])
+    adapter_part = product("rd,nd->rn", flat_inputs, down).reshape(ranks, own_lines, all_rows)
+
+    up_copies = jnp.broadcast_to(up.transpose()[None], (ranks, own_columns, all_rows))
+    last = exchange(jnp.concatenate([*two_terms(adapter_part), up_copies], axis=1), "tp")
+    rank_space = last[:, : 2 * own_lines].astype(jnp.float32).sum(axis=0)
+    rank_space = rank_space[:own_lines] + rank_space[own_lines:]
+    full_up = last[:, 2 * own_lines :].reshape(columns, all_rows)
+    adapter_sum = jnp.concatenate(
+        [
+            sum(
+                product("rn,cn->rc", term, full_up)
+                for term in two_terms(jnp.where(is_value[None, :] == bool(kind), rank_space, 0.0))
+            )
+            for kind in range(kinds)
+        ],
+        axis=1,
+    )
+    raw = frozen_sum + ADAPTER_SCALE * adapter_sum
+    summed = raw.reshape(row_count, steps_count, kinds, columns)
+
     scaling = 1.0 / math.sqrt(head_size)
     query_heads = queries.reshape(row_count, steps_count, head_groups, -1, head_size)
-    cache_scores = (
-        jnp.einsum(
-            "rtghe,rgpe->rtghp", query_heads, rotated_key_cache, preferred_element_type=jnp.float32
-        )
-        * scaling
-    )
+    cache_scores = product("rtghe,rgpe->rtghp", query_heads, rotated_key_cache) * scaling
     valid = jnp.arange(cache_slots, dtype=jnp.int32)[None, :] < lengths[:, None]
     cache_scores = jnp.where(valid[:, None, None, None, :], cache_scores, MASKED)
-    local_down = adapter_down_master.astype(jnp.bfloat16)
-    local_up = adapter_up_master.astype(jnp.bfloat16)
-    bfloat_down_factors, bfloat_up_factors = (
-        lax.all_gather(local_down, "grp", axis=1, tiled=True),
-        lax.all_gather(local_up, "grp", axis=2, tiled=True),
-    )
-    projected_rows = jnp.einsum(
-        "td,jrd->jtr", trainer_token_inputs, bfloat_down_factors, preferred_element_type=jnp.float32
-    )
-    gathered_rows = jnp.einsum(
-        "jct,jcr->jtr",
-        weighted_output_cotangents,
-        bfloat_up_factors,
-        preferred_element_type=jnp.float32,
-    )
-    projected_rows, gathered_rows = lax.psum((projected_rows, gathered_rows), "tp")
-    projected_low = projected_rows.astype(jnp.bfloat16)
-    pulled_low = gathered_rows.astype(jnp.bfloat16)
-    down_gradient = ADAPTER_SCALE * jnp.einsum(
-        "jtr,td->jrd", pulled_low, trainer_token_inputs, preferred_element_type=jnp.float32
-    )
-    up_gradient = ADAPTER_SCALE * jnp.einsum(
-        "jct,jtr->jcr",
-        weighted_output_cotangents,
-        projected_low,
-        preferred_element_type=jnp.float32,
-    )
-    owned_part = adapter_down_master.shape[1]
-    total_down, total_up = lax.psum((down_gradient, up_gradient), "grp")
-    offset = lax.axis_index("grp") * owned_part
-    down_gradient = lax.dynamic_slice_in_dim(total_down, offset, owned_part, 1)
-    up_gradient = lax.dynamic_slice_in_dim(total_up, offset, owned_part, 2)
-    fresh_down_factors, fresh_down_first_moment, fresh_down_second_moment = optimizer_update(
-        adapter_down_master, down_gradient, down_first_moment, down_second_moment
-    )
-    fresh_up_factors, fresh_up_first_moment, fresh_up_second_moment = optimizer_update(
-        adapter_up_master, up_gradient, up_first_moment, up_second_moment
-    )
-    full_down, part_up = (
-        lax.all_gather(fresh_down_factors, "grp", axis=1, tiled=True),
-        lax.all_gather(fresh_up_factors, "grp", axis=2, tiled=True),
-    )
-    full_up = lax.all_gather(part_up, "tp", axis=1, tiled=True)
-    weight_change = jnp.einsum("jrd,jcr->jdc", full_down, full_up, precision=lax.Precision.HIGHEST)
-    merged_weight = (frozen_weights.astype(jnp.float32) + ADAPTER_SCALE * weight_change).astype(
-        jnp.bfloat16
-    )
-    per_step = []
-    for step_index in range(steps_count):
-        per_step.append(
-            lax.psum_scatter(
-                project_step(
-                    inputs=decode_step_inputs, merged_weight=merged_weight, step_index=step_index
-                ),
-                "tp",
-                scatter_dimension=0,
-                tiled=True,
-            )
-        )
-    summed = jnp.stack(per_step, axis=1)
     positions = lengths[:, None] + jnp.arange(steps_count, dtype=jnp.int32)[None, :]
     key_raw = summed[:, :, 0].reshape(row_count, steps_count, head_groups, head_size)
     new_keys = rotate_keys(key_raw, positions).reshape(
@@ -191,17 +239,24 @@
         fresh_value_heads,
         preferred_element_type=jnp.float32,
     )
-    attended = result.reshape(row_count, steps_count, queries.shape[2])
+    attended = result.reshape(row_count, steps_count, query_width)
+
+    def back_down(values):
+        return values.reshape(kinds, own_rank, own_width)
+
+    def back_up(values):
+        return values.reshape(kinds, own_rank, own_columns).transpose(0, 2, 1)
+
     return (
         attended,
         new_keys,
         new_values,
-        fresh_down_factors,
-        fresh_up_factors,
-        fresh_down_first_moment,
-        fresh_down_second_moment,
-        fresh_up_first_moment,
-        fresh_up_second_moment,
+        back_down(fresh_down[0]),
+        back_up(fresh_up[0]),
+        back_down(fresh_down[1]),
+        back_down(fresh_down[2]),
+        back_up(fresh_up[1]),
+        back_up(fresh_up[2]),
     )
 
 
@@ -233,4 +288,5 @@
         P(None, "tp", "grp"),
         P(None, "tp", "grp"),
     )
-    return jax.shard_map(body, mesh=mesh, in_specs=in_specs, out_specs=out_specs, check_vma=False)
+    placed = functools.partial(body, mesh.shape["grp"], mesh.shape["tp"])
+    return jax.shard_map(placed, mesh=mesh, in_specs=in_specs, out_specs=out_specs, check_vma=False)

time: 842 us -> 138 us (0.16)
  blocking collectives: 566 us -> 0 us
  waiting for transfers between devices: 235 us -> 64.8 us
  starting transfers between devices: 0.08 us -> 48 us
  between operations: 15 us -> 1.14 us
    all_gather x5 -> x0, blocking collectives: 335 us -> none  [the longest x1 77 us: body(): full_up = lax.all_gather(part_up, 'tp', axis=1, tiled=True)]
    psum x2 -> x0, blocking collectives: 231 us -> none  [the longest x1 124 us: body(): total_down, total_up = lax.psum((down_gradient, up_gradient), 'grp')]
    unnamed x3 -> x0, waiting for transfers between devices: 212 us -> none
    all_to_all x0 -> x6, waiting for transfers between devices: none -> 64.8 us  [exchange(): return lax.all_to_all(pieces, axis, 0, 0, tiled=True)]
    all_to_all x0 -> x6, starting transfers between devices: none -> 48 us  [exchange(): return lax.all_to_all(pieces, axis, 0, 0, tiled=True)]
    psum x1 -> x0, waiting for transfers between devices: 23.3 us -> none  [body(): total_down, total_up = lax.psum((down_gradient, up_gradient), 'grp')]
  transfers between devices with their start and end apart: 2 -> 6, of which waited for: 2 -> 6; matrix products, arithmetic and copies ran while one was open for 1% -> 5% of each run, Pallas kernels for 0% -> 0%
where the time goes in v1:
time: 138 us; the launch traced here: 137 us
  waiting for transfers between devices  64.8 us (47%)
  starting transfers between devices  48 us (35%)
  local copies, waits for them, and re-layouts  11.9 us (9%)
  matrix products  6 us (4%)
  other arithmetic  4.86 us (4%)
    all_to_all x6, waiting for transfers between devices, exchange(): return lax.all_to_all(pieces, axis, 0, 0, tiled=True)  64.8 us
    all_to_all x6, starting transfers between devices, exchange(): return lax.all_to_all(pieces, axis, 0, 0, tiled=True)  48 us
    dot_general x12, matrix products, product(): return jnp.einsum(spec, left, right, preferred_element_type=jnp.float32)  5.2 us
  transfers between devices with their start and end apart: 6, of which 6 were waited for; matrix products, arithmetic and copies ran while one was open for 5% of the time, Pallas kernels for 0%

profile of v1, /device:TPU:1, one launch (start us, length us, event | category | flops | bytes accessed | tf_op | source)
XLA Modules:
  0.0 136.7 jit_solution(11854401513741129958)
XLA Ops:
  0.7 0.8 reshape.256
  1.5 0.7 convert_element_type.81
  2.2 0.8 broadcast_in_dim.69
  2.9 13.5 %all-to-all-start = ((bf16[32,4,1152]{2,1,0:T(4,128)(2,1)}), bf16[32,4,1152]{2,1,0:T(4,128)(2,1)S(1)}, u32[]{:S(2)}, u32[]{:S(2)}) async-start(bf16[32,4,1152]{2,1,0:T(4,128)(2,1)} %broadcast_in_dim.69), calls=%async_computation | async-start | bytes 589824 | tf_op jit(solution)/shard_map/all_to_all | solution.py:66
  16.4 1.0 reshape.259
  17.5 1.5 %convolution_convert_fusion.1 = bf16[128,512]{1,0:T(8,128)(2,1)S(1)} fusion(bf16[128,1024]{1,0:T(8,128)(2,1)S(1)} %reshape.259, bf16[2,1024,512]{2,1,0:T(8,128)(2,1)} %param.22), kind=kOutput, calls=%fused_computation.10 | convolution fusion | flops 134283264 | bytes 1441792 | tf_op jit(solution)/shard_map/rd,dc->rc/dot_general | solution.py:79
  19.0 1.5 %convolution_convert_fusion = bf16[128,512]{1,0:T(8,128)(2,1)S(1)} fusion(bf16[128,1024]{1,0:T(8,128)(2,1)S(1)} %reshape.259, bf16[2,1024,512]{2,1,0:T(8,128)(2,1)} %param.22), kind=kOutput, calls=%fused_computation.9 | convolution fusion | flops 134283264 | bytes 1441792 | tf_op jit(solution)/shard_map/rd,dc->rc/dot_general | solution.py:79
  20.6 8.3 %all-to-all-done = bf16[32,4,1152]{2,1,0:T(4,128)(2,1)S(1)} async-done(((bf16[32,4,1152]{2,1,0:T(4,128)(2,1)}), bf16[32,4,1152]{2,1,0:T(4,128)(2,1)S(1)}, u32[]{:S(2)}, u32[]{:S(2)}) %all-to-all-start) | async-done | bytes 294944 | tf_op jit(solution)/shard_map/all_to_all | solution.py:66
  28.9 0.2 convolution_bitcast_fusion.2
  29.4 0.3 fusion.4
  29.8 0.7 maximum_dynamic-update-slice_fusion
  30.5 0.7 fusion.30
  31.2 0.7 fusion.29
  31.8 0.7 fusion.28
  32.5 0.6 fusion.27
  33.1 12.5 %all-to-all-start.1 = ((bf16[16,48,256]{2,1,0:T(8,128)(2,1)}), bf16[16,48,256]{2,1,0:T(8,128)(2,1)S(1)}, u32[]{:S(2)}, u32[]{:S(2)}) async-start(bf16[16,48,256]{2,1,0:T(8,128)(2,1)} %fusion.27), calls=%async_computation.1 | async-start | bytes 786432 | tf_op jit(solution)/shard_map/all_to_all | solution.py:66
  45.7 14.4 %all-to-all-done.1 = bf16[16,48,256]{2,1,0:T(8,128)(2,1)S(1)} async-done(((bf16[16,48,256]{2,1,0:T(8,128)(2,1)}), bf16[16,48,256]{2,1,0:T(8,128)(2,1)S(1)}, u32[]{:S(2)}, u32[]{:S(2)}) %all-to-all-start.1) | async-done | bytes 393248 | tf_op jit(solution)/shard_map/all_to_all | solution.py:66
  60.1 0.7 broadcast_in_dim.106
  60.8 4.4 %all-to-all-start.2 = ((bf16[16,16,256]{2,1,0:T(8,128)(2,1)}), bf16[16,16,256]{2,1,0:T(8,128)(2,1)S(1)}, u32[]{:S(2)}, u32[]{:S(2)}) async-start(bf16[16,16,256]{2,1,0:T(8,128)(2,1)} %broadcast_in_dim.106), calls=%async_computation.2 | async-start | bytes 262144 | tf_op jit(solution)/shard_map/all_to_all | solution.py:66
  65.2 0.2 reshape.255
  65.5 9.8 %all-to-all-done.2 = bf16[16,16,256]{2,1,0:T(8,128)(2,1)S(1)} async-done(((bf16[16,16,256]{2,1,0:T(8,128)(2,1)}), bf16[16,16,256]{2,1,0:T(8,128)(2,1)S(1)}, u32[]{:S(2)}, u32[]{:S(2)}) %all-to-all-start.2) | async-done | bytes 131104 | tf_op jit(solution)/shard_map/all_to_all | solution.py:66
  75.3 0.2 convolution_bitcast_fusion.3
  75.5 0.3 fusion.2
  75.9 0.8 reshape.265
  76.7 6.3 %all-to-all-start.3 = ((bf16[32,4,1152]{2,1,0:T(4,128)(2,1)}), bf16[32,4,1152]{2,1,0:T(4,128)(2,1)S(1)}, u32[]{:S(2)}, u32[]{:S(2)}) async-start(bf16[32,4,1152]{2,1,0:T(4,128)(2,1)} %reshape.265), calls=%async_computation.3 | async-start | bytes 589824 | tf_op jit(solution)/shard_map/all_to_all | solution.py:66
  83.1 12.7 %all-to-all-done.3 = bf16[32,4,1152]{2,1,0:T(4,128)(2,1)S(1)} async-done(((bf16[32,4,1152]{2,1,0:T(4,128)(2,1)}), bf16[32,4,1152]{2,1,0:T(4,128)(2,1)S(1)}, u32[]{:S(2)}, u32[]{:S(2)}) %all-to-all-start.3) | async-done | bytes 294944 | tf_op jit(solution)/shard_map/all_to_all | solution.py:66
  96.0 0.6 fusion.66
  96.6 0.8 broadcast_in_dim.108
  97.4 4.4 %all-to-all-start.4 = ((bf16[32,4,1152]{2,1,0:T(4,128)(2,1)}), bf16[32,4,1152]{2,1,0:T(4,128)(2,1)S(1)}, u32[]{:S(2)}, u32[]{:S(2)}) async-start(bf16[32,4,1152]{2,1,0:T(4,128)(2,1)} %broadcast_in_dim.108), calls=%async_computation.4 | async-start | bytes 589824 | tf_op jit(solution)/shard_map/all_to_all | solution.py:66
  102.0 0.4 fusion.71
  102.4 10.9 %all-to-all-done.4 = bf16[32,4,1152]{2,1,0:T(4,128)(2,1)S(1)} async-done(((bf16[32,4,1152]{2,1,0:T(4,128)(2,1)}), bf16[32,4,1152]{2,1,0:T(4,128)(2,1)S(1)}, u32[]{:S(2)}, u32[]{:S(2)}) %all-to-all-start.4) | async-done | bytes 294944 | tf_op jit(solution)/shard_map/all_to_all | solution.py:66
  113.3 0.2 reduce-precision_convert_fusion
  113.7 0.7 pad_maximum_fusion
  114.4 6.9 %all-to-all-start.5 = ((bf16[16,48,128]{2,1,0:T(8,128)(2,1)}), bf16[16,48,128]{2,1,0:T(8,128)(2,1)S(1)}, u32[]{:S(2)}, u32[]{:S(2)}) async-start(bf16[16,48,128]{2,1,0:T(8,128)(2,1)} %pad_maximum_fusion), calls=%async_computation.5 | async-start | bytes 393216 | tf_op jit(solution)/shard_map/all_to_all | solution.py:66
  121.3 0.6 reshape.271
  122.0 0.6 reshape.273
  122.6 0.6 reshape.274
  123.2 8.8 %all-to-all-done.5 = bf16[16,48,128]{2,1,0:T(8,128)(2,1)S(1)} async-done(((bf16[16,48,128]{2,1,0:T(8,128)(2,1)}), bf16[16,48,128]{2,1,0:T(8,128)(2,1)S(1)}, u32[]{:S(2)}, u32[]{:S(2)}) %all-to-all-start.5) | async-done | bytes 196640 | tf_op jit(solution)/shard_map/all_to_all | solution.py:66
  132.3 0.2 convolution_add_fusion.1
  132.8 0.7 fusion.42
  133.5 0.4 fusion.19
  134.1 0.3 copy.92
  134.4 0.3 fusion.11
  134.7 0.2 divide_convert_fusion
  134.9 0.6 copy.122
  135.5 0.2 convolution_bitcast_fusion.1
  135.7 0.2 fusion.3
  135.9 0.8 reshape.269
  (69 shorter events, 2.2 us)
Async XLA Ops:
  0.6 28.7 %copy-start = (bf16[256,1024]{1,0:T(8,128)(2,1)S(1)}, bf16[256,1024]{1,0:T(8,128)(2,1)}, u32[]{:S(2)}) copy-start(bf16[256,1024]{1,0:T(8,128)(2,1)} %param.14) | copy-start | bytes 1572868
  2.9 25.9 %all-to-all-start = ((bf16[32,4,1152]{2,1,0:T(4,128)(2,1)}), bf16[32,4,1152]{2,1,0:T(4,128)(2,1)S(1)}, u32[]{:S(2)}, u32[]{:S(2)}) async-start(bf16[32,4,1152]{2,1,0:T(4,128)(2,1)} %broadcast_in_dim.69), calls=%async_computation | async-start | bytes 589824 | tf_op jit(solution)/shard_map/all_to_all | solution.py:66
  16.4 12.5 %copy-start.4 = (bf16[2,32,256]{2,1,0:T(8,128)(2,1)S(1)}, bf16[2,32,256]{2,1,0:T(8,128)(2,1)}, u32[]{:S(2)}) copy-start(bf16[2,32,256]{2,1,0:T(8,128)(2,1)} %param.15) | copy-start | bytes 98308
  20.6 25.1 %copy-start.5 = (f32[2,2,1024]{2,1,0:T(2,128)S(1)}, f32[2,2,1024]{2,1,0:T(2,128)}, u32[]{:S(2)}) copy-start(f32[2,2,1024]{2,1,0:T(2,128)} %param.18) | copy-start | bytes 49156
  29.1 36.1 %copy-start.6 = (f32[2,2,1024]{2,1,0:T(2,128)S(1)}, f32[2,2,1024]{2,1,0:T(2,128)}, u32[]{:S(2)}) copy-start(f32[2,2,1024]{2,1,0:T(2,128)} %param.19) | copy-start | bytes 49156
  29.1 36.1 %copy-start.3 = (bf16[2,4,8192]{2,1,0:T(4,128)(2,1)S(1)}, bf16[2,4,8192]{2,1,0:T(4,128)(2,1)}, u32[]{:S(2)}) copy-start(bf16[2,4,8192]{2,1,0:T(4,128)(2,1)} %param.24) | copy-start | bytes 393220
  29.2 36.2 %copy-start.10 = (s32[2]{0:T(128)S(1)}, s32[2]{0:T(128)}, u32[]{:S(2)}) copy-start(s32[2]{0:T(128)} %param.27) | copy-start | bytes 28
  33.1 26.9 %all-to-all-start.1 = ((bf16[16,48,256]{2,1,0:T(8,128)(2,1)}), bf16[16,48,256]{2,1,0:T(8,128)(2,1)S(1)}, u32[]{:S(2)}, u32[]{:S(2)}) async-start(bf16[16,48,256]{2,1,0:T(8,128)(2,1)} %fusion.27), calls=%async_computation.1 | async-start | bytes 786432 | tf_op jit(solution)/shard_map/all_to_all | solution.py:66
  45.6 37.4 %copy-start.8 = (f32[2,32,2]{1,2,0:T(2,128)S(1)}, f32[2,32,2]{1,2,0:T(2,128)}, u32[]{:S(2)}) copy-start(f32[2,32,2]{1,2,0:T(2,128)} %param.20) | copy-start | bytes 1540
  45.7 37.4 %copy-start.9 = (f32[2,32,2]{1,2,0:T(2,128)S(1)}, f32[2,32,2]{1,2,0:T(2,128)}, u32[]{:S(2)}) copy-start(f32[2,32,2]{1,2,0:T(2,128)} %param.21) | copy-start | bytes 1540
  60.1 35.8 %copy-start.7 = (f32[2,32,2]{1,2,0:T(2,128)S(1)}, f32[2,32,2]{1,2,0:T(2,128)}, u32[]{:S(2)}) copy-start(f32[2,32,2]{1,2,0:T(2,128)} %param.17) | copy-start | bytes 1540
  60.8 14.5 %all-to-all-start.2 = ((bf16[16,16,256]{2,1,0:T(8,128)(2,1)}), bf16[16,16,256]{2,1,0:T(8,128)(2,1)S(1)}, u32[]{:S(2)}, u32[]{:S(2)}) async-start(bf16[16,16,256]{2,1,0:T(8,128)(2,1)} %broadcast_in_dim.106), calls=%async_computation.2 | async-start | bytes 262144 | tf_op jit(solution)/shard_map/all_to_all | solution.py:66
  75.5 26.5 %copy-start.1 = (bf16[2,4,256,128]{3,2,1,0:T(8,128)(2,1)S(1)}, bf16[2,4,256,128]{3,2,1,0:T(8,128)(2,1)}, u32[]{:S(2)}) copy-start(bf16[2,4,256,128]{3,2,1,0:T(8,128)(2,1)} %param.25) | copy-start | bytes 1572868
  76.7 19.1 %all-to-all-start.3 = ((bf16[32,4,1152]{2,1,0:T(4,128)(2,1)}), bf16[32,4,1152]{2,1,0:T(4,128)(2,1)S(1)}, u32[]{:S(2)}, u32[]{:S(2)}) async-start(bf16[32,4,1152]{2,1,0:T(4,128)(2,1)} %reshape.265), calls=%async_computation.3 | async-start | bytes 589824 | tf_op jit(solution)/shard_map/all_to_all | solution.py:66
  97.4 15.9 %all-to-all-start.4 = ((bf16[32,4,1152]{2,1,0:T(4,128)(2,1)}), bf16[32,4,1152]{2,1,0:T(4,128)(2,1)S(1)}, u32[]{:S(2)}, u32[]{:S(2)}) async-start(bf16[32,4,1152]{2,1,0:T(4,128)(2,1)} %broadcast_in_dim.108), calls=%async_computation.4 | async-start | bytes 589824 | tf_op jit(solution)/shard_map/all_to_all | solution.py:66
  114.4 17.6 %all-to-all-start.5 = ((bf16[16,48,128]{2,1,0:T(8,128)(2,1)}), bf16[16,48,128]{2,1,0:T(8,128)(2,1)S(1)}, u32[]{:S(2)}, u32[]{:S(2)}) async-start(bf16[16,48,128]{2,1,0:T(8,128)(2,1)} %pad_maximum_fusion), calls=%async_computation.5 | async-start | bytes 393216 | tf_op jit(solution)/shard_map/all_to_all | solution.py:66
  132.2 3.5 %copy-start.2 = (bf16[2,4,256,128]{3,2,1,0:T(8,128)(2,1)S(1)}, bf16[2,4,256,128]{3,2,1,0:T(8,128)(2,1)}, u32[]{:S(2)}) copy-start(bf16[2,4,256,128]{3,2,1,0:T(8,128)(2,1)} %param.26) | copy-start | bytes 1572868

commit v2 on v1

--- a/solution.py
+++ b/solution.py
@@ -4,6 +4,8 @@
 import jax
 import jax.numpy as jnp
 from jax import lax
+from jax.experimental import pallas as pl
+from jax.experimental.pallas import tpu as pltpu
 from jax.sharding import PartitionSpec as P
 
 OPT_STEP = 20
@@ -36,23 +38,6 @@
     return jnp.where(wavelength < INITIAL_CONTEXT / HIGH_FACTOR, base_frequency, scaled)
 
 
-def rotate_keys(vectors, positions):
-    half_head = vectors.shape[-1] // 2
-    frequency = rope_frequencies(vectors.shape[-1])
-    angles = positions.astype(jnp.float32)[..., None] * frequency
-    cosine = jnp.cos(angles)[..., None, :]
-    sine_part = jnp.sin(angles)[..., None, :]
-    first_half = vectors[..., :half_head]
-    second_half = vectors[..., half_head:]
-    return jnp.concatenate(
-        [
-            first_half * cosine - second_half * sine_part,
-            second_half * cosine + first_half * sine_part,
-        ],
-        axis=-1,
-    )
-
-
 def optimizer_update(current, gradient, moment_mean, moment_square):
     mean_next = BETA_FIRST * moment_mean + (1.0 - BETA_FIRST) * gradient
     square_next = BETA_SECOND * moment_square + (1.0 - BETA_SECOND) * gradient * gradient
@@ -77,6 +62,119 @@
 
 def product(spec, left, right):
     return jnp.einsum(spec, left, right, preferred_element_type=jnp.float32)
+
+
+def scatter_sum_by_halves(values, axis, count):
+    index = lax.axis_index(axis)
+    bits = count.bit_length() - 1
+    values = values.reshape((2,) * bits + values.shape[1:])
+    left = list(range(bits - 1, -1, -1))
+    for bit in [0] + list(range(bits - 1, 0, -1)):
+        at = left.index(bit)
+        left.remove(bit)
+        low = lax.index_in_dim(values, 0, at, keepdims=False)
+        high = lax.index_in_dim(values, 1, at, keepdims=False)
+        upper = (index >> bit) & 1 == 1
+        pairs = [(place, place ^ (1 << bit)) for place in range(count)]
+        arrived = lax.ppermute(jnp.where(upper, low, high), axis, pairs)
+        values = jnp.where(upper, high, low) + arrived
+    return values
+
+
+def dot_last(left, right):
+    return lax.dot_general(
+        left, right, (((1,), (1,)), ((), ())), preferred_element_type=jnp.float32
+    )
+
+
+def cached_attention(lengths_ref, query_ref, key_ref, value_ref, peak_ref, total_ref, sum_ref):
+    row_count, heads, slots, size = key_ref.shape
+    lines = query_ref.shape[1]
+    steps = 4
+    line = lax.broadcasted_iota(jnp.int32, (lines, slots), 0) // steps % row_count
+    slot = lax.broadcasted_iota(jnp.int32, (lines, slots), 1)
+    valid = [(line == row) & (slot < lengths_ref[row]) for row in range(row_count)]
+    for head in range(heads):
+        query = query_ref[head]
+        scores = jnp.full((lines, slots), MASKED, jnp.float32)
+        for row in range(row_count):
+            found = dot_last(query, key_ref[row, head]) * (1.0 / math.sqrt(size))
+            scores = jnp.where(valid[row], found, scores)
+        peak = jnp.max(scores, axis=1, keepdims=True)
+        weights = jnp.exp(scores - peak)
+        result = jnp.zeros((lines, size), jnp.float32)
+        for row in range(row_count):
+            own = jnp.where(valid[row], weights, 0.0).astype(jnp.bfloat16)
+            result += jnp.dot(own, value_ref[row, head], preferred_element_type=jnp.float32)
+        peak_ref[head] = peak
+        total_ref[head] = jnp.sum(weights, axis=1, keepdims=True)
+        sum_ref[head] = result
+
+
+def finish(
+    last_ref,
+    frozen_ref,
+    cosine_ref,
+    sine_ref,
+    query_ref,
+    peak_ref,
+    total_ref,
+    sum_ref,
+    attended_ref,
+    keys_ref,
+    values_ref,
+    own_rank,
+):
+    row_count, steps, _ = keys_ref.shape
+    heads, lines, size = query_ref.shape
+    own_lines = row_count * steps
+    ranks, _, all_rows = last_ref.shape
+    parts = jnp.sum(last_ref[:, : 2 * own_lines, :].astype(jnp.float32), axis=0)
+    rank_space = parts[:own_lines] + parts[own_lines:]
+    full_up = last_ref[:, 2 * own_lines :, :].reshape(-1, all_rows)
+    columns = full_up.shape[0]
+    adapter_row = lax.broadcasted_iota(jnp.int32, (own_lines, all_rows), 1)
+    raw = []
+    for kind in range(2):
+        own = jnp.where(adapter_row // own_rank % 2 == kind, rank_space, 0.0)
+        high = own.astype(jnp.bfloat16).astype(jnp.float32)
+        both = jnp.concatenate([high, own - high], axis=0).astype(jnp.bfloat16)
+        both = dot_last(both, full_up)
+        raw.append(
+            frozen_ref[:, kind * columns : (kind + 1) * columns]
+            + ADAPTER_SCALE * (both[:own_lines] + both[own_lines:])
+        )
+    for row in range(row_count):
+        values_ref[row] = raw[1][row * steps : (row + 1) * steps]
+
+    line = lax.broadcasted_iota(jnp.int32, (lines, 2 * own_lines), 0)
+    entry = lax.broadcasted_iota(jnp.int32, (lines, 2 * own_lines), 1)
+    valid = (line // steps % row_count == entry // steps) & (entry % steps <= line % steps)
+    for head in range(heads):
+        lanes = slice(head * size, (head + 1) * size)
+        vector = raw[0][:, lanes]
+        turned = pltpu.roll(vector, size // 2, 1)
+        rotated = vector * cosine_ref[...] + turned * sine_ref[...]
+        for row in range(row_count):
+            keys_ref[row, :, lanes] = rotated[row * steps : (row + 1) * steps]
+        fresh_keys = jnp.concatenate([rotated, rotated], axis=0).astype(jnp.bfloat16)
+        fresh_values = jnp.concatenate([raw[1][:, lanes]] * 2, axis=0).astype(jnp.bfloat16)
+        scores = dot_last(query_ref[head], fresh_keys) * (1.0 / math.sqrt(size))
+        scores = jnp.where(valid, scores, MASKED)
+        peak = jnp.maximum(peak_ref[head], jnp.max(scores, axis=1, keepdims=True))
+        scale = jnp.exp(peak_ref[head] - peak)
+        weights = jnp.where(valid, jnp.exp(scores - peak), 0.0)
+        total = total_ref[head] * scale + jnp.sum(weights, axis=1, keepdims=True)
+        result = sum_ref[head] * scale + jnp.dot(
+            weights.astype(jnp.bfloat16), fresh_values, preferred_element_type=jnp.float32
+        )
+        result = result * (1.0 / total)
+        group = lines // own_lines
+        for query_head in range(group):
+            at = (head * group + query_head) * size
+            for row in range(row_count):
+                start = query_head * own_lines + row * steps
+                attended_ref[row, :, at : at + size] = result[start : start + steps]
 
 
 def body(
@@ -125,35 +223,24 @@
 
     flat_inputs = decode_step_inputs.reshape(-1, own_width)
     frozen_part = [
-        product("rd,dc->rc", flat_inputs, frozen_weights[kind]).astype(jnp.bfloat16)
-        for kind in range(kinds)
+        product("rd,dc->rc", flat_inputs, frozen_weights[kind]) for kind in range(kinds)
     ]
+    frozen_sum = scatter_sum_by_halves(
+        jnp.concatenate(frozen_part, axis=1).reshape(ranks, own_lines, kinds * columns),
+        "tp",
+        ranks,
+    )
 
     down, up = all_factors(own_down(adapter_down_master), own_up(adapter_up_master))
     projected = product("td,nd->tn", trainer_token_inputs, down)
     pulled = product("jct,nc->jtn", weighted_output_cotangents, up)
     pulled = jnp.where(is_value[None, :], pulled[1], pulled[0])
 
-    width = 2 * all_rows
-    pieces = [
-        jnp.concatenate([projected, pulled], axis=1)
-        .astype(jnp.bfloat16)
-        .reshape(ranks, -1, width)
-    ] + [
-        part[:, at : at + width].reshape(ranks, own_lines, width)
-        for part in frozen_part
-        for at in range(0, columns, width)
-    ]
-    sums = exchange(jnp.concatenate(pieces, axis=1), "tp").astype(jnp.float32).sum(axis=0)
-    own_tokens = tokens // ranks
-    frozen_sum = jnp.concatenate(
-        [
-            sums[at : at + own_lines]
-            for at in range(own_tokens, sums.shape[0], own_lines)
-        ],
-        axis=1,
-    )
-    both = gather_over(sums[:own_tokens].astype(jnp.bfloat16), "tp", ranks).reshape(tokens, width)
+    pieces = jnp.concatenate([projected, pulled], axis=1).astype(jnp.bfloat16)
+    sums = (
+        exchange(pieces.reshape(ranks, -1, 2 * all_rows), "tp").astype(jnp.float32).sum(axis=0)
+    )
+    both = gather_over(sums.astype(jnp.bfloat16), "tp", ranks).reshape(tokens, 2 * all_rows)
     projected, pulled = both[:, :all_rows], both[:, all_rows:]
 
     down_gradient = ADAPTER_SCALE * product("tn,td->nd", pulled, trainer_token_inputs)
@@ -180,66 +267,52 @@
         own_up(up_second_moment),
     )
     down, up = all_factors(fresh_down[0], fresh_up[0])
+    up, frozen_sum = lax.optimization_barrier((up, frozen_sum))
     adapter_part = product("rd,nd->rn", flat_inputs, down).reshape(ranks, own_lines, all_rows)
 
     up_copies = jnp.broadcast_to(up.transpose()[None], (ranks, own_columns, all_rows))
     last = exchange(jnp.concatenate([*two_terms(adapter_part), up_copies], axis=1), "tp")
-    rank_space = last[:, : 2 * own_lines].astype(jnp.float32).sum(axis=0)
-    rank_space = rank_space[:own_lines] + rank_space[own_lines:]
-    full_up = last[:, 2 * own_lines :].reshape(columns, all_rows)
-    adapter_sum = jnp.concatenate(
-        [
-            sum(
-                product("rn,cn->rc", term, full_up)
-                for term in two_terms(jnp.where(is_value[None, :] == bool(kind), rank_space, 0.0))
-            )
-            for kind in range(kinds)
-        ],
-        axis=1,
-    )
-    raw = frozen_sum + ADAPTER_SCALE * adapter_sum
-    summed = raw.reshape(row_count, steps_count, kinds, columns)
-
-    scaling = 1.0 / math.sqrt(head_size)
-    query_heads = queries.reshape(row_count, steps_count, head_groups, -1, head_size)
-    cache_scores = product("rtghe,rgpe->rtghp", query_heads, rotated_key_cache) * scaling
-    valid = jnp.arange(cache_slots, dtype=jnp.int32)[None, :] < lengths[:, None]
-    cache_scores = jnp.where(valid[:, None, None, None, :], cache_scores, MASKED)
+
+    lines = query_width // (head_groups * head_size) * own_lines
+    query_lines = (
+        queries.reshape(row_count, steps_count, head_groups, -1, head_size)
+        .transpose(2, 3, 0, 1, 4)
+        .reshape(head_groups, lines, head_size)
+    )
+    column = jax.ShapeDtypeStruct((head_groups, lines, 1), jnp.float32)
+    peak, total, cached = pl.pallas_call(
+        cached_attention,
+        out_shape=(
+            column,
+            column,
+            jax.ShapeDtypeStruct((head_groups, lines, head_size), jnp.float32),
+        ),
+        in_specs=[pl.BlockSpec(memory_space=pltpu.SMEM)]
+        + [pl.BlockSpec(memory_space=pltpu.VMEM)] * 3,
+        cost_estimate=pl.CostEstimate(
+            flops=8 * lines * cache_slots * head_size * head_groups,
+            bytes_accessed=4 * row_count * head_groups * cache_slots * head_size,
+            transcendentals=lines * cache_slots * head_groups,
+        ),
+    )(lengths, query_lines, rotated_key_cache, stored_value_cache)
+
     positions = lengths[:, None] + jnp.arange(steps_count, dtype=jnp.int32)[None, :]
-    key_raw = summed[:, :, 0].reshape(row_count, steps_count, head_groups, head_size)
-    new_keys = rotate_keys(key_raw, positions).reshape(
-        row_count, steps_count, head_groups * head_size
-    )
-    new_values = summed[:, :, 1]
-    key_entries = new_keys.astype(jnp.bfloat16)
-    value_entries = new_values.astype(jnp.bfloat16)
-    fresh_heads = key_entries.reshape(row_count, steps_count, head_groups, head_size)
-    fresh_scores = (
-        jnp.einsum(
-            "rtghe,rsge->rtghs", query_heads, fresh_heads, preferred_element_type=jnp.float32
-        )
-        * scaling
-    )
-    causal = jnp.arange(steps_count)[:, None] >= jnp.arange(steps_count)[None, :]
-    fresh_scores = jnp.where(causal[None, :, None, None, :], fresh_scores, MASKED)
-    scores = jnp.concatenate([cache_scores, fresh_scores], axis=-1)
-    peak_score = jnp.max(scores, axis=-1, keepdims=True)
-    exponent = jnp.exp(scores - peak_score)
-    weights = (exponent / jnp.sum(exponent, axis=-1, keepdims=True)).astype(jnp.bfloat16)
-    fresh_value_heads = value_entries.reshape(row_count, steps_count, head_groups, head_size)
-    result = jnp.einsum(
-        "rtghp,rgpe->rtghe",
-        weights[..., :cache_slots],
-        stored_value_cache,
-        preferred_element_type=jnp.float32,
-    )
-    result = result + jnp.einsum(
-        "rtghs,rsge->rtghe",
-        weights[..., cache_slots:],
-        fresh_value_heads,
-        preferred_element_type=jnp.float32,
-    )
-    attended = result.reshape(row_count, steps_count, query_width)
+    angles = positions.astype(jnp.float32).reshape(-1, 1) * rope_frequencies(head_size)
+    cosine, sine = jnp.cos(angles), jnp.sin(angles)
+    cosine = jnp.concatenate([cosine, cosine], axis=1)
+    sine = jnp.concatenate([-sine, sine], axis=1)
+
+    fresh = jax.ShapeDtypeStruct((row_count, steps_count, columns), jnp.float32)
+    attended, new_keys, new_values = pl.pallas_call(
+        functools.partial(finish, own_rank=own_rank),
+        out_shape=(jax.ShapeDtypeStruct(queries.shape, jnp.float32), fresh, fresh),
+        in_specs=[pl.BlockSpec(memory_space=pltpu.VMEM)] * 8,
+        cost_estimate=pl.CostEstimate(
+            flops=4 * lines * own_lines * head_size * head_groups,
+            bytes_accessed=4 * queries.size,
+            transcendentals=lines * own_lines * head_groups,
+        ),
+    )(last, frozen_sum, cosine, sine, query_lines, peak, total, cached)
 
     def back_down(values):
         return values.reshape(kinds, own_rank, own_width)

time: 138 us -> 128 us (0.928)
  waiting for transfers between devices: 64.8 us -> 43.8 us
  starting transfers between devices: 48 us -> 57.5 us
  Pallas kernels: 0 us -> 6.01 us
  local copies, waits for them, and re-layouts: 11.9 us -> 9.16 us
  matrix products: 6 us -> 4.23 us
    all_to_all x6, waiting for transfers between devices: 64.8 us -> 33.3 us  [exchange(): return lax.all_to_all(pieces, axis, 0, 0, tiled=True)]
    ppermute x0 -> x4, starting transfers between devices: none -> 11.8 us  [scatter_sum_by_halves(): arrived = lax.ppermute(jnp.where(upper, low, high), axis, pairs)]
    ppermute x0 -> x4, waiting for transfers between devices: none -> 10.5 us  [scatter_sum_by_halves(): arrived = lax.ppermute(jnp.where(upper, low, high), axis, pairs)]
    pallas_call x0 -> x2, Pallas kernels: none -> 6.01 us  [the longest x1 3.19 us: body(): pl.pallas_call(cached_attention, out_shape=(column, column, jax.ShapeDtyp...]
    all_to_all x6, starting transfers between devices: 48 us -> 45.7 us  [exchange(): return lax.all_to_all(pieces, axis, 0, 0, tiled=True)]
    unnamed x27 -> x20, local copies, waits for them, and re-layouts: 2.64 us -> 0.74 us
    concatenate x0 -> x3, other arithmetic: none -> 1.38 us  [the longest x1 0.67 us: body(): cosine = jnp.concatenate([cosine, cosine], axis=1)]
    dot_general x12 -> x7, matrix products: 5.2 us -> 4.23 us  [product(): return jnp.einsum(spec, left, right, preferred_element_type=jnp.float32)]
  transfers between devices with their start and end apart: 6 -> 10, of which waited for: 6 -> 8; matrix products, arithmetic and copies ran while one was open for 5% -> 9% of each run, Pallas kernels for 0% -> 3%
where the time goes in v2:
time: 128 us; the launch traced here: 127 us
  starting transfers between devices  57.5 us (45%)
  waiting for transfers between devices  43.8 us (34%)
  local copies, waits for them, and re-layouts  9.16 us (7%)
  Pallas kernels  6.01 us (5%)
  other arithmetic  4.73 us (4%)
  matrix products  4.23 us (3%)
    all_to_all x6, starting transfers between devices, exchange(): return lax.all_to_all(pieces, axis, 0, 0, tiled=True)  45.7 us
    all_to_all x6, waiting for transfers between devices, exchange(): return lax.all_to_all(pieces, axis, 0, 0, tiled=True)  33.3 us
    ppermute x4, starting transfers between devices, scatter_sum_by_halves(): arrived = lax.ppermute(jnp.where(upper, low, high), axis, pairs)  11.8 us
    ppermute x4, waiting for transfers between devices, scatter_sum_by_halves(): arrived = lax.ppermute(jnp.where(upper, low, high), axis, pairs)  10.5 us
    dot_general x7, matrix products, product(): return jnp.einsum(spec, left, right, preferred_element_type=jnp.float32)  4.23 us
    pallas_call x1, Pallas kernels, body(): pl.pallas_call(cached_attention, out_shape=(column, column, jax.ShapeDtyp...  3.19 us
    pallas_call x1, Pallas kernels, body(): pl.pallas_call(functools.partial(finish, own_rank=own_rank), out_shape=(j...  2.82 us
  transfers between devices with their start and end apart: 10, of which 8 were waited for; matrix products, arithmetic and copies ran while one was open for 9% of the time, Pallas kernels for 3%

profile of v2, /device:TPU:1, one launch (start us, length us, event | category | flops | bytes accessed | tf_op | source)
XLA Modules:
  0.0 126.6 jit_solution(2094408443877385339)
XLA Ops:
  0.7 0.8 reshape.199
  1.5 0.7 convert_element_type.47
  2.2 0.8 broadcast_in_dim.24
  3.0 13.5 %all-to-all-start = ((bf16[32,4,1152]{2,1,0:T(4,128)(2,1)}), bf16[32,4,1152]{2,1,0:T(4,128)(2,1)S(1)}, u32[]{:S(2)}, u32[]{:S(2)}) async-start(bf16[32,4,1152]{2,1,0:T(4,128)(2,1)} %broadcast_in_dim.24), calls=%async_computation | async-start | bytes 589824 | tf_op jit(solution)/shard_map/all_to_all | solution.py:51
  16.4 1.0 reshape.205
  17.5 1.5 %fusion.2 = f32[128,512]{1,0:T(8,128)S(1)} fusion(bf16[128,1024]{1,0:T(8,128)(2,1)S(1)} %reshape.205, bf16[2,1024,512]{2,1,0:T(8,128)(2,1)} %param.22), kind=kOutput, calls=%fused_computation.7 | convolution fusion | flops 134217728 | bytes 1572864 | tf_op jit(solution)/shard_map/rd,dc->rc/dot_general | solution.py:64
  19.0 1.5 %fusion.4 = f32[128,512]{1,0:T(8,128)S(1)} fusion(bf16[128,1024]{1,0:T(8,128)(2,1)S(1)} %reshape.205, bf16[2,1024,512]{2,1,0:T(8,128)(2,1)} %param.22), kind=kOutput, calls=%fused_computation.9 | convolution fusion | flops 134217728 | bytes 1572864 | tf_op jit(solution)/shard_map/rd,dc->rc/dot_general | solution.py:64
  20.7 2.9 %collective-permute-start = (f32[2,2,2,8,1024]{4,3,2,1,0:T(8,128)S(1)}, f32[2,2,2,8,1024]{4,3,2,1,0:T(8,128)S(1)}, u32[]{:S(2)}, u32[]{:S(2)}) collective-permute-start(f32[2,2,2,8,1024]{4,3,2,1,0:T(8,128)S(1)} %select_bitcast_fusion), channel_id=1, source_target_pairs={{0,1},{1,0},{2,3},{3,2},{4,5},{5,4},{6,7},{7,6},{8,9},{9,8},{10,11... | collective-permute-start | bytes 786440 | tf_op jit(solution)/shard_map/ppermute | solution.py:79
  23.6 5.2 %all-to-all-done = bf16[32,4,1152]{2,1,0:T(4,128)(2,1)S(1)} async-done(((bf16[32,4,1152]{2,1,0:T(4,128)(2,1)}), bf16[32,4,1152]{2,1,0:T(4,128)(2,1)S(1)}, u32[]{:S(2)}, u32[]{:S(2)}) %all-to-all-start) | async-done | bytes 294944 | tf_op jit(solution)/shard_map/all_to_all | solution.py:51
  28.9 0.2 convolution_bitcast_fusion
  29.3 0.1 copy.30
  29.4 0.3 fusion.1
  29.7 0.1 copy.27
  29.8 0.7 pad_maximum_fusion.2
  30.5 12.5 %all-to-all-start.1 = ((bf16[16,16,256]{2,1,0:T(8,128)(2,1)}), bf16[16,16,256]{2,1,0:T(8,128)(2,1)S(1)}, u32[]{:S(2)}, u32[]{:S(2)}) async-start(bf16[16,16,256]{2,1,0:T(8,128)(2,1)} %pad_maximum_fusion.2), calls=%async_computation.1 | async-start | bytes 262144 | tf_op jit(solution)/shard_map/all_to_all | solution.py:51
  43.1 4.8 %collective-permute-start.1 = (f32[2,2,8,1024]{3,2,1,0:T(8,128)S(1)}, f32[2,2,8,1024]{3,2,1,0:T(8,128)S(1)}, u32[]{:S(2)}, u32[]{:S(2)}) collective-permute-start(f32[2,2,8,1024]{3,2,1,0:T(8,128)S(1)} %select_bitcast_fusion.1), channel_id=1, source_target_pairs={{0,8},{1,9},{2,10},{3,11},{4,12},{5,13},{6,14},{7,15},{8,0},{9,1},... | collective-permute-start | bytes 393224 | tf_op jit(solution)/shard_map/ppermute | solution.py:79
  47.9 5.2 %all-to-all-done.1 = bf16[16,16,256]{2,1,0:T(8,128)(2,1)S(1)} async-done(((bf16[16,16,256]{2,1,0:T(8,128)(2,1)}), bf16[16,16,256]{2,1,0:T(8,128)(2,1)S(1)}, u32[]{:S(2)}, u32[]{:S(2)}) %all-to-all-start.1) | async-done | bytes 131104 | tf_op jit(solution)/shard_map/all_to_all | solution.py:51
  53.1 0.7 broadcast_in_dim.26
  53.8 4.0 %all-to-all-start.2 = ((bf16[16,16,256]{2,1,0:T(8,128)(2,1)}), bf16[16,16,256]{2,1,0:T(8,128)(2,1)S(1)}, u32[]{:S(2)}, u32[]{:S(2)}) async-start(bf16[16,16,256]{2,1,0:T(8,128)(2,1)} %broadcast_in_dim.26), calls=%async_computation.2 | async-start | bytes 262144 | tf_op jit(solution)/shard_map/all_to_all | solution.py:51
  57.8 10.1 %all-to-all-done.2 = bf16[16,16,256]{2,1,0:T(8,128)(2,1)S(1)} async-done(((bf16[16,16,256]{2,1,0:T(8,128)(2,1)}), bf16[16,16,256]{2,1,0:T(8,128)(2,1)S(1)}, u32[]{:S(2)}, u32[]{:S(2)}) %all-to-all-start.2) | async-done | bytes 131104 | tf_op jit(solution)/shard_map/all_to_all | solution.py:51
  67.9 0.2 convolution_bitcast_fusion.1
  68.1 0.3 fusion
  68.5 0.8 reshape.203
  69.3 4.7 %all-to-all-start.3 = ((bf16[32,4,1152]{2,1,0:T(4,128)(2,1)}), bf16[32,4,1152]{2,1,0:T(4,128)(2,1)S(1)}, u32[]{:S(2)}, u32[]{:S(2)}) async-start(bf16[32,4,1152]{2,1,0:T(4,128)(2,1)} %reshape.203), calls=%async_computation.3 | async-start | bytes 589824 | tf_op jit(solution)/shard_map/all_to_all | solution.py:51
  74.0 2.1 %collective-permute-start.2 = (f32[2,8,1024]{2,1,0:T(8,128)S(1)}, f32[2,8,1024]{2,1,0:T(8,128)S(1)}, u32[]{:S(2)}, u32[]{:S(2)}) collective-permute-start(f32[2,8,1024]{2,1,0:T(8,128)S(1)} %select_bitcast_fusion.2), channel_id=1, source_target_pairs={{0,4},{1,5},{2,6},{3,7},{4,0},{5,1},{6,2},{7,3},{8,12},{9,13},{10,... | collective-permute-start | bytes 196616 | tf_op jit(solution)/shard_map/ppermute | solution.py:79
  76.2 3.3 %collective-permute-done.2 = f32[2,8,1024]{2,1,0:T(8,128)S(1)} collective-permute-done((f32[2,8,1024]{2,1,0:T(8,128)S(1)}, f32[2,8,1024]{2,1,0:T(8,128)S(1)}, u32[]{:S(2)}, u32[]{:S(2)}) %collective-permute-start.2) | collective-permute-done | bytes 65568 | tf_op jit(solution)/shard_map/ppermute | solution.py:79
  79.4 7.3 %all-to-all-done.3 = bf16[32,4,1152]{2,1,0:T(4,128)(2,1)S(1)} async-done(((bf16[32,4,1152]{2,1,0:T(4,128)(2,1)}), bf16[32,4,1152]{2,1,0:T(4,128)(2,1)S(1)}, u32[]{:S(2)}, u32[]{:S(2)}) %all-to-all-start.3) | async-done | bytes 294944 | tf_op jit(solution)/shard_map/all_to_all | solution.py:51
  86.8 0.1 convert_reduce_fusion
  87.0 0.6 fusion.28
  87.6 0.8 broadcast_in_dim.28
  88.4 4.4 %all-to-all-start.4 = ((bf16[32,4,1152]{2,1,0:T(4,128)(2,1)}), bf16[32,4,1152]{2,1,0:T(4,128)(2,1)S(1)}, u32[]{:S(2)}, u32[]{:S(2)}) async-start(bf16[32,4,1152]{2,1,0:T(4,128)(2,1)} %broadcast_in_dim.28), calls=%async_computation.4 | async-start | bytes 589824 | tf_op jit(solution)/shard_map/all_to_all | solution.py:51
  92.8 2.1 %collective-permute-start.3 = (f32[8,1024]{1,0:T(8,128)S(1)}, f32[8,1024]{1,0:T(8,128)S(1)}, u32[]{:S(2)}, u32[]{:S(2)}) collective-permute-start(f32[8,1024]{1,0:T(8,128)S(1)} %select_bitcast_fusion.3), channel_id=1, source_target_pairs={{0,2},{1,3},{2,0},{3,1},{4,6},{5,7},{6,4},{7,5},{8,10},{9,11},{10,... | collective-permute-start | bytes 98312 | tf_op jit(solution)/shard_map/ppermute | solution.py:79
  95.0 7.2 %collective-permute-done.3 = f32[8,1024]{1,0:T(8,128)S(1)} collective-permute-done((f32[8,1024]{1,0:T(8,128)S(1)}, f32[8,1024]{1,0:T(8,128)S(1)}, u32[]{:S(2)}, u32[]{:S(2)}) %collective-permute-start.3) | collective-permute-done | bytes 32800 | tf_op jit(solution)/shard_map/ppermute | solution.py:79
  102.3 0.6 bitcast_add_fusion.3.frozen_ref
  102.9 1.7 %all-to-all-done.4 = bf16[32,4,1152]{2,1,0:T(4,128)(2,1)S(1)} async-done(((bf16[32,4,1152]{2,1,0:T(4,128)(2,1)}), bf16[32,4,1152]{2,1,0:T(4,128)(2,1)S(1)}, u32[]{:S(2)}, u32[]{:S(2)}) %all-to-all-start.4) | async-done | bytes 294944 | tf_op jit(solution)/shard_map/all_to_all | solution.py:51
  104.6 0.2 reduce-precision_convert_fusion
  105.0 0.7 pad_maximum_fusion.1
  105.7 6.6 %all-to-all-start.5 = ((bf16[16,48,128]{2,1,0:T(8,128)(2,1)}), bf16[16,48,128]{2,1,0:T(8,128)(2,1)S(1)}, u32[]{:S(2)}, u32[]{:S(2)}) async-start(bf16[16,48,128]{2,1,0:T(8,128)(2,1)} %pad_maximum_fusion.1), calls=%async_computation.5 | async-start | bytes 393216 | tf_op jit(solution)/shard_map/all_to_all | solution.py:51
  112.4 0.2 reshape.207
  112.6 0.8 copy.35
  113.4 3.2 %shard_map.205 = (f32[4,128,1]{2,1,0:T(8,128)}, f32[4,128,1]{2,1,0:T(8,128)}, f32[4,128,128]{2,1,0:T(8,128)}) custom-call(s32[2]{0:T(128)} %lengths_ref.1, bf16[4,128,128]{2,1,0:T(8,128)(2,1)} %bitcast.99, bf16[2,4,256,128]{3,2,1,0:T(8,128)(2,1)} %key_ref.1, bf16[2,4,256,128]{3,2,1,0:T(8,128)(2,1)} %value_ref.1), custom_call_target="tpu_custom_call" | custom-call | flops 134217728 | bytes 1048576 | tf_op jit(solution)/shard_map/pallas_call | solution.py:283
  116.7 0.7 pad_maximum_fusion.3
  117.3 0.6 reshape.209
  118.0 0.6 reshape.211
  118.6 0.6 reshape.212
  119.2 3.9 %all-to-all-done.5.last_ref = bf16[16,48,128]{2,1,0:T(8,128)(2,1)S(1)} async-done(((bf16[16,48,128]{2,1,0:T(8,128)(2,1)}), bf16[16,48,128]{2,1,0:T(8,128)(2,1)S(1)}, u32[]{:S(2)}, u32[]{:S(2)}) %all-to-all-start.5) | async-done | bytes 196640 | tf_op jit(solution)/shard_map/all_to_all | solution.py:51
  123.1 0.7 copy-done.1
  123.8 2.8 %shard_map.206 = (f32[2,4,8192]{2,1,0:T(4,128)}, f32[2,4,512]{2,1,0:T(4,128)}, f32[2,4,512]{2,1,0:T(4,128)}) custom-call(bf16[16,48,128]{2,1,0:T(8,128)(2,1)} %copy-done.1, f32[8,1024]{1,0:T(8,128)} %bitcast_add_fusion.3.frozen_ref, f32[8,128]{1,0:T(8,128)} %get-tuple-element.40.cosine_ref, f32[8,128]{1,0:T(8,128)} %get-tuple-element.41.sine_ref, ...), custom_call_target="tpu_custom_call" | custom-call | flops 2097152 | bytes 262144 | tf_op jit(solution)/shard_map/pallas_call | solution.py:306
  (55 shorter events, 1.2 us)
Async XLA Ops:
  0.6 28.7 %copy-start = (bf16[256,1024]{1,0:T(8,128)(2,1)S(1)}, bf16[256,1024]{1,0:T(8,128)(2,1)}, u32[]{:S(2)}) copy-start(bf16[256,1024]{1,0:T(8,128)(2,1)} %param.14) | copy-start | bytes 1572868
  3.0 25.9 %all-to-all-start = ((bf16[32,4,1152]{2,1,0:T(4,128)(2,1)}), bf16[32,4,1152]{2,1,0:T(4,128)(2,1)S(1)}, u32[]{:S(2)}, u32[]{:S(2)}) async-start(bf16[32,4,1152]{2,1,0:T(4,128)(2,1)} %broadcast_in_dim.24), calls=%async_computation | async-start | bytes 589824 | tf_op jit(solution)/shard_map/all_to_all | solution.py:51
  19.0 4.6 %copy-start.4 = (f32[2,2,1024]{2,1,0:T(2,128)S(1)}, f32[2,2,1024]{2,1,0:T(2,128)}, u32[]{:S(2)}) copy-start(f32[2,2,1024]{2,1,0:T(2,128)} %param.18) | copy-start | bytes 49156
  19.0 4.6 %copy-start.5 = (f32[2,2,1024]{2,1,0:T(2,128)S(1)}, f32[2,2,1024]{2,1,0:T(2,128)}, u32[]{:S(2)}) copy-start(f32[2,2,1024]{2,1,0:T(2,128)} %param.19) | copy-start | bytes 49156
  19.0 9.9 %copy-start.3 = (bf16[2,32,256]{2,1,0:T(8,128)(2,1)S(1)}, bf16[2,32,256]{2,1,0:T(8,128)(2,1)}, u32[]{:S(2)}) copy-start(bf16[2,32,256]{2,1,0:T(8,128)(2,1)} %param.15) | copy-start | bytes 98308
  20.7 22.4 %collective-permute-start = (f32[2,2,2,8,1024]{4,3,2,1,0:T(8,128)S(1)}, f32[2,2,2,8,1024]{4,3,2,1,0:T(8,128)S(1)}, u32[]{:S(2)}, u32[]{:S(2)}) collective-permute-start(f32[2,2,2,8,1024]{4,3,2,1,0:T(8,128)S(1)} %select_bitcast_fusion), channel_id=1, source_target_pairs={{0,1},{1,0},{2,3},{3,2},{4,5},{5,4},{6,7},{7,6},{8,9},{9,8},{10,11... | collective-permute-start | bytes 786440 | tf_op jit(solution)/shard_map/ppermute | solution.py:79
  29.1 28.6 %copy-start.7 = (f32[2,32,2]{1,2,0:T(2,128)S(1)}, f32[2,32,2]{1,2,0:T(2,128)}, u32[]{:S(2)}) copy-start(f32[2,32,2]{1,2,0:T(2,128)} %param.20) | copy-start | bytes 1540
  30.5 22.6 %all-to-all-start.1 = ((bf16[16,16,256]{2,1,0:T(8,128)(2,1)}), bf16[16,16,256]{2,1,0:T(8,128)(2,1)S(1)}, u32[]{:S(2)}, u32[]{:S(2)}) async-start(bf16[16,16,256]{2,1,0:T(8,128)(2,1)} %pad_maximum_fusion.2), calls=%async_computation.1 | async-start | bytes 262144 | tf_op jit(solution)/shard_map/all_to_all | solution.py:51
  43.1 14.7 %collective-permute-start.1 = (f32[2,2,8,1024]{3,2,1,0:T(8,128)S(1)}, f32[2,2,8,1024]{3,2,1,0:T(8,128)S(1)}, u32[]{:S(2)}, u32[]{:S(2)}) collective-permute-start(f32[2,2,8,1024]{3,2,1,0:T(8,128)S(1)} %select_bitcast_fusion.1), channel_id=1, source_target_pairs={{0,8},{1,9},{2,10},{3,11},{4,12},{5,13},{6,14},{7,15},{8,0},{9,1},... | collective-permute-start | bytes 393224 | tf_op jit(solution)/shard_map/ppermute | solution.py:79
  53.1 23.0 %copy-start.8 = (f32[2,32,2]{1,2,0:T(2,128)S(1)}, f32[2,32,2]{1,2,0:T(2,128)}, u32[]{:S(2)}) copy-start(f32[2,32,2]{1,2,0:T(2,128)} %param.21) | copy-start | bytes 1540
  53.8 14.1 %all-to-all-start.2 = ((bf16[16,16,256]{2,1,0:T(8,128)(2,1)}), bf16[16,16,256]{2,1,0:T(8,128)(2,1)S(1)}, u32[]{:S(2)}, u32[]{:S(2)}) async-start(bf16[16,16,256]{2,1,0:T(8,128)(2,1)} %broadcast_in_dim.26), calls=%async_computation.2 | async-start | bytes 262144 | tf_op jit(solution)/shard_map/all_to_all | solution.py:51
  57.8 29.1 %copy-start.6 = (f32[2,32,2]{1,2,0:T(2,128)S(1)}, f32[2,32,2]{1,2,0:T(2,128)}, u32[]{:S(2)}) copy-start(f32[2,32,2]{1,2,0:T(2,128)} %param.17) | copy-start | bytes 1540
  68.3 26.6 %copy-start.9 = (s32[2]{0:T(128)S(1)}, s32[2]{0:T(128)}, u32[]{:S(2)}) copy-start(s32[2]{0:T(128)} %lengths_ref.1) | copy-start | bytes 28
  69.3 17.5 %all-to-all-start.3 = ((bf16[32,4,1152]{2,1,0:T(4,128)(2,1)}), bf16[32,4,1152]{2,1,0:T(4,128)(2,1)S(1)}, u32[]{:S(2)}, u32[]{:S(2)}) async-start(bf16[32,4,1152]{2,1,0:T(4,128)(2,1)} %reshape.203), calls=%async_computation.3 | async-start | bytes 589824 | tf_op jit(solution)/shard_map/all_to_all | solution.py:51
  74.0 38.5 %copy-start.2 = (bf16[2,4,8192]{2,1,0:T(4,128)(2,1)S(1)}, bf16[2,4,8192]{2,1,0:T(4,128)(2,1)}, u32[]{:S(2)}) copy-start(bf16[2,4,8192]{2,1,0:T(4,128)(2,1)} %param.24) | copy-start | bytes 393220
  74.0 5.4 %collective-permute-start.2 = (f32[2,8,1024]{2,1,0:T(8,128)S(1)}, f32[2,8,1024]{2,1,0:T(8,128)S(1)}, u32[]{:S(2)}, u32[]{:S(2)}) collective-permute-start(f32[2,8,1024]{2,1,0:T(8,128)S(1)} %select_bitcast_fusion.2), channel_id=1, source_target_pairs={{0,4},{1,5},{2,6},{3,7},{4,0},{5,1},{6,2},{7,3},{8,12},{9,13},{10,... | collective-permute-start | bytes 196616 | tf_op jit(solution)/shard_map/ppermute | solution.py:79
  88.4 16.2 %all-to-all-start.4 = ((bf16[32,4,1152]{2,1,0:T(4,128)(2,1)}), bf16[32,4,1152]{2,1,0:T(4,128)(2,1)S(1)}, u32[]{:S(2)}, u32[]{:S(2)}) async-start(bf16[32,4,1152]{2,1,0:T(4,128)(2,1)} %broadcast_in_dim.28), calls=%async_computation.4 | async-start | bytes 589824 | tf_op jit(solution)/shard_map/all_to_all | solution.py:51
  92.8 9.4 %collective-permute-start.3 = (f32[8,1024]{1,0:T(8,128)S(1)}, f32[8,1024]{1,0:T(8,128)S(1)}, u32[]{:S(2)}, u32[]{:S(2)}) collective-permute-start(f32[8,1024]{1,0:T(8,128)S(1)} %select_bitcast_fusion.3), channel_id=1, source_target_pairs={{0,2},{1,3},{2,0},{3,1},{4,6},{5,7},{6,4},{7,5},{8,10},{9,11},{10,... | collective-permute-start | bytes 98312 | tf_op jit(solution)/shard_map/ppermute | solution.py:79
  105.7 17.4 %all-to-all-start.5 = ((bf16[16,48,128]{2,1,0:T(8,128)(2,1)}), bf16[16,48,128]{2,1,0:T(8,128)(2,1)S(1)}, u32[]{:S(2)}, u32[]{:S(2)}) async-start(bf16[16,48,128]{2,1,0:T(8,128)(2,1)} %pad_maximum_fusion.1), calls=%async_computation.5 | async-start | bytes 393216 | tf_op jit(solution)/shard_map/all_to_all | solution.py:51
  123.1 0.7 copy-start.1

commit v3 on v2

--- a/solution.py
+++ b/solution.py
@@ -23,6 +23,7 @@
 HIGH_FACTOR = 4.0
 INITIAL_CONTEXT = 8192.0
 MASKED = -1e30
+KERNEL_BYTES = 8 * 1024 * 1024
 
 
 def rope_frequencies(head_size):
@@ -51,25 +52,18 @@
     return lax.all_to_all(pieces, axis, 0, 0, tiled=True)
 
 
-def gather_over(block, axis, count):
-    return exchange(jnp.broadcast_to(block[None], (count,) + block.shape), axis)
-
-
-def two_terms(values):
-    high = lax.reduce_precision(values, 8, 7)
-    return high.astype(jnp.bfloat16), (values - high).astype(jnp.bfloat16)
-
-
 def product(spec, left, right):
     return jnp.einsum(spec, left, right, preferred_element_type=jnp.float32)
 
 
-def scatter_sum_by_halves(values, axis, count):
+def scatter_sum_by_halves(values, axis, count, before_last):
     index = lax.axis_index(axis)
     bits = count.bit_length() - 1
     values = values.reshape((2,) * bits + values.shape[1:])
     left = list(range(bits - 1, -1, -1))
     for bit in [0] + list(range(bits - 1, 0, -1)):
+        if len(left) == 1:
+            before_last, values = lax.optimization_barrier((before_last, values))
         at = left.index(bit)
         left.remove(bit)
         low = lax.index_in_dim(values, 0, at, keepdims=False)
@@ -78,13 +72,148 @@
         pairs = [(place, place ^ (1 << bit)) for place in range(count)]
         arrived = lax.ppermute(jnp.where(upper, low, high), axis, pairs)
         values = jnp.where(upper, high, low) + arrived
-    return values
+    return before_last, values
 
 
 def dot_last(left, right):
     return lax.dot_general(
         left, right, (((1,), (1,)), ((), ())), preferred_element_type=jnp.float32
     )
+
+
+def dot_first(left, right):
+    return lax.dot_general(
+        left, right, (((0,), (0,)), ((), ())), preferred_element_type=jnp.float32
+    )
+
+
+def kind_of_row(shape, own_rank):
+    return lax.broadcasted_iota(jnp.int32, shape, 0) // own_rank % 2
+
+
+def stack_kinds(ref):
+    return jnp.concatenate([ref[0], ref[1]], axis=0)
+
+
+def send_masters(down_ref, up_ref, out_ref):
+    groups, _, wide = out_ref.shape
+    own_rank, own_width = down_ref.shape[1:]
+    own_columns = up_ref.shape[2]
+    rest = wide - own_width
+    rows = []
+    for kind in range(2):
+        line = up_ref[kind]
+        before = jnp.zeros((own_rank, kind * own_columns), jnp.float32)
+        after = jnp.zeros((own_rank, rest - (kind + 1) * own_columns), jnp.float32)
+        parts = [part for part in (before, line, after) if part.shape[1]]
+        rows.append(jnp.concatenate(parts, axis=1))
+    block = jnp.concatenate([stack_kinds(down_ref), jnp.concatenate(rows, axis=0)], axis=1)
+    block = block.astype(jnp.bfloat16)
+    for group in range(groups):
+        out_ref[group] = block
+
+
+def project_tokens(factors_ref, inputs_ref, cotangents_ref, out_ref):
+    all_rows = factors_ref.shape[0]
+    own_width = inputs_ref.shape[1]
+    both = cotangents_ref.shape[0]
+    projected = dot_last(inputs_ref[...], factors_ref[:, :own_width])
+    pulled = lax.dot_general(
+        cotangents_ref[...],
+        factors_ref[:, own_width : own_width + both],
+        (((0,), (1,)), ((), ())),
+        preferred_element_type=jnp.float32,
+    )
+    out_ref[:, :all_rows] = projected.astype(jnp.bfloat16)
+    out_ref[:, all_rows:] = pulled.astype(jnp.bfloat16)
+
+
+def sum_tokens(parts_ref, out_ref):
+    total = jnp.sum(parts_ref[...].astype(jnp.float32), axis=0).astype(jnp.bfloat16)
+    for rank in range(out_ref.shape[0]):
+        out_ref[rank] = total
+
+
+def send_gradients(tokens_ref, inputs_ref, cotangents_ref, out_ref, own_rank):
+    groups, own_rows, wide = out_ref.shape
+    all_rows = groups * own_rows
+    own_width = inputs_ref.shape[1]
+    both = cotangents_ref.shape[0]
+    down = ADAPTER_SCALE * dot_first(tokens_ref[:, all_rows:], inputs_ref[...])
+    cotangents = cotangents_ref[...]
+    if wide - own_width > both:
+        empty = jnp.zeros((wide - own_width - both, cotangents.shape[1]), jnp.bfloat16)
+        cotangents = jnp.concatenate([cotangents, empty], axis=0)
+    up = lax.dot_general(
+        tokens_ref[:, :all_rows],
+        cotangents,
+        (((0,), (1,)), ((), ())),
+        preferred_element_type=jnp.float32,
+    )
+    lane_kind = lax.broadcasted_iota(jnp.int32, up.shape, 1) // (both // 2)
+    up = jnp.where(lane_kind == kind_of_row(up.shape, own_rank), ADAPTER_SCALE * up, 0.0)
+    down = down.astype(jnp.bfloat16)
+    up = up.astype(jnp.bfloat16)
+    for group in range(groups):
+        rows = slice(group * own_rows, (group + 1) * own_rows)
+        out_ref[group, :, :own_width] = down[rows]
+        out_ref[group, :, own_width:] = up[rows]
+
+
+def update_factors(
+    parts_ref,
+    down_ref,
+    down_first_ref,
+    down_second_ref,
+    up_ref,
+    up_first_ref,
+    up_second_ref,
+    fresh_down_ref,
+    fresh_down_first_ref,
+    fresh_down_second_ref,
+    fresh_up_ref,
+    fresh_up_first_ref,
+    fresh_up_second_ref,
+    out_ref,
+):
+    groups = out_ref.shape[0]
+    own_rank, own_width = down_ref.shape[1:]
+    gradient = jnp.sum(parts_ref[...].astype(jnp.float32), axis=0)
+    down = optimizer_update(
+        stack_kinds(down_ref),
+        gradient[:, :own_width],
+        stack_kinds(down_first_ref),
+        stack_kinds(down_second_ref),
+    )
+    up = optimizer_update(
+        up_ref[...], gradient[:, own_width:], up_first_ref[...], up_second_ref[...]
+    )
+    for ref, values in zip(
+        (fresh_down_ref, fresh_down_first_ref, fresh_down_second_ref), down
+    ):
+        for kind in range(2):
+            ref[kind] = values[kind * own_rank : (kind + 1) * own_rank]
+    for ref, values in zip((fresh_up_ref, fresh_up_first_ref, fresh_up_second_ref), up):
+        ref[...] = values
+    block = jnp.concatenate([down[0], up[0]], axis=1).astype(jnp.bfloat16)
+    for group in range(groups):
+        out_ref[group] = block
+
+
+def send_rank_space(factors_ref, inputs_ref, out_ref, own_lines):
+    ranks, height, _ = out_ref.shape
+    own_columns = height - 2 * own_lines
+    own_width = inputs_ref.shape[1]
+    values = dot_last(inputs_ref[...], factors_ref[:, :own_width])
+    high = values.astype(jnp.bfloat16).astype(jnp.float32)
+    low = values - high
+    up = factors_ref[:, own_width:].astype(jnp.float32).T
+    up = (up[:own_columns] + up[own_columns : 2 * own_columns]).astype(jnp.bfloat16)
+    for rank in range(ranks):
+        rows = slice(rank * own_lines, (rank + 1) * own_lines)
+        both = jnp.concatenate([high[rows], low[rows]], axis=0)
+        out_ref[rank, : 2 * own_lines] = both.astype(jnp.bfloat16)
+        out_ref[rank, 2 * own_lines :] = up
 
 
 def cached_attention(lengths_ref, query_ref, key_ref, value_ref, peak_ref, total_ref, sum_ref):
@@ -203,75 +332,88 @@
     own_rows = kinds * own_rank
     all_rows = own_rows * groups
     own_lines = row_count * steps_count
-    lanes = 128
-    fill = -own_columns % lanes
-    is_value = (jnp.arange(all_rows) // own_rank) % kinds == 1
-
-    def own_down(values):
-        return values.reshape(own_rows, own_width)
-
-    def own_up(values):
-        return values.transpose(0, 2, 1).reshape(own_rows, own_columns)
-
-    def side_by_side(down, up):
-        parts = [down.astype(jnp.bfloat16), up.astype(jnp.bfloat16)]
-        return jnp.concatenate([parts[0], jnp.pad(parts[1], ((0, 0), (0, fill)))], axis=1)
-
-    def all_factors(down, up):
-        both = gather_over(side_by_side(down, up), "grp", groups).reshape(all_rows, -1)
-        return both[:, :own_width], both[:, own_width : own_width + own_columns]
+    wide = own_width + -(-kinds * own_columns // 128) * 128
+
+    def by_rank(values):
+        return values.transpose(0, 2, 1)
+
+    def placed(values):
+        rest = wide - own_width - own_columns
+        return jnp.concatenate(
+            [
+                jnp.pad(by_rank(values)[kind], ((0, 0), (at, rest - at)))
+                for kind, at in ((0, 0), (1, own_columns))
+            ]
+        )
+
+    def brought_back(values):
+        blocks = [
+            values[kind * own_rank : (kind + 1) * own_rank, at : at + own_columns]
+            for kind, at in ((0, 0), (1, own_columns))
+        ]
+        return by_rank(jnp.stack(blocks))
+
+    def call(kernel, outs, *operands):
+        flops = 4 * max(operand.size for operand in operands)
+        return pl.pallas_call(
+            kernel,
+            out_shape=outs,
+            in_specs=[pl.BlockSpec(memory_space=pltpu.VMEM)] * len(operands),
+            compiler_params=pltpu.CompilerParams(vmem_limit_bytes=KERNEL_BYTES),
+            cost_estimate=pl.CostEstimate(
+                flops=flops, bytes_accessed=flops, transcendentals=0
+            ),
+        )(*operands)
+
+    def out(shape, kind=jnp.bfloat16):
+        return jax.ShapeDtypeStruct(shape, kind)
 
     flat_inputs = decode_step_inputs.reshape(-1, own_width)
-    frozen_part = [
-        product("rd,dc->rc", flat_inputs, frozen_weights[kind]) for kind in range(kinds)
-    ]
-    frozen_sum = scatter_sum_by_halves(
-        jnp.concatenate(frozen_part, axis=1).reshape(ranks, own_lines, kinds * columns),
-        "tp",
-        ranks,
-    )
-
-    down, up = all_factors(own_down(adapter_down_master), own_up(adapter_up_master))
-    projected = product("td,nd->tn", trainer_token_inputs, down)
-    pulled = product("jct,nc->jtn", weighted_output_cotangents, up)
-    pulled = jnp.where(is_value[None, :], pulled[1], pulled[0])
-
-    pieces = jnp.concatenate([projected, pulled], axis=1).astype(jnp.bfloat16)
-    sums = (
-        exchange(pieces.reshape(ranks, -1, 2 * all_rows), "tp").astype(jnp.float32).sum(axis=0)
-    )
-    both = gather_over(sums.astype(jnp.bfloat16), "tp", ranks).reshape(tokens, 2 * all_rows)
-    projected, pulled = both[:, :all_rows], both[:, all_rows:]
-
-    down_gradient = ADAPTER_SCALE * product("tn,td->nd", pulled, trainer_token_inputs)
-    up_gradient = product("jct,tn->jnc", weighted_output_cotangents, projected)
-    up_gradient = ADAPTER_SCALE * jnp.where(is_value[:, None], up_gradient[1], up_gradient[0])
-
-    totals = (
-        exchange(
-            side_by_side(down_gradient, up_gradient).reshape(groups, own_rows, -1), "grp"
-        )
-        .astype(jnp.float32)
-        .sum(axis=0)
-    )
-    fresh_down = optimizer_update(
-        own_down(adapter_down_master),
-        totals[:, :own_width],
-        own_down(down_first_moment),
-        own_down(down_second_moment),
-    )
-    fresh_up = optimizer_update(
-        own_up(adapter_up_master),
-        totals[:, own_width : own_width + own_columns],
-        own_up(up_first_moment),
-        own_up(up_second_moment),
-    )
-    down, up = all_factors(fresh_down[0], fresh_up[0])
-    up, frozen_sum = lax.optimization_barrier((up, frozen_sum))
-    adapter_part = product("rd,nd->rn", flat_inputs, down).reshape(ranks, own_lines, all_rows)
-
-    up_copies = jnp.broadcast_to(up.transpose()[None], (ranks, own_columns, all_rows))
-    last = exchange(jnp.concatenate([*two_terms(adapter_part), up_copies], axis=1), "tp")
+    frozen_part = jnp.concatenate(
+        [product("rd,dc->rc", flat_inputs, frozen_weights[kind]) for kind in range(kinds)], axis=1
+    ).reshape(ranks, own_lines, kinds * columns)
+
+    sent = out((groups, own_rows, wide))
+    masters = call(send_masters, sent, adapter_down_master, by_rank(adapter_up_master))
+    factors = exchange(masters, "grp").reshape(all_rows, wide)
+
+    cotangents = weighted_output_cotangents.reshape(-1, tokens)
+    shares = call(
+        project_tokens, out((tokens, 2 * all_rows)), factors, trainer_token_inputs, cotangents
+    ).reshape(ranks, -1, 2 * all_rows)
+    sums = call(sum_tokens, out(shares.shape), exchange(shares, "tp"))
+    token_sums = exchange(sums, "tp").reshape(tokens, 2 * all_rows)
+
+    gradients = call(
+        functools.partial(send_gradients, own_rank=own_rank),
+        sent,
+        token_sums,
+        trainer_token_inputs,
+        cotangents,
+    )
+    gradients, frozen_sum = scatter_sum_by_halves(frozen_part, "tp", ranks, gradients)
+    own = out(adapter_down_master.shape, jnp.float32)
+    small = out((own_rows, wide - own_width), jnp.float32)
+    *fresh, fresh_factors = call(
+        update_factors,
+        (own, own, own, small, small, small, sent),
+        exchange(gradients, "grp"),
+        adapter_down_master,
+        down_first_moment,
+        down_second_moment,
+        placed(adapter_up_master),
+        placed(up_first_moment),
+        placed(up_second_moment),
+    )
+    fresh_factors, frozen_sum = lax.optimization_barrier((fresh_factors, frozen_sum))
+    factors = exchange(fresh_factors, "grp").reshape(all_rows, wide)
+
+    rank_space = call(
+        functools.partial(send_rank_space, own_lines=own_lines),
+        out((ranks, 2 * own_lines + own_columns, all_rows)),
+        factors,
+        flat_inputs,
+    )
 
     lines = query_width // (head_groups * head_size) * own_lines
     query_lines = (
@@ -289,6 +431,7 @@
         ),
         in_specs=[pl.BlockSpec(memory_space=pltpu.SMEM)]
         + [pl.BlockSpec(memory_space=pltpu.VMEM)] * 3,
+        compiler_params=pltpu.CompilerParams(vmem_limit_bytes=KERNEL_BYTES),
         cost_estimate=pl.CostEstimate(
             flops=8 * lines * cache_slots * head_size * head_groups,
             bytes_accessed=4 * row_count * head_groups * cache_slots * head_size,
@@ -302,11 +445,16 @@
     cosine = jnp.concatenate([cosine, cosine], axis=1)
     sine = jnp.concatenate([-sine, sine], axis=1)
 
-    fresh = jax.ShapeDtypeStruct((row_count, steps_count, columns), jnp.float32)
+    rank_space, peak, total, cached, cosine, sine = lax.optimization_barrier(
+        (rank_space, peak, total, cached, cosine, sine)
+    )
+    last = exchange(rank_space, "tp")
+    entries = jax.ShapeDtypeStruct((row_count, steps_count, columns), jnp.float32)
     attended, new_keys, new_values = pl.pallas_call(
         functools.partial(finish, own_rank=own_rank),
-        out_shape=(jax.ShapeDtypeStruct(queries.shape, jnp.float32), fresh, fresh),
+        out_shape=(jax.ShapeDtypeStruct(queries.shape, jnp.float32), entries, entries),
         in_specs=[pl.BlockSpec(memory_space=pltpu.VMEM)] * 8,
+        compiler_params=pltpu.CompilerParams(vmem_limit_bytes=KERNEL_BYTES),
         cost_estimate=pl.CostEstimate(
             flops=4 * lines * own_lines * head_size * head_groups,
             bytes_accessed=4 * queries.size,
@@ -314,22 +462,16 @@
         ),
     )(last, frozen_sum, cosine, sine, query_lines, peak, total, cached)
 
-    def back_down(values):
-        return values.reshape(kinds, own_rank, own_width)
-
-    def back_up(values):
-        return values.reshape(kinds, own_rank, own_columns).transpose(0, 2, 1)
-
     return (
         attended,
         new_keys,
         new_values,
-        back_down(fresh_down[0]),
-        back_up(fresh_up[0]),
-        back_down(fresh_down[1]),
-        back_down(fresh_down[2]),
-        back_up(fresh_up[1]),
-        back_up(fresh_up[2]),
+        fresh[0],
+        brought_back(fresh[3]),
+        fresh[1],
+        fresh[2],
+        brought_back(fresh[4]),
+        brought_back(fresh[5]),
     )
 
 

time: 128 us -> 130 us (1.016)
  waiting for transfers between devices: 43.8 us -> 53.2 us
  local copies, waits for them, and re-layouts: 9.16 us -> 1.88 us
  starting transfers between devices: 57.5 us -> 60.6 us
  Pallas kernels: 6.01 us -> 8.59 us
  matrix products: 4.23 us -> 1.84 us
  other arithmetic: 4.73 us -> 2.45 us
    all_to_all x6, waiting for transfers between devices: 33.3 us -> 46.8 us  [exchange(): return lax.all_to_all(pieces, axis, 0, 0, tiled=True)]
    ppermute x4, starting transfers between devices: 11.8 us -> 19.1 us  [scatter_sum_by_halves(): arrived = lax.ppermute(jnp.where(upper, low, high), axis, pairs)]
    pallas_call x0 -> x6, Pallas kernels: none -> 5.35 us  [call(): pl.pallas_call(kernel, out_shape=outs, in_specs=[pl.BlockSpec(memory_spac...]
    all_to_all x6, starting transfers between devices: 45.7 us -> 41.5 us  [exchange(): return lax.all_to_all(pieces, axis, 0, 0, tiled=True)]
    ppermute x4, waiting for transfers between devices: 10.5 us -> 6.42 us  [scatter_sum_by_halves(): arrived = lax.ppermute(jnp.where(upper, low, high), axis, pairs)]
    reshape x7 -> x2, local copies, waits for them, and re-layouts: 3.61 us -> 0.14 us  [the longest x1 0.07 us: body(): factors = exchange(fresh_factors, 'grp').reshape(all_rows, wide)]
    dot_general x7 -> x2, matrix products: 4.23 us -> 1.84 us  [product(): return jnp.einsum(spec, left, right, preferred_element_type=jnp.float32)]
    broadcast_in_dim x4 -> x0, local copies, waits for them, and re-layouts: 2.31 us -> none  [the longest x3 2.27 us: gather_over(): return exchange(jnp.broadcast_to(block[None], (count,) + block.shape), axis)]
  transfers between devices with their start and end apart: 10 -> 10, of which waited for: 8 -> 7; matrix products, arithmetic and copies ran while one was open for 9% -> 2% of each run, Pallas kernels for 3% -> 3%
where the time goes in v3:
time: 130 us
  starting transfers between devices  60.6 us (47%)
  waiting for transfers between devices  53.2 us (41%)
  Pallas kernels  8.59 us (7%)
  other arithmetic  2.45 us (2%)
  local copies, waits for them, and re-layouts  1.88 us (1%)
  matrix products  1.84 us (1%)
    all_to_all x6, waiting for transfers between devices, exchange(): return lax.all_to_all(pieces, axis, 0, 0, tiled=True)  46.8 us
    all_to_all x6, starting transfers between devices, exchange(): return lax.all_to_all(pieces, axis, 0, 0, tiled=True)  41.5 us
    ppermute x4, starting transfers between devices, scatter_sum_by_halves(): arrived = lax.ppermute(jnp.where(upper, low, high), axis, pairs)  19.1 us
    ppermute x4, waiting for transfers between devices, scatter_sum_by_halves(): arrived = lax.ppermute(jnp.where(upper, low, high), axis, pairs)  6.42 us
    pallas_call x6, Pallas kernels, call(): pl.pallas_call(kernel, out_shape=outs, in_specs=[pl.BlockSpec(memory_spac...  5.35 us
  transfers between devices with their start and end apart: 10, of which 7 were waited for; matrix products, arithmetic and copies ran while one was open for 2% of the time, Pallas kernels for 3%

profile of v3, /device:TPU:1, one launch (start us, length us, event | category | flops | bytes accessed | tf_op | source)
XLA Modules:
  0.0 129.6 jit_solution(10332258507381053239)
XLA Ops:
  0.7 1.2 reshape.101.inputs_ref
  1.8 1.5 %fusion = f32[128,512]{1,0:T(8,128)S(1)} fusion(bf16[128,1024]{1,0:T(8,128)(2,1)S(1)} %reshape.101.inputs_ref, bf16[2,1024,512]{2,1,0:T(8,128)(2,1)} %param.22), kind=kOutput, calls=%fused_computation | convolution fusion | flops 134217728 | bytes 1572864 | tf_op jit(solution)/shard_map/rd,dc->rc/dot_general | solution.py:56
  3.4 0.0 copy-start.4
  3.4 0.0 copy-start.7
  3.4 0.3 fusion.2
  3.8 0.0 copy-start
  3.9 8.9 %collective-permute-start = (f32[2,2,2,8,1024]{4,3,2,1,0:T(8,128)S(1)}, f32[2,2,2,8,1024]{4,3,2,1,0:T(8,128)S(1)}, u32[]{:S(2)}, u32[]{:S(2)}) collective-permute-start(f32[2,2,2,8,1024]{4,3,2,1,0:T(8,128)S(1)} %select_bitcast_fusion), channel_id=1, source_target_pairs={{0,1},{1,0},{2,3},{3,2},{4,5},{5,4},{6,7},{7,6},{8,9},{9,8},{10,11... | collective-permute-start | bytes 786440 | tf_op jit(solution)/shard_map/ppermute | solution.py:73
  12.8 0.8 shard_map.205
  13.6 7.3 %all-to-all-start = ((bf16[32,4,1152]{2,1,0:T(4,128)(2,1)}), bf16[32,4,1152]{2,1,0:T(4,128)(2,1)S(1)}, u32[]{:S(2)}, u32[]{:S(2)}) async-start(bf16[32,4,1152]{2,1,0:T(4,128)(2,1)} %shard_map.205), calls=%async_computation | async-start | bytes 589824 | tf_op jit(solution)/shard_map/all_to_all | solution.py:52
  21.0 4.6 %collective-permute-start.1 = (f32[2,2,8,1024]{3,2,1,0:T(8,128)S(1)}, f32[2,2,8,1024]{3,2,1,0:T(8,128)S(1)}, u32[]{:S(2)}, u32[]{:S(2)}) collective-permute-start(f32[2,2,8,1024]{3,2,1,0:T(8,128)S(1)} %select_bitcast_fusion.1), channel_id=1, source_target_pairs={{0,8},{1,9},{2,10},{3,11},{4,12},{5,13},{6,14},{7,15},{8,0},{9,1},... | collective-permute-start | bytes 393224 | tf_op jit(solution)/shard_map/ppermute | solution.py:73
  25.7 0.1 add_convert_fusion
  25.8 0.1 select_maximum_fusion.2.up_ref
  25.9 8.3 %all-to-all-done = bf16[32,4,1152]{2,1,0:T(4,128)(2,1)S(1)} async-done(((bf16[32,4,1152]{2,1,0:T(4,128)(2,1)}), bf16[32,4,1152]{2,1,0:T(4,128)(2,1)S(1)}, u32[]{:S(2)}, u32[]{:S(2)}) %all-to-all-start) | async-done | bytes 294944 | tf_op jit(solution)/shard_map/all_to_all | solution.py:52
  34.2 0.1 reshape.97.factors_ref
  34.3 0.0 copy-start.9
  34.3 1.0 shard_map.206
  35.3 12.1 %all-to-all-start.1 = ((bf16[16,16,256]{2,1,0:T(8,128)(2,1)}), bf16[16,16,256]{2,1,0:T(8,128)(2,1)S(1)}, u32[]{:S(2)}, u32[]{:S(2)}) async-start(bf16[16,16,256]{2,1,0:T(8,128)(2,1)} %bitcast.2), calls=%async_computation.1 | async-start | bytes 262144 | tf_op jit(solution)/shard_map/all_to_all | solution.py:52
  47.5 3.4 %collective-permute-start.2 = (f32[2,8,1024]{2,1,0:T(8,128)S(1)}, f32[2,8,1024]{2,1,0:T(8,128)S(1)}, u32[]{:S(2)}, u32[]{:S(2)}) collective-permute-start(f32[2,8,1024]{2,1,0:T(8,128)S(1)} %select_bitcast_fusion.2), channel_id=1, source_target_pairs={{0,4},{1,5},{2,6},{3,7},{4,0},{5,1},{6,2},{7,3},{8,12},{9,13},{10,... | collective-permute-start | bytes 196616 | tf_op jit(solution)/shard_map/ppermute | solution.py:73
  50.9 6.5 %all-to-all-done.1.parts_ref = bf16[16,16,256]{2,1,0:T(8,128)(2,1)S(1)} async-done(((bf16[16,16,256]{2,1,0:T(8,128)(2,1)}), bf16[16,16,256]{2,1,0:T(8,128)(2,1)S(1)}, u32[]{:S(2)}, u32[]{:S(2)}) %all-to-all-start.1) | async-done | bytes 131104 | tf_op jit(solution)/shard_map/all_to_all | solution.py:52
  57.4 0.7 shard_map.207
  58.1 4.0 %all-to-all-start.2 = ((bf16[16,16,256]{2,1,0:T(8,128)(2,1)}), bf16[16,16,256]{2,1,0:T(8,128)(2,1)S(1)}, u32[]{:S(2)}, u32[]{:S(2)}) async-start(bf16[16,16,256]{2,1,0:T(8,128)(2,1)} %shard_map.207), calls=%async_computation.2 | async-start | bytes 262144 | tf_op jit(solution)/shard_map/all_to_all | solution.py:52
  62.1 0.1 select_maximum_fusion.1.up_first_ref
  62.2 10.0 %all-to-all-done.2 = bf16[16,16,256]{2,1,0:T(8,128)(2,1)S(1)} async-done(((bf16[16,16,256]{2,1,0:T(8,128)(2,1)}), bf16[16,16,256]{2,1,0:T(8,128)(2,1)S(1)}, u32[]{:S(2)}, u32[]{:S(2)}) %all-to-all-start.2) | async-done | bytes 131104 | tf_op jit(solution)/shard_map/all_to_all | solution.py:52
  72.2 1.0 shard_map.208
  73.2 4.3 %all-to-all-start.3 = ((bf16[32,4,1152]{2,1,0:T(4,128)(2,1)}), bf16[32,4,1152]{2,1,0:T(4,128)(2,1)S(1)}, u32[]{:S(2)}, u32[]{:S(2)}) async-start(bf16[32,4,1152]{2,1,0:T(4,128)(2,1)} %shard_map.208), calls=%async_computation.3 | async-start | bytes 589824 | tf_op jit(solution)/shard_map/all_to_all | solution.py:52
  77.6 0.1 select_maximum_fusion.up_second_ref
  77.6 2.1 %collective-permute-start.3 = (f32[8,1024]{1,0:T(8,128)S(1)}, f32[8,1024]{1,0:T(8,128)S(1)}, u32[]{:S(2)}, u32[]{:S(2)}) collective-permute-start(f32[8,1024]{1,0:T(8,128)S(1)} %select_bitcast_fusion.3), channel_id=1, source_target_pairs={{0,2},{1,3},{2,0},{3,1},{4,6},{5,7},{6,4},{7,5},{8,10},{9,11},{10,... | collective-permute-start | bytes 98312 | tf_op jit(solution)/shard_map/ppermute | solution.py:73
  79.7 0.1 convert_element_type.19
  79.8 0.2 reshape.103
  80.0 0.1 copy.26
  80.1 6.4 %collective-permute-done.3 = f32[8,1024]{1,0:T(8,128)S(1)} collective-permute-done((f32[8,1024]{1,0:T(8,128)S(1)}, f32[8,1024]{1,0:T(8,128)S(1)}, u32[]{:S(2)}, u32[]{:S(2)}) %collective-permute-start.3) | collective-permute-done | bytes 32800 | tf_op jit(solution)/shard_map/ppermute | solution.py:73
  86.5 3.8 %all-to-all-done.3.parts_ref = bf16[32,4,1152]{2,1,0:T(4,128)(2,1)S(1)} async-done(((bf16[32,4,1152]{2,1,0:T(4,128)(2,1)}), bf16[32,4,1152]{2,1,0:T(4,128)(2,1)S(1)}, u32[]{:S(2)}, u32[]{:S(2)}) %all-to-all-start.3) | async-done | bytes 294944 | tf_op jit(solution)/shard_map/all_to_all | solution.py:52
  90.4 0.9 shard_map.209
  91.3 5.6 %all-to-all-start.4 = ((bf16[32,4,1152]{2,1,0:T(4,128)(2,1)}), bf16[32,4,1152]{2,1,0:T(4,128)(2,1)S(1)}, u32[]{:S(2)}, u32[]{:S(2)}) async-start(bf16[32,4,1152]{2,1,0:T(4,128)(2,1)} %get-tuple-element.35), calls=%async_computation.4 | async-start | bytes 589824 | tf_op jit(solution)/shard_map/all_to_all | solution.py:52
  96.9 1.7 %shard_map.211 = (f32[4,128,1]{2,1,0:T(8,128)S(1)}, f32[4,128,1]{2,1,0:T(8,128)S(1)}, f32[4,128,128]{2,1,0:T(8,128)S(1)}) custom-call(s32[2]{0:T(128)S(1)} %copy-done.8, bf16[4,128,128]{2,1,0:T(8,128)(2,1)S(1)} %bitcast.76, bf16[2,4,256,128]{3,2,1,0:T(8,128)(2,1)S(1)} %copy-done.1, bf16[2,4,256,128]{3,2,1,0:T(8,128)(2,1)S(1)} %copy-done.2), custom_call_target="tpu_custom_call" | custom-call | flops 134217728 | bytes 1048576 | tf_op jit(solution)/shard_map/pallas_call | solution.py:425
  98.6 0.1 fusion.6
  98.8 0.1 pad_maximum_fusion.1
  98.8 0.1 slice_bitcast_fusion.9
  98.9 9.3 %all-to-all-done.4 = bf16[32,4,1152]{2,1,0:T(4,128)(2,1)S(1)} async-done(((bf16[32,4,1152]{2,1,0:T(4,128)(2,1)}), bf16[32,4,1152]{2,1,0:T(4,128)(2,1)S(1)}, u32[]{:S(2)}, u32[]{:S(2)}) %all-to-all-start.4) | async-done | bytes 294944 | tf_op jit(solution)/shard_map/all_to_all | solution.py:52
  108.2 0.1 reshape.102.factors_ref
  108.2 0.9 shard_map.210
  109.2 8.3 %all-to-all-start.5 = ((bf16[16,48,128]{2,1,0:T(8,128)(2,1)}), bf16[16,48,128]{2,1,0:T(8,128)(2,1)S(1)}, u32[]{:S(2)}, u32[]{:S(2)}) async-start(bf16[16,48,128]{2,1,0:T(8,128)(2,1)} %shard_map.210), calls=%async_computation.5 | async-start | bytes 393216 | tf_op jit(solution)/shard_map/all_to_all | solution.py:52
  117.4 0.1 slice_bitcast_fusion.13
  117.5 0.6 maximum_bitcast_fusion
  118.1 0.6 maximum_bitcast_fusion.2
  118.7 0.6 maximum_bitcast_fusion.1
  119.2 8.8 %all-to-all-done.5.last_ref = bf16[16,48,128]{2,1,0:T(8,128)(2,1)S(1)} async-done(((bf16[16,48,128]{2,1,0:T(8,128)(2,1)}), bf16[16,48,128]{2,1,0:T(8,128)(2,1)S(1)}, u32[]{:S(2)}, u32[]{:S(2)}) %all-to-all-start.5) | async-done | bytes 196640 | tf_op jit(solution)/shard_map/all_to_all | solution.py:52
  128.1 1.5 %shard_map.212 = (f32[2,4,8192]{2,1,0:T(4,128)}, f32[2,4,512]{2,1,0:T(4,128)}, f32[2,4,512]{2,1,0:T(4,128)}) custom-call(bf16[16,48,128]{2,1,0:T(8,128)(2,1)S(1)} %all-to-all-done.5.last_ref, f32[8,1024]{1,0:T(8,128)S(1)} %bitcast_add_fusion.3.frozen_ref, f32[8,128]{1,0:T(8,128)S(1)} %get-tuple-element.41.cosine_ref, ...), custom_call_target="tpu_custom_call" | custom-call | flops 2097152 | bytes 262144 | tf_op jit(solution)/shard_map/pallas_call | solution.py:453
  (38 shorter events, 0.3 us)
Async XLA Ops:
  0.6 2.7 %copy-start.12 = (bf16[2,1024,512]{2,1,0:T(8,128)(2,1)S(1)}, bf16[2,1024,512]{2,1,0:T(8,128)(2,1)}, u32[]{:S(2)}) copy-start(bf16[2,1024,512]{2,1,0:T(8,128)(2,1)} %param.22) | copy-start | bytes 6291460
  3.4 9.4 %copy-start.4 = (f32[2,2,1024]{2,1,0:T(2,128)S(1)}, f32[2,2,1024]{2,1,0:T(2,128)}, u32[]{:S(2)}) copy-start(f32[2,2,1024]{2,1,0:T(2,128)} %down_ref.3) | copy-start | bytes 49156
  3.4 9.4 %copy-start.7 = (f32[2,32,2]{1,2,0:T(2,128)S(1)}, f32[2,32,2]{1,2,0:T(2,128)}, u32[]{:S(2)}) copy-start(f32[2,32,2]{1,2,0:T(2,128)} %param.17) | copy-start | bytes 1540
  3.4 17.5 %copy-start.10 = (f32[2,32,2]{1,2,0:T(2,128)S(1)}, f32[2,32,2]{1,2,0:T(2,128)}, u32[]{:S(2)}) copy-start(f32[2,32,2]{1,2,0:T(2,128)} %param.20) | copy-start | bytes 1540
  3.4 17.5 %copy-start.11 = (f32[2,32,2]{1,2,0:T(2,128)S(1)}, f32[2,32,2]{1,2,0:T(2,128)}, u32[]{:S(2)}) copy-start(f32[2,32,2]{1,2,0:T(2,128)} %param.21) | copy-start | bytes 1540
  3.7 22.0 %copy-start.8 = (s32[2]{0:T(128)S(1)}, s32[2]{0:T(128)}, u32[]{:S(2)}) copy-start(s32[2]{0:T(128)} %lengths_ref.1) | copy-start | bytes 28
  3.8 30.4 %copy-start = (bf16[256,1024]{1,0:T(8,128)(2,1)S(1)}, bf16[256,1024]{1,0:T(8,128)(2,1)}, u32[]{:S(2)}) copy-start(bf16[256,1024]{1,0:T(8,128)(2,1)} %inputs_ref.3) | copy-start | bytes 1572868
  3.8 30.4 %copy-start.3 = (bf16[2,32,256]{2,1,0:T(8,128)(2,1)S(1)}, bf16[2,32,256]{2,1,0:T(8,128)(2,1)}, u32[]{:S(2)}) copy-start(bf16[2,32,256]{2,1,0:T(8,128)(2,1)} %param.15) | copy-start | bytes 98308
  3.9 17.1 %collective-permute-start = (f32[2,2,2,8,1024]{4,3,2,1,0:T(8,128)S(1)}, f32[2,2,2,8,1024]{4,3,2,1,0:T(8,128)S(1)}, u32[]{:S(2)}, u32[]{:S(2)}) collective-permute-start(f32[2,2,2,8,1024]{4,3,2,1,0:T(8,128)S(1)} %select_bitcast_fusion), channel_id=1, source_target_pairs={{0,1},{1,0},{2,3},{3,2},{4,5},{5,4},{6,7},{7,6},{8,9},{9,8},{10,11... | collective-permute-start | bytes 786440 | tf_op jit(solution)/shard_map/ppermute | solution.py:73
  13.6 20.5 %all-to-all-start = ((bf16[32,4,1152]{2,1,0:T(4,128)(2,1)}), bf16[32,4,1152]{2,1,0:T(4,128)(2,1)S(1)}, u32[]{:S(2)}, u32[]{:S(2)}) async-start(bf16[32,4,1152]{2,1,0:T(4,128)(2,1)} %shard_map.205), calls=%async_computation | async-start | bytes 589824 | tf_op jit(solution)/shard_map/all_to_all | solution.py:52
  21.0 26.3 %collective-permute-start.1 = (f32[2,2,8,1024]{3,2,1,0:T(8,128)S(1)}, f32[2,2,8,1024]{3,2,1,0:T(8,128)S(1)}, u32[]{:S(2)}, u32[]{:S(2)}) collective-permute-start(f32[2,2,8,1024]{3,2,1,0:T(8,128)S(1)} %select_bitcast_fusion.1), channel_id=1, source_target_pairs={{0,8},{1,9},{2,10},{3,11},{4,12},{5,13},{6,14},{7,15},{8,0},{9,1},... | collective-permute-start | bytes 393224 | tf_op jit(solution)/shard_map/ppermute | solution.py:73
  34.3 45.6 %copy-start.9 = (bf16[2,4,8192]{2,1,0:T(4,128)(2,1)S(1)}, bf16[2,4,8192]{2,1,0:T(4,128)(2,1)}, u32[]{:S(2)}) copy-start(bf16[2,4,8192]{2,1,0:T(4,128)(2,1)} %param.24) | copy-start | bytes 393220
  35.3 55.1 %copy-start.5 = (f32[2,2,1024]{2,1,0:T(2,128)S(1)}, f32[2,2,1024]{2,1,0:T(2,128)}, u32[]{:S(2)}) copy-start(f32[2,2,1024]{2,1,0:T(2,128)} %down_first_ref.1) | copy-start | bytes 49156
  35.3 55.1 %copy-start.6 = (f32[2,2,1024]{2,1,0:T(2,128)S(1)}, f32[2,2,1024]{2,1,0:T(2,128)}, u32[]{:S(2)}) copy-start(f32[2,2,1024]{2,1,0:T(2,128)} %down_second_ref.1) | copy-start | bytes 49156
  35.3 22.2 %all-to-all-start.1 = ((bf16[16,16,256]{2,1,0:T(8,128)(2,1)}), bf16[16,16,256]{2,1,0:T(8,128)(2,1)S(1)}, u32[]{:S(2)}, u32[]{:S(2)}) async-start(bf16[16,16,256]{2,1,0:T(8,128)(2,1)} %bitcast.2), calls=%async_computation.1 | async-start | bytes 262144 | tf_op jit(solution)/shard_map/all_to_all | solution.py:52
  47.4 49.5 %copy-start.1 = (bf16[2,4,256,128]{3,2,1,0:T(8,128)(2,1)S(1)}, bf16[2,4,256,128]{3,2,1,0:T(8,128)(2,1)}, u32[]{:S(2)}) copy-start(bf16[2,4,256,128]{3,2,1,0:T(8,128)(2,1)} %key_ref.1) | copy-start | bytes 1572868
  47.4 49.5 %copy-start.2 = (bf16[2,4,256,128]{3,2,1,0:T(8,128)(2,1)S(1)}, bf16[2,4,256,128]{3,2,1,0:T(8,128)(2,1)}, u32[]{:S(2)}) copy-start(bf16[2,4,256,128]{3,2,1,0:T(8,128)(2,1)} %value_ref.1) | copy-start | bytes 1572868
  47.5 14.7 %collective-permute-start.2 = (f32[2,8,1024]{2,1,0:T(8,128)S(1)}, f32[2,8,1024]{2,1,0:T(8,128)S(1)}, u32[]{:S(2)}, u32[]{:S(2)}) collective-permute-start(f32[2,8,1024]{2,1,0:T(8,128)S(1)} %select_bitcast_fusion.2), channel_id=1, source_target_pairs={{0,4},{1,5},{2,6},{3,7},{4,0},{5,1},{6,2},{7,3},{8,12},{9,13},{10,... | collective-permute-start | bytes 196616 | tf_op jit(solution)/shard_map/ppermute | solution.py:73
  58.1 14.1 %all-to-all-start.2 = ((bf16[16,16,256]{2,1,0:T(8,128)(2,1)}), bf16[16,16,256]{2,1,0:T(8,128)(2,1)S(1)}, u32[]{:S(2)}, u32[]{:S(2)}) async-start(bf16[16,16,256]{2,1,0:T(8,128)(2,1)} %shard_map.207), calls=%async_computation.2 | async-start | bytes 262144 | tf_op jit(solution)/shard_map/all_to_all | solution.py:52
  73.2 17.2 %all-to-all-start.3 = ((bf16[32,4,1152]{2,1,0:T(4,128)(2,1)}), bf16[32,4,1152]{2,1,0:T(4,128)(2,1)S(1)}, u32[]{:S(2)}, u32[]{:S(2)}) async-start(bf16[32,4,1152]{2,1,0:T(4,128)(2,1)} %shard_map.208), calls=%async_computation.3 | async-start | bytes 589824 | tf_op jit(solution)/shard_map/all_to_all | solution.py:52
  77.6 8.9 %collective-permute-start.3 = (f32[8,1024]{1,0:T(8,128)S(1)}, f32[8,1024]{1,0:T(8,128)S(1)}, u32[]{:S(2)}, u32[]{:S(2)}) collective-permute-start(f32[8,1024]{1,0:T(8,128)S(1)} %select_bitcast_fusion.3), channel_id=1, source_target_pairs={{0,2},{1,3},{2,0},{3,1},{4,6},{5,7},{6,4},{7,5},{8,10},{9,11},{10,... | collective-permute-start | bytes 98312 | tf_op jit(solution)/shard_map/ppermute | solution.py:73
  91.3 16.8 %all-to-all-start.4 = ((bf16[32,4,1152]{2,1,0:T(4,128)(2,1)}), bf16[32,4,1152]{2,1,0:T(4,128)(2,1)S(1)}, u32[]{:S(2)}, u32[]{:S(2)}) async-start(bf16[32,4,1152]{2,1,0:T(4,128)(2,1)} %get-tuple-element.35), calls=%async_computation.4 | async-start | bytes 589824 | tf_op jit(solution)/shard_map/all_to_all | solution.py:52
  109.2 18.9 %all-to-all-start.5 = ((bf16[16,48,128]{2,1,0:T(8,128)(2,1)}), bf16[16,48,128]{2,1,0:T(8,128)(2,1)S(1)}, u32[]{:S(2)}, u32[]{:S(2)}) async-start(bf16[16,48,128]{2,1,0:T(8,128)(2,1)} %shard_map.210), calls=%async_computation.5 | async-start | bytes 393216 | tf_op jit(solution)/shard_map/all_to_all | solution.py:52

commit v4 on v3

--- a/solution.py
+++ b/solution.py
@@ -56,14 +56,12 @@
     return jnp.einsum(spec, left, right, preferred_element_type=jnp.float32)
 
 
-def scatter_sum_by_halves(values, axis, count, before_last):
+def scatter_sum_by_halves(values, axis, count):
     index = lax.axis_index(axis)
     bits = count.bit_length() - 1
     values = values.reshape((2,) * bits + values.shape[1:])
     left = list(range(bits - 1, -1, -1))
     for bit in [0] + list(range(bits - 1, 0, -1)):
-        if len(left) == 1:
-            before_last, values = lax.optimization_barrier((before_last, values))
         at = left.index(bit)
         left.remove(bit)
         low = lax.index_in_dim(values, 0, at, keepdims=False)
@@ -72,7 +70,7 @@
         pairs = [(place, place ^ (1 << bit)) for place in range(count)]
         arrived = lax.ppermute(jnp.where(upper, low, high), axis, pairs)
         values = jnp.where(upper, high, low) + arrived
-    return before_last, values
+    return values
 
 
 def dot_last(left, right):
@@ -372,48 +370,7 @@
     frozen_part = jnp.concatenate(
         [product("rd,dc->rc", flat_inputs, frozen_weights[kind]) for kind in range(kinds)], axis=1
     ).reshape(ranks, own_lines, kinds * columns)
-
-    sent = out((groups, own_rows, wide))
-    masters = call(send_masters, sent, adapter_down_master, by_rank(adapter_up_master))
-    factors = exchange(masters, "grp").reshape(all_rows, wide)
-
-    cotangents = weighted_output_cotangents.reshape(-1, tokens)
-    shares = call(
-        project_tokens, out((tokens, 2 * all_rows)), factors, trainer_token_inputs, cotangents
-    ).reshape(ranks, -1, 2 * all_rows)
-    sums = call(sum_tokens, out(shares.shape), exchange(shares, "tp"))
-    token_sums = exchange(sums, "tp").reshape(tokens, 2 * all_rows)
-
-    gradients = call(
-        functools.partial(send_gradients, own_rank=own_rank),
-        sent,
-        token_sums,
-        trainer_token_inputs,
-        cotangents,
-    )
-    gradients, frozen_sum = scatter_sum_by_halves(frozen_part, "tp", ranks, gradients)
-    own = out(adapter_down_master.shape, jnp.float32)
-    small = out((own_rows, wide - own_width), jnp.float32)
-    *fresh, fresh_factors = call(
-        update_factors,
-        (own, own, own, small, small, small, sent),
-        exchange(gradients, "grp"),
-        adapter_down_master,
-        down_first_moment,
-        down_second_moment,
-        placed(adapter_up_master),
-        placed(up_first_moment),
-        placed(up_second_moment),
-    )
-    fresh_factors, frozen_sum = lax.optimization_barrier((fresh_factors, frozen_sum))
-    factors = exchange(fresh_factors, "grp").reshape(all_rows, wide)
-
-    rank_space = call(
-        functools.partial(send_rank_space, own_lines=own_lines),
-        out((ranks, 2 * own_lines + own_columns, all_rows)),
-        factors,
-        flat_inputs,
-    )
+    frozen_sum = scatter_sum_by_halves(frozen_part, "tp", ranks)
 
     lines = query_width // (head_groups * head_size) * own_lines
     query_lines = (
@@ -439,15 +396,54 @@
         ),
     )(lengths, query_lines, rotated_key_cache, stored_value_cache)
 
+    sent = out((groups, own_rows, wide))
+    masters = call(send_masters, sent, adapter_down_master, by_rank(adapter_up_master))
+    factors = exchange(masters, "grp").reshape(all_rows, wide)
+
+    cotangents = weighted_output_cotangents.reshape(-1, tokens)
+    shares = call(
+        project_tokens, out((tokens, 2 * all_rows)), factors, trainer_token_inputs, cotangents
+    ).reshape(ranks, -1, 2 * all_rows)
+    sums = call(sum_tokens, out(shares.shape), exchange(shares, "tp"))
+    token_sums = exchange(sums, "tp").reshape(tokens, 2 * all_rows)
+
+    gradients = call(
+        functools.partial(send_gradients, own_rank=own_rank),
+        sent,
+        token_sums,
+        trainer_token_inputs,
+        cotangents,
+    )
+    gradients, peak, total, cached = lax.optimization_barrier((gradients, peak, total, cached))
+    own = out(adapter_down_master.shape, jnp.float32)
+    small = out((own_rows, wide - own_width), jnp.float32)
+    *fresh, fresh_factors = call(
+        update_factors,
+        (own, own, own, small, small, small, sent),
+        exchange(gradients, "grp"),
+        adapter_down_master,
+        down_first_moment,
+        down_second_moment,
+        placed(adapter_up_master),
+        placed(up_first_moment),
+        placed(up_second_moment),
+    )
+    factors = exchange(fresh_factors, "grp").reshape(all_rows, wide)
+
+    rank_space = call(
+        functools.partial(send_rank_space, own_lines=own_lines),
+        out((ranks, 2 * own_lines + own_columns, all_rows)),
+        factors,
+        flat_inputs,
+    )
+
     positions = lengths[:, None] + jnp.arange(steps_count, dtype=jnp.int32)[None, :]
     angles = positions.astype(jnp.float32).reshape(-1, 1) * rope_frequencies(head_size)
     cosine, sine = jnp.cos(angles), jnp.sin(angles)
     cosine = jnp.concatenate([cosine, cosine], axis=1)
     sine = jnp.concatenate([-sine, sine], axis=1)
 
-    rank_space, peak, total, cached, cosine, sine = lax.optimization_barrier(
-        (rank_space, peak, total, cached, cosine, sine)
-    )
+    rank_space, frozen_sum = lax.optimization_barrier((rank_space, frozen_sum))
     last = exchange(rank_space, "tp")
     entries = jax.ShapeDtypeStruct((row_count, steps_count, columns), jnp.float32)
     attended, new_keys, new_values = pl.pallas_call(

time: 130 us -> 133 us (1.023)
    all_to_all x6, waiting for transfers between devices: 46.8 us -> 50.6 us  [exchange(): return lax.all_to_all(pieces, axis, 0, 0, tiled=True)]
    ppermute x4, waiting for transfers between devices: 6.42 us -> 3.27 us  [scatter_sum_by_halves(): arrived = lax.ppermute(jnp.where(upper, low, high), axis, pairs)]
    all_to_all x6, starting transfers between devices: 41.5 us -> 43.3 us  [exchange(): return lax.all_to_all(pieces, axis, 0, 0, tiled=True)]
  transfers between devices with their start and end apart: 10 -> 10, of which waited for: 7 -> 7; matrix products, arithmetic and copies ran while one was open for 2% -> 3% of each run, Pallas kernels for 3% -> 3%
where the time goes in v4:
time: 133 us; the launch traced here: 132 us
  starting transfers between devices  61.1 us (46%)
  waiting for transfers between devices  53.8 us (40%)
  Pallas kernels  8.57 us (6%)
  other arithmetic  3.11 us (2%)
  matrix products  3.08 us (2%)
  local copies, waits for them, and re-layouts  1.72 us (1%)
    all_to_all x6, waiting for transfers between devices, exchange(): return lax.all_to_all(pieces, axis, 0, 0, tiled=True)  50.6 us
    all_to_all x6, starting transfers between devices, exchange(): return lax.all_to_all(pieces, axis, 0, 0, tiled=True)  43.3 us
    ppermute x4, starting transfers between devices, scatter_sum_by_halves(): arrived = lax.ppermute(jnp.where(upper, low, high), axis, pairs)  17.8 us
    pallas_call x6, Pallas kernels, call(): pl.pallas_call(kernel, out_shape=outs, in_specs=[pl.BlockSpec(memory_spac...  5.3 us
    ppermute x4, waiting for transfers between devices, scatter_sum_by_halves(): arrived = lax.ppermute(jnp.where(upper, low, high), axis, pairs)  3.27 us
    dot_general x2, matrix products, product(): return jnp.einsum(spec, left, right, preferred_element_type=jnp.float32)  3.08 us
  transfers between devices with their start and end apart: 10, of which 7 were waited for; matrix products, arithmetic and copies ran while one was open for 3% of the time, Pallas kernels for 3%

profile of v4, /device:TPU:1, one launch (start us, length us, event | category | flops | bytes accessed | tf_op | source)
XLA Modules:
  0.0 132.4 jit_solution(6118034825529406007)
XLA Ops:
  0.6 1.0 reshape.104.inputs_ref
  1.7 1.5 %fusion = f32[128,512]{1,0:T(8,128)S(1)} fusion(bf16[128,1024]{1,0:T(8,128)(2,1)S(1)} %reshape.104.inputs_ref, bf16[2,1024,512]{2,1,0:T(8,128)(2,1)} %param.22), kind=kOutput, calls=%fused_computation | convolution fusion | flops 134217728 | bytes 1572864 | tf_op jit(solution)/shard_map/rd,dc->rc/dot_general | solution.py:56
  3.2 0.0 copy-start.7
  3.2 0.0 copy-start.10
  3.3 1.5 %fusion.2 = f32[128,512]{1,0:T(8,128)S(1)} fusion(bf16[128,1024]{1,0:T(8,128)(2,1)S(1)} %reshape.104.inputs_ref, bf16[2,1024,512]{2,1,0:T(8,128)(2,1)} %param.22), kind=kOutput, calls=%fused_computation.2 | convolution fusion | flops 134217728 | bytes 1572864 | tf_op jit(solution)/shard_map/rd,dc->rc/dot_general | solution.py:56
  4.8 0.0 copy-start
  4.9 8.9 %collective-permute-start = (f32[2,2,2,8,1024]{4,3,2,1,0:T(8,128)S(1)}, f32[2,2,2,8,1024]{4,3,2,1,0:T(8,128)S(1)}, u32[]{:S(2)}, u32[]{:S(2)}) collective-permute-start(f32[2,2,2,8,1024]{4,3,2,1,0:T(8,128)S(1)} %select_bitcast_fusion), channel_id=1, source_target_pairs={{0,1},{1,0},{2,3},{3,2},{4,5},{5,4},{6,7},{7,6},{8,9},{9,8},{10,11... | collective-permute-start | bytes 786440 | tf_op jit(solution)/shard_map/ppermute | solution.py:71
  13.9 0.8 shard_map.205
  14.7 7.3 %all-to-all-start = ((bf16[32,4,1152]{2,1,0:T(4,128)(2,1)}), bf16[32,4,1152]{2,1,0:T(4,128)(2,1)S(1)}, u32[]{:S(2)}, u32[]{:S(2)}) async-start(bf16[32,4,1152]{2,1,0:T(4,128)(2,1)} %shard_map.205), calls=%async_computation | async-start | bytes 589824 | tf_op jit(solution)/shard_map/all_to_all | solution.py:52
  22.0 0.1 add_convert_fusion
  22.1 0.1 convert_element_type.19
  22.2 0.1 fusion.6
  22.4 12.8 %all-to-all-done = bf16[32,4,1152]{2,1,0:T(4,128)(2,1)S(1)} async-done(((bf16[32,4,1152]{2,1,0:T(4,128)(2,1)}), bf16[32,4,1152]{2,1,0:T(4,128)(2,1)S(1)}, u32[]{:S(2)}, u32[]{:S(2)}) %all-to-all-start) | async-done | bytes 294944 | tf_op jit(solution)/shard_map/all_to_all | solution.py:52
  35.2 0.1 reshape.97.factors_ref
  35.3 1.0 shard_map.206
  36.3 12.0 %all-to-all-start.1 = ((bf16[16,16,256]{2,1,0:T(8,128)(2,1)}), bf16[16,16,256]{2,1,0:T(8,128)(2,1)S(1)}, u32[]{:S(2)}, u32[]{:S(2)}) async-start(bf16[16,16,256]{2,1,0:T(8,128)(2,1)} %bitcast.2), calls=%async_computation.1 | async-start | bytes 262144 | tf_op jit(solution)/shard_map/all_to_all | solution.py:52
  48.3 0.7 select_bitcast_fusion.1
  49.0 4.8 %collective-permute-start.1 = (f32[2,2,8,1024]{3,2,1,0:T(8,128)}, f32[2,2,8,1024]{3,2,1,0:T(8,128)S(1)}, u32[]{:S(2)}, u32[]{:S(2)}) collective-permute-start(f32[2,2,8,1024]{3,2,1,0:T(8,128)} %select_bitcast_fusion.1), channel_id=1, source_target_pairs={{0,8},{1,9},{2,10},{3,11},{4,12},{5,13},{6,14},{7,15},{8,0},{9,1},... | collective-permute-start | bytes 393224 | tf_op jit(solution)/shard_map/ppermute | solution.py:71
  53.7 0.1 select_maximum_fusion.2.up_ref
  53.8 0.2 reshape.101
  54.0 0.1 copy.24
  54.1 0.1 select_maximum_fusion.up_second_ref
  54.2 4.2 %all-to-all-done.1.parts_ref = bf16[16,16,256]{2,1,0:T(8,128)(2,1)S(1)} async-done(((bf16[16,16,256]{2,1,0:T(8,128)(2,1)}), bf16[16,16,256]{2,1,0:T(8,128)(2,1)S(1)}, u32[]{:S(2)}, u32[]{:S(2)}) %all-to-all-start.1) | async-done | bytes 131104 | tf_op jit(solution)/shard_map/all_to_all | solution.py:52
  58.4 0.7 shard_map.207
  59.1 4.1 %all-to-all-start.2 = ((bf16[16,16,256]{2,1,0:T(8,128)(2,1)}), bf16[16,16,256]{2,1,0:T(8,128)(2,1)S(1)}, u32[]{:S(2)}, u32[]{:S(2)}) async-start(bf16[16,16,256]{2,1,0:T(8,128)(2,1)} %shard_map.207), calls=%async_computation.2 | async-start | bytes 262144 | tf_op jit(solution)/shard_map/all_to_all | solution.py:52
  63.2 1.7 %shard_map.209 = (f32[4,128,1]{2,1,0:T(8,128)S(1)}, f32[4,128,1]{2,1,0:T(8,128)S(1)}, f32[4,128,128]{2,1,0:T(8,128)S(1)}) custom-call(s32[2]{0:T(128)S(1)} %copy-done.8, bf16[4,128,128]{2,1,0:T(8,128)(2,1)S(1)} %bitcast.76, bf16[2,4,256,128]{3,2,1,0:T(8,128)(2,1)S(1)} %copy-done.1, bf16[2,4,256,128]{3,2,1,0:T(8,128)(2,1)S(1)} %copy-done.2), custom_call_target="tpu_custom_call" | custom-call | flops 134217728 | bytes 1048576 | tf_op jit(solution)/shard_map/pallas_call | solution.py:382
  64.9 8.3 %all-to-all-done.2 = bf16[16,16,256]{2,1,0:T(8,128)(2,1)S(1)} async-done(((bf16[16,16,256]{2,1,0:T(8,128)(2,1)}), bf16[16,16,256]{2,1,0:T(8,128)(2,1)S(1)}, u32[]{:S(2)}, u32[]{:S(2)}) %all-to-all-start.2) | async-done | bytes 131104 | tf_op jit(solution)/shard_map/all_to_all | solution.py:52
  73.3 1.0 shard_map.208
  74.3 4.3 %all-to-all-start.3 = ((bf16[32,4,1152]{2,1,0:T(4,128)(2,1)}), bf16[32,4,1152]{2,1,0:T(4,128)(2,1)S(1)}, u32[]{:S(2)}, u32[]{:S(2)}) async-start(bf16[32,4,1152]{2,1,0:T(4,128)(2,1)} %shard_map.208), calls=%async_computation.3 | async-start | bytes 589824 | tf_op jit(solution)/shard_map/all_to_all | solution.py:52
  78.6 2.0 %collective-permute-start.2 = (f32[2,8,1024]{2,1,0:T(8,128)S(1)}, f32[2,8,1024]{2,1,0:T(8,128)S(1)}, u32[]{:S(2)}, u32[]{:S(2)}) collective-permute-start(f32[2,8,1024]{2,1,0:T(8,128)S(1)} %select_bitcast_fusion.2), channel_id=1, source_target_pairs={{0,4},{1,5},{2,6},{3,7},{4,0},{5,1},{6,2},{7,3},{8,12},{9,13},{10,... | collective-permute-start | bytes 196616 | tf_op jit(solution)/shard_map/ppermute | solution.py:71
  80.6 0.1 select_maximum_fusion.1.up_first_ref
  80.7 3.3 %collective-permute-done.2 = f32[2,8,1024]{2,1,0:T(8,128)S(1)} collective-permute-done((f32[2,8,1024]{2,1,0:T(8,128)S(1)}, f32[2,8,1024]{2,1,0:T(8,128)S(1)}, u32[]{:S(2)}, u32[]{:S(2)}) %collective-permute-start.2) | collective-permute-done | bytes 65568 | tf_op jit(solution)/shard_map/ppermute | solution.py:71
  84.0 2.1 %collective-permute-start.3 = (f32[8,1024]{1,0:T(8,128)S(1)}, f32[8,1024]{1,0:T(8,128)S(1)}, u32[]{:S(2)}, u32[]{:S(2)}) collective-permute-start(f32[8,1024]{1,0:T(8,128)S(1)} %select_bitcast_fusion.3), channel_id=1, source_target_pairs={{0,2},{1,3},{2,0},{3,1},{4,6},{5,7},{6,4},{7,5},{8,10},{9,11},{10,... | collective-permute-start | bytes 98312 | tf_op jit(solution)/shard_map/ppermute | solution.py:71
  86.1 5.3 %all-to-all-done.3.parts_ref = bf16[32,4,1152]{2,1,0:T(4,128)(2,1)S(1)} async-done(((bf16[32,4,1152]{2,1,0:T(4,128)(2,1)}), bf16[32,4,1152]{2,1,0:T(4,128)(2,1)S(1)}, u32[]{:S(2)}, u32[]{:S(2)}) %all-to-all-start.3) | async-done | bytes 294944 | tf_op jit(solution)/shard_map/all_to_all | solution.py:52
  91.4 0.9 shard_map.210
  92.4 4.4 %all-to-all-start.4 = ((bf16[32,4,1152]{2,1,0:T(4,128)(2,1)}), bf16[32,4,1152]{2,1,0:T(4,128)(2,1)S(1)}, u32[]{:S(2)}, u32[]{:S(2)}) async-start(bf16[32,4,1152]{2,1,0:T(4,128)(2,1)} %get-tuple-element.32), calls=%async_computation.4 | async-start | bytes 589824 | tf_op jit(solution)/shard_map/all_to_all | solution.py:52
  96.8 0.1 pad_maximum_fusion.1
  96.9 0.1 slice_bitcast_fusion.9
  97.0 0.6 maximum_bitcast_fusion.2
  97.6 10.5 %all-to-all-done.4 = bf16[32,4,1152]{2,1,0:T(4,128)(2,1)S(1)} async-done(((bf16[32,4,1152]{2,1,0:T(4,128)(2,1)}), bf16[32,4,1152]{2,1,0:T(4,128)(2,1)S(1)}, u32[]{:S(2)}, u32[]{:S(2)}) %all-to-all-start.4) | async-done | bytes 294944 | tf_op jit(solution)/shard_map/all_to_all | solution.py:52
  108.1 0.1 reshape.103.factors_ref
  108.2 0.9 shard_map.211
  109.1 11.2 %all-to-all-start.5 = ((bf16[16,48,128]{2,1,0:T(8,128)(2,1)}), bf16[16,48,128]{2,1,0:T(8,128)(2,1)S(1)}, u32[]{:S(2)}, u32[]{:S(2)}) async-start(bf16[16,48,128]{2,1,0:T(8,128)(2,1)} %shard_map.211), calls=%async_computation.5 | async-start | bytes 393216 | tf_op jit(solution)/shard_map/all_to_all | solution.py:52
  120.3 0.6 maximum_bitcast_fusion.1
  120.8 0.1 slice_bitcast_fusion.13
  120.9 0.6 maximum_bitcast_fusion
  121.5 9.4 %all-to-all-done.5.last_ref = bf16[16,48,128]{2,1,0:T(8,128)(2,1)S(1)} async-done(((bf16[16,48,128]{2,1,0:T(8,128)(2,1)}), bf16[16,48,128]{2,1,0:T(8,128)(2,1)S(1)}, u32[]{:S(2)}, u32[]{:S(2)}) %all-to-all-start.5) | async-done | bytes 196640 | tf_op jit(solution)/shard_map/all_to_all | solution.py:52
  130.8 1.5 %shard_map.212 = (f32[2,4,8192]{2,1,0:T(4,128)}, f32[2,4,512]{2,1,0:T(4,128)}, f32[2,4,512]{2,1,0:T(4,128)}) custom-call(bf16[16,48,128]{2,1,0:T(8,128)(2,1)S(1)} %all-to-all-done.5.last_ref, f32[8,1024]{1,0:T(8,128)S(1)} %bitcast_add_fusion.3.frozen_ref, f32[8,128]{1,0:T(8,128)S(1)} %get-tuple-element.64.cosine_ref, ...), custom_call_target="tpu_custom_call" | custom-call | flops 2097152 | bytes 262144 | tf_op jit(solution)/shard_map/pallas_call | solution.py:449
  (36 shorter events, 0.3 us)
Async XLA Ops:
  3.2 10.7 %copy-start.4 = (f32[2,2,1024]{2,1,0:T(2,128)S(1)}, f32[2,2,1024]{2,1,0:T(2,128)}, u32[]{:S(2)}) copy-start(f32[2,2,1024]{2,1,0:T(2,128)} %down_ref.3) | copy-start | bytes 49156
  3.2 10.7 %copy-start.7 = (f32[2,32,2]{1,2,0:T(2,128)S(1)}, f32[2,32,2]{1,2,0:T(2,128)}, u32[]{:S(2)}) copy-start(f32[2,32,2]{1,2,0:T(2,128)} %param.17) | copy-start | bytes 1540
  3.2 18.7 %copy-start.10 = (f32[2,32,2]{1,2,0:T(2,128)S(1)}, f32[2,32,2]{1,2,0:T(2,128)}, u32[]{:S(2)}) copy-start(f32[2,32,2]{1,2,0:T(2,128)} %param.21) | copy-start | bytes 1540
  3.2 18.8 %copy-start.11 = (f32[2,32,2]{1,2,0:T(2,128)S(1)}, f32[2,32,2]{1,2,0:T(2,128)}, u32[]{:S(2)}) copy-start(f32[2,32,2]{1,2,0:T(2,128)} %param.20) | copy-start | bytes 1540
  3.2 18.8 %copy-start.8 = (s32[2]{0:T(128)S(1)}, s32[2]{0:T(128)}, u32[]{:S(2)}) copy-start(s32[2]{0:T(128)} %lengths_ref.1) | copy-start | bytes 28
  4.8 30.5 %copy-start = (bf16[256,1024]{1,0:T(8,128)(2,1)S(1)}, bf16[256,1024]{1,0:T(8,128)(2,1)}, u32[]{:S(2)}) copy-start(bf16[256,1024]{1,0:T(8,128)(2,1)} %inputs_ref.3) | copy-start | bytes 1572868
  4.8 30.5 %copy-start.3 = (bf16[2,32,256]{2,1,0:T(8,128)(2,1)S(1)}, bf16[2,32,256]{2,1,0:T(8,128)(2,1)}, u32[]{:S(2)}) copy-start(bf16[2,32,256]{2,1,0:T(8,128)(2,1)} %param.15) | copy-start | bytes 98308
  4.9 17.4 %collective-permute-start = (f32[2,2,2,8,1024]{4,3,2,1,0:T(8,128)S(1)}, f32[2,2,2,8,1024]{4,3,2,1,0:T(8,128)S(1)}, u32[]{:S(2)}, u32[]{:S(2)}) collective-permute-start(f32[2,2,2,8,1024]{4,3,2,1,0:T(8,128)S(1)} %select_bitcast_fusion), channel_id=1, source_target_pairs={{0,1},{1,0},{2,3},{3,2},{4,5},{5,4},{6,7},{7,6},{8,9},{9,8},{10,11... | collective-permute-start | bytes 786440 | tf_op jit(solution)/shard_map/ppermute | solution.py:71
  13.9 40.0 %copy-start.9 = (bf16[2,4,8192]{2,1,0:T(4,128)(2,1)S(1)}, bf16[2,4,8192]{2,1,0:T(4,128)(2,1)}, u32[]{:S(2)}) copy-start(bf16[2,4,8192]{2,1,0:T(4,128)(2,1)} %param.24) | copy-start | bytes 393220
  14.7 20.5 %all-to-all-start = ((bf16[32,4,1152]{2,1,0:T(4,128)(2,1)}), bf16[32,4,1152]{2,1,0:T(4,128)(2,1)S(1)}, u32[]{:S(2)}, u32[]{:S(2)}) async-start(bf16[32,4,1152]{2,1,0:T(4,128)(2,1)} %shard_map.205), calls=%async_computation | async-start | bytes 589824 | tf_op jit(solution)/shard_map/all_to_all | solution.py:52
  22.3 40.8 %copy-start.1 = (bf16[2,4,256,128]{3,2,1,0:T(8,128)(2,1)S(1)}, bf16[2,4,256,128]{3,2,1,0:T(8,128)(2,1)}, u32[]{:S(2)}) copy-start(bf16[2,4,256,128]{3,2,1,0:T(8,128)(2,1)} %key_ref.1) | copy-start | bytes 1572868
  22.3 40.8 %copy-start.2 = (bf16[2,4,256,128]{3,2,1,0:T(8,128)(2,1)S(1)}, bf16[2,4,256,128]{3,2,1,0:T(8,128)(2,1)}, u32[]{:S(2)}) copy-start(bf16[2,4,256,128]{3,2,1,0:T(8,128)(2,1)} %value_ref.1) | copy-start | bytes 1572868
  36.3 22.1 %all-to-all-start.1 = ((bf16[16,16,256]{2,1,0:T(8,128)(2,1)}), bf16[16,16,256]{2,1,0:T(8,128)(2,1)S(1)}, u32[]{:S(2)}, u32[]{:S(2)}) async-start(bf16[16,16,256]{2,1,0:T(8,128)(2,1)} %bitcast.2), calls=%async_computation.1 | async-start | bytes 262144 | tf_op jit(solution)/shard_map/all_to_all | solution.py:52
  49.0 16.0 %collective-permute-start.1 = (f32[2,2,8,1024]{3,2,1,0:T(8,128)}, f32[2,2,8,1024]{3,2,1,0:T(8,128)S(1)}, u32[]{:S(2)}, u32[]{:S(2)}) collective-permute-start(f32[2,2,8,1024]{3,2,1,0:T(8,128)} %select_bitcast_fusion.1), channel_id=1, source_target_pairs={{0,8},{1,9},{2,10},{3,11},{4,12},{5,13},{6,14},{7,15},{8,0},{9,1},... | collective-permute-start | bytes 393224 | tf_op jit(solution)/shard_map/ppermute | solution.py:71
  59.1 32.4 %copy-start.5 = (f32[2,2,1024]{2,1,0:T(2,128)S(1)}, f32[2,2,1024]{2,1,0:T(2,128)}, u32[]{:S(2)}) copy-start(f32[2,2,1024]{2,1,0:T(2,128)} %down_first_ref.1) | copy-start | bytes 49156
  59.1 32.4 %copy-start.6 = (f32[2,2,1024]{2,1,0:T(2,128)S(1)}, f32[2,2,1024]{2,1,0:T(2,128)}, u32[]{:S(2)}) copy-start(f32[2,2,1024]{2,1,0:T(2,128)} %down_second_ref.1) | copy-start | bytes 49156
  59.1 14.2 %all-to-all-start.2 = ((bf16[16,16,256]{2,1,0:T(8,128)(2,1)}), bf16[16,16,256]{2,1,0:T(8,128)(2,1)S(1)}, u32[]{:S(2)}, u32[]{:S(2)}) async-start(bf16[16,16,256]{2,1,0:T(8,128)(2,1)} %shard_map.207), calls=%async_computation.2 | async-start | bytes 262144 | tf_op jit(solution)/shard_map/all_to_all | solution.py:52
  74.3 17.1 %all-to-all-start.3 = ((bf16[32,4,1152]{2,1,0:T(4,128)(2,1)}), bf16[32,4,1152]{2,1,0:T(4,128)(2,1)S(1)}, u32[]{:S(2)}, u32[]{:S(2)}) async-start(bf16[32,4,1152]{2,1,0:T(4,128)(2,1)} %shard_map.208), calls=%async_computation.3 | async-start | bytes 589824 | tf_op jit(solution)/shard_map/all_to_all | solution.py:52
  78.6 5.3 %collective-permute-start.2 = (f32[2,8,1024]{2,1,0:T(8,128)S(1)}, f32[2,8,1024]{2,1,0:T(8,128)S(1)}, u32[]{:S(2)}, u32[]{:S(2)}) collective-permute-start(f32[2,8,1024]{2,1,0:T(8,128)S(1)} %select_bitcast_fusion.2), channel_id=1, source_target_pairs={{0,4},{1,5},{2,6},{3,7},{4,0},{5,1},{6,2},{7,3},{8,12},{9,13},{10,... | collective-permute-start | bytes 196616 | tf_op jit(solution)/shard_map/ppermute | solution.py:71
  84.0 12.9 %collective-permute-start.3 = (f32[8,1024]{1,0:T(8,128)S(1)}, f32[8,1024]{1,0:T(8,128)S(1)}, u32[]{:S(2)}, u32[]{:S(2)}) collective-permute-start(f32[8,1024]{1,0:T(8,128)S(1)} %select_bitcast_fusion.3), channel_id=1, source_target_pairs={{0,2},{1,3},{2,0},{3,1},{4,6},{5,7},{6,4},{7,5},{8,10},{9,11},{10,... | collective-permute-start | bytes 98312 | tf_op jit(solution)/shard_map/ppermute | solution.py:71
  92.4 15.7 %all-to-all-start.4 = ((bf16[32,4,1152]{2,1,0:T(4,128)(2,1)}), bf16[32,4,1152]{2,1,0:T(4,128)(2,1)S(1)}, u32[]{:S(2)}, u32[]{:S(2)}) async-start(bf16[32,4,1152]{2,1,0:T(4,128)(2,1)} %get-tuple-element.32), calls=%async_computation.4 | async-start | bytes 589824 | tf_op jit(solution)/shard_map/all_to_all | solution.py:52
  109.1 21.8 %all-to-all-start.5 = ((bf16[16,48,128]{2,1,0:T(8,128)(2,1)}), bf16[16,48,128]{2,1,0:T(8,128)(2,1)S(1)}, u32[]{:S(2)}, u32[]{:S(2)}) async-start(bf16[16,48,128]{2,1,0:T(8,128)(2,1)} %shard_map.211), calls=%async_computation.5 | async-start | bytes 393216 | tf_op jit(solution)/shard_map/all_to_all | solution.py:52

commit v5 on v4

--- a/solution.py
+++ b/solution.py
@@ -56,21 +56,22 @@
     return jnp.einsum(spec, left, right, preferred_element_type=jnp.float32)
 
 
-def scatter_sum_by_halves(values, axis, count):
-    index = lax.axis_index(axis)
-    bits = count.bit_length() - 1
-    values = values.reshape((2,) * bits + values.shape[1:])
-    left = list(range(bits - 1, -1, -1))
-    for bit in [0] + list(range(bits - 1, 0, -1)):
-        at = left.index(bit)
-        left.remove(bit)
-        low = lax.index_in_dim(values, 0, at, keepdims=False)
-        high = lax.index_in_dim(values, 1, at, keepdims=False)
-        upper = (index >> bit) & 1 == 1
-        pairs = [(place, place ^ (1 << bit)) for place in range(count)]
-        arrived = lax.ppermute(jnp.where(upper, low, high), axis, pairs)
-        values = jnp.where(upper, high, low) + arrived
-    return values
+def after(values, earlier):
+    return lax.optimization_barrier((values, earlier))[0]
+
+
+def half_sum(values, axis, count, at, bit, earlier_sum=None, earlier_send=None):
+    if earlier_send is not None:
+        values = after(values, earlier_send)
+    low = lax.index_in_dim(values, 0, at, keepdims=False)
+    high = lax.index_in_dim(values, 1, at, keepdims=False)
+    upper = (lax.axis_index(axis) >> bit) & 1 == 1
+    pairs = [(place, place ^ (1 << bit)) for place in range(count)]
+    arrived = lax.ppermute(jnp.where(upper, low, high), axis, pairs)
+    kept = jnp.where(upper, high, low)
+    if earlier_sum is not None:
+        kept = after(kept, earlier_sum)
+    return kept + arrived
 
 
 def dot_last(left, right):
@@ -367,10 +368,6 @@
         return jax.ShapeDtypeStruct(shape, kind)
 
     flat_inputs = decode_step_inputs.reshape(-1, own_width)
-    frozen_part = jnp.concatenate(
-        [product("rd,dc->rc", flat_inputs, frozen_weights[kind]) for kind in range(kinds)], axis=1
-    ).reshape(ranks, own_lines, kinds * columns)
-    frozen_sum = scatter_sum_by_halves(frozen_part, "tp", ranks)
 
     lines = query_width // (head_groups * head_size) * own_lines
     query_lines = (
@@ -398,7 +395,16 @@
 
     sent = out((groups, own_rows, wide))
     masters = call(send_masters, sent, adapter_down_master, by_rank(adapter_up_master))
+    later_inputs = after(flat_inputs, masters)
+    frozen_part = jnp.concatenate(
+        [product("rd,dc->rc", later_inputs, frozen_weights[kind]) for kind in range(kinds)], axis=1
+    ).reshape(ranks, own_lines, kinds * columns)
+    bits = ranks.bit_length() - 1
+    frozen_part = frozen_part.reshape((2,) * bits + (own_lines, kinds * columns))
     factors = exchange(masters, "grp").reshape(all_rows, wide)
+
+    frozen_part = half_sum(frozen_part, "tp", ranks, bits - 1, 0, earlier_sum=factors)
+    frozen_part = half_sum(frozen_part, "tp", ranks, 0, bits - 1)
 
     cotangents = weighted_output_cotangents.reshape(-1, tokens)
     shares = call(
@@ -414,6 +420,7 @@
         trainer_token_inputs,
         cotangents,
     )
+    frozen_part = half_sum(frozen_part, "tp", ranks, 0, 2, earlier_send=gradients)
     gradients, peak, total, cached = lax.optimization_barrier((gradients, peak, total, cached))
     own = out(adapter_down_master.shape, jnp.float32)
     small = out((own_rows, wide - own_width), jnp.float32)
@@ -428,6 +435,7 @@
         placed(up_first_moment),
         placed(up_second_moment),
     )
+    frozen_sum = half_sum(frozen_part, "tp", ranks, 0, 1, earlier_send=fresh_factors)
     factors = exchange(fresh_factors, "grp").reshape(all_rows, wide)
 
     rank_space = call(

time: 133 us -> 124 us (0.932)
  waiting for transfers between devices: 53.8 us -> 45.6 us
  starting transfers between devices: 61.1 us -> 58.9 us
  local copies, waits for them, and re-layouts: 1.72 us -> 3.11 us
    all_to_all x6, waiting for transfers between devices: 50.6 us -> 37.2 us  [exchange(): return lax.all_to_all(pieces, axis, 0, 0, tiled=True)]
    ppermute x4, waiting for transfers between devices: 3.27 us -> 8.38 us  [half_sum(): arrived = lax.ppermute(jnp.where(upper, low, high), axis, pairs)]
    ppermute x4, starting transfers between devices: 17.8 us -> 13.2 us  [half_sum(): arrived = lax.ppermute(jnp.where(upper, low, high), axis, pairs)]
    all_to_all x6, starting transfers between devices: 43.3 us -> 45.7 us  [exchange(): return lax.all_to_all(pieces, axis, 0, 0, tiled=True)]
    unnamed x24 -> x28, local copies, waits for them, and re-layouts: 0.07 us -> 1.46 us
  transfers between devices with their start and end apart: 10 -> 10, of which waited for: 7 -> 8; matrix products, arithmetic and copies ran while one was open for 3% -> 6% of each run, Pallas kernels for 3% -> 3%
where the time goes in v5:
time: 124 us; the launch traced here: 123 us
  starting transfers between devices  58.9 us (48%)
  waiting for transfers between devices  45.6 us (37%)
  Pallas kernels  8.54 us (7%)
  matrix products  3.12 us (3%)
  local copies, waits for them, and re-layouts  3.11 us (3%)
  other arithmetic  2.45 us (2%)
    all_to_all x6, starting transfers between devices, exchange(): return lax.all_to_all(pieces, axis, 0, 0, tiled=True)  45.7 us
    all_to_all x6, waiting for transfers between devices, exchange(): return lax.all_to_all(pieces, axis, 0, 0, tiled=True)  37.2 us
    ppermute x4, starting transfers between devices, half_sum(): arrived = lax.ppermute(jnp.where(upper, low, high), axis, pairs)  13.2 us
    ppermute x4, waiting for transfers between devices, half_sum(): arrived = lax.ppermute(jnp.where(upper, low, high), axis, pairs)  8.38 us
    pallas_call x6, Pallas kernels, call(): pl.pallas_call(kernel, out_shape=outs, in_specs=[pl.BlockSpec(memory_spac...  5.3 us
    dot_general x2, matrix products, product(): return jnp.einsum(spec, left, right, preferred_element_type=jnp.float32)  3.12 us
  transfers between devices with their start and end apart: 10, of which 8 were waited for; matrix products, arithmetic and copies ran while one was open for 6% of the time, Pallas kernels for 3%

profile of v5, /device:TPU:1, one launch (start us, length us, event | category | flops | bytes accessed | tf_op | source)
XLA Modules:
  0.0 122.7 jit_solution(3345289847965737866)
XLA Ops:
  0.6 0.0 copy-start.4
  0.7 0.7 copy-done.4
  1.4 0.7 copy-done.8
  2.0 0.8 shard_map.205
  2.8 13.5 %all-to-all-start = ((bf16[32,4,1152]{2,1,0:T(4,128)(2,1)}), bf16[32,4,1152]{2,1,0:T(4,128)(2,1)S(1)}, u32[]{:S(2)}, u32[]{:S(2)}) async-start(bf16[32,4,1152]{2,1,0:T(4,128)(2,1)} %shard_map.205), calls=%async_computation | async-start | bytes 589824 | tf_op jit(solution)/shard_map/all_to_all | solution.py:52
  16.3 1.0 reshape.104.inputs_ref
  17.3 1.5 %fusion = f32[128,512]{1,0:T(8,128)S(1)} fusion(bf16[128,1024]{1,0:T(8,128)(2,1)S(1)} %reshape.104.inputs_ref, bf16[2,1024,512]{2,1,0:T(8,128)(2,1)} %param.22), kind=kOutput, calls=%fused_computation | convolution fusion | flops 134217728 | bytes 1572864 | tf_op jit(solution)/shard_map/rd,dc->rc/dot_general | solution.py:56
  18.9 1.6 %fusion.2 = f32[128,512]{1,0:T(8,128)S(1)} fusion(bf16[128,1024]{1,0:T(8,128)(2,1)S(1)} %reshape.104.inputs_ref, bf16[2,1024,512]{2,1,0:T(8,128)(2,1)} %param.22), kind=kOutput, calls=%fused_computation.2 | convolution fusion | flops 134217728 | bytes 1572864 | tf_op jit(solution)/shard_map/rd,dc->rc/dot_general | solution.py:56
  20.7 3.0 %collective-permute-start = (f32[2,2,2,8,1024]{4,3,2,1,0:T(8,128)S(1)}, f32[2,2,2,8,1024]{4,3,2,1,0:T(8,128)S(1)}, u32[]{:S(2)}, u32[]{:S(2)}) collective-permute-start(f32[2,2,2,8,1024]{4,3,2,1,0:T(8,128)S(1)} %get-tuple-element.55), channel_id=1, source_target_pairs={{0,1},{1,0},{2,3},{3,2},{4,5},{5,4},{6,7},{7,6},{8,9},{9,8},{10,11... | collective-permute-start | bytes 786440 | tf_op jit(solution)/shard_map/ppermute | solution.py:70
  23.7 0.1 add_convert_fusion
  23.8 0.1 select_maximum_fusion.2.up_ref
  23.9 4.8 %all-to-all-done = bf16[32,4,1152]{2,1,0:T(4,128)(2,1)S(1)} async-done(((bf16[32,4,1152]{2,1,0:T(4,128)(2,1)}), bf16[32,4,1152]{2,1,0:T(4,128)(2,1)S(1)}, u32[]{:S(2)}, u32[]{:S(2)}) %all-to-all-start) | async-done | bytes 294944 | tf_op jit(solution)/shard_map/all_to_all | solution.py:52
  28.7 0.1 reshape.97.factors_ref
  28.8 1.0 shard_map.206
  29.8 12.5 %all-to-all-start.1 = ((bf16[16,16,256]{2,1,0:T(8,128)(2,1)}), bf16[16,16,256]{2,1,0:T(8,128)(2,1)S(1)}, u32[]{:S(2)}, u32[]{:S(2)}) async-start(bf16[16,16,256]{2,1,0:T(8,128)(2,1)} %bitcast.2), calls=%async_computation.1 | async-start | bytes 262144 | tf_op jit(solution)/shard_map/all_to_all | solution.py:52
  42.3 0.1 convert_element_type.19
  42.4 0.1 fusion.6
  42.6 9.8 %all-to-all-done.1.parts_ref = bf16[16,16,256]{2,1,0:T(8,128)(2,1)S(1)} async-done(((bf16[16,16,256]{2,1,0:T(8,128)(2,1)}), bf16[16,16,256]{2,1,0:T(8,128)(2,1)S(1)}, u32[]{:S(2)}, u32[]{:S(2)}) %all-to-all-start.1) | async-done | bytes 131104 | tf_op jit(solution)/shard_map/all_to_all | solution.py:52
  52.4 0.7 shard_map.207
  53.0 4.0 %all-to-all-start.2 = ((bf16[16,16,256]{2,1,0:T(8,128)(2,1)}), bf16[16,16,256]{2,1,0:T(8,128)(2,1)S(1)}, u32[]{:S(2)}, u32[]{:S(2)}) async-start(bf16[16,16,256]{2,1,0:T(8,128)(2,1)} %shard_map.207), calls=%async_computation.2 | async-start | bytes 262144 | tf_op jit(solution)/shard_map/all_to_all | solution.py:52
  57.0 4.8 %collective-permute-start.1 = (f32[2,2,8,1024]{3,2,1,0:T(8,128)S(1)}, f32[2,2,8,1024]{3,2,1,0:T(8,128)S(1)}, u32[]{:S(2)}, u32[]{:S(2)}) collective-permute-start(f32[2,2,8,1024]{3,2,1,0:T(8,128)S(1)} %select_bitcast_fusion.2), channel_id=1, source_target_pairs={{0,8},{1,9},{2,10},{3,11},{4,12},{5,13},{6,14},{7,15},{8,0},{9,1},... | collective-permute-start | bytes 393224 | tf_op jit(solution)/shard_map/ppermute | solution.py:70
  61.9 0.1 select_maximum_fusion.up_second_ref
  62.0 0.2 reshape.101
  62.1 0.1 copy.24
  62.3 1.7 %shard_map.209 = (f32[4,128,1]{2,1,0:T(8,128)S(1)}, f32[4,128,1]{2,1,0:T(8,128)S(1)}, f32[4,128,128]{2,1,0:T(8,128)S(1)}) custom-call(s32[2]{0:T(128)S(1)} %copy-done.10, bf16[4,128,128]{2,1,0:T(8,128)(2,1)S(1)} %bitcast.76, bf16[2,4,256,128]{3,2,1,0:T(8,128)(2,1)S(1)} %copy-done.1, bf16[2,4,256,128]{3,2,1,0:T(8,128)(2,1)S(1)} %copy-done.2), custom_call_target="tpu_custom_call" | custom-call | flops 134217728 | bytes 1048576 | tf_op jit(solution)/shard_map/pallas_call | solution.py:379
  64.0 0.1 pad_maximum_fusion.1
  64.1 3.1 %all-to-all-done.2 = bf16[16,16,256]{2,1,0:T(8,128)(2,1)S(1)} async-done(((bf16[16,16,256]{2,1,0:T(8,128)(2,1)}), bf16[16,16,256]{2,1,0:T(8,128)(2,1)S(1)}, u32[]{:S(2)}, u32[]{:S(2)}) %all-to-all-start.2) | async-done | bytes 131104 | tf_op jit(solution)/shard_map/all_to_all | solution.py:52
  67.1 1.0 shard_map.208
  68.1 4.7 %all-to-all-start.3 = ((bf16[32,4,1152]{2,1,0:T(4,128)(2,1)}), bf16[32,4,1152]{2,1,0:T(4,128)(2,1)S(1)}, u32[]{:S(2)}, u32[]{:S(2)}) async-start(bf16[32,4,1152]{2,1,0:T(4,128)(2,1)} %shard_map.208), calls=%async_computation.3 | async-start | bytes 589824 | tf_op jit(solution)/shard_map/all_to_all | solution.py:52
  72.9 2.0 %collective-permute-start.2 = (f32[2,8,1024]{2,1,0:T(8,128)S(1)}, f32[2,8,1024]{2,1,0:T(8,128)S(1)}, u32[]{:S(2)}, u32[]{:S(2)}) collective-permute-start(f32[2,8,1024]{2,1,0:T(8,128)S(1)} %select_bitcast_fusion.3), channel_id=1, source_target_pairs={{0,4},{1,5},{2,6},{3,7},{4,0},{5,1},{6,2},{7,3},{8,12},{9,13},{10,... | collective-permute-start | bytes 196616 | tf_op jit(solution)/shard_map/ppermute | solution.py:70
  74.8 0.1 select_maximum_fusion.1.up_first_ref
  74.9 3.3 %collective-permute-done.2 = f32[2,8,1024]{2,1,0:T(8,128)S(1)} collective-permute-done((f32[2,8,1024]{2,1,0:T(8,128)S(1)}, f32[2,8,1024]{2,1,0:T(8,128)S(1)}, u32[]{:S(2)}, u32[]{:S(2)}) %collective-permute-start.2) | collective-permute-done | bytes 65568 | tf_op jit(solution)/shard_map/ppermute | solution.py:70
  78.2 7.4 %all-to-all-done.3.parts_ref = bf16[32,4,1152]{2,1,0:T(4,128)(2,1)S(1)} async-done(((bf16[32,4,1152]{2,1,0:T(4,128)(2,1)}), bf16[32,4,1152]{2,1,0:T(4,128)(2,1)S(1)}, u32[]{:S(2)}, u32[]{:S(2)}) %all-to-all-start.3) | async-done | bytes 294944 | tf_op jit(solution)/shard_map/all_to_all | solution.py:52
  85.6 0.9 shard_map.210
  86.6 4.4 %all-to-all-start.4 = ((bf16[32,4,1152]{2,1,0:T(4,128)(2,1)}), bf16[32,4,1152]{2,1,0:T(4,128)(2,1)S(1)}, u32[]{:S(2)}, u32[]{:S(2)}) async-start(bf16[32,4,1152]{2,1,0:T(4,128)(2,1)} %get-tuple-element.36), calls=%async_computation.4 | async-start | bytes 589824 | tf_op jit(solution)/shard_map/all_to_all | solution.py:52
  91.0 3.4 %collective-permute-start.3 = (f32[8,1024]{1,0:T(8,128)S(1)}, f32[8,1024]{1,0:T(8,128)S(1)}, u32[]{:S(2)}, u32[]{:S(2)}) collective-permute-start(f32[8,1024]{1,0:T(8,128)S(1)} %select_bitcast_fusion.4), channel_id=1, source_target_pairs={{0,2},{1,3},{2,0},{3,1},{4,6},{5,7},{6,4},{7,5},{8,10},{9,11},{10,... | collective-permute-start | bytes 98312 | tf_op jit(solution)/shard_map/ppermute | solution.py:70
  94.4 0.1 slice_bitcast_fusion.9
  94.5 0.6 maximum_bitcast_fusion.2
  95.1 5.1 %collective-permute-done.3 = f32[8,1024]{1,0:T(8,128)S(1)} collective-permute-done((f32[8,1024]{1,0:T(8,128)S(1)}, f32[8,1024]{1,0:T(8,128)S(1)}, u32[]{:S(2)}, u32[]{:S(2)}) %collective-permute-start.3) | collective-permute-done | bytes 32800 | tf_op jit(solution)/shard_map/ppermute | solution.py:70
  100.2 2.7 %all-to-all-done.4 = bf16[32,4,1152]{2,1,0:T(4,128)(2,1)S(1)} async-done(((bf16[32,4,1152]{2,1,0:T(4,128)(2,1)}), bf16[32,4,1152]{2,1,0:T(4,128)(2,1)S(1)}, u32[]{:S(2)}, u32[]{:S(2)}) %all-to-all-start.4) | async-done | bytes 294944 | tf_op jit(solution)/shard_map/all_to_all | solution.py:52
  102.9 0.1 reshape.103.factors_ref
  102.9 0.9 shard_map.211
  103.9 6.7 %all-to-all-start.5 = ((bf16[16,48,128]{2,1,0:T(8,128)(2,1)}), bf16[16,48,128]{2,1,0:T(8,128)(2,1)S(1)}, u32[]{:S(2)}, u32[]{:S(2)}) async-start(bf16[16,48,128]{2,1,0:T(8,128)(2,1)} %shard_map.211), calls=%async_computation.5 | async-start | bytes 393216 | tf_op jit(solution)/shard_map/all_to_all | solution.py:52
  110.5 0.6 maximum_bitcast_fusion.1
  111.1 0.1 slice_bitcast_fusion.13
  111.2 0.6 maximum_bitcast_fusion
  111.8 9.4 %all-to-all-done.5.last_ref = bf16[16,48,128]{2,1,0:T(8,128)(2,1)S(1)} async-done(((bf16[16,48,128]{2,1,0:T(8,128)(2,1)}), bf16[16,48,128]{2,1,0:T(8,128)(2,1)S(1)}, u32[]{:S(2)}, u32[]{:S(2)}) %all-to-all-start.5) | async-done | bytes 196640 | tf_op jit(solution)/shard_map/all_to_all | solution.py:52
  121.2 1.5 %shard_map.212 = (f32[2,4,8192]{2,1,0:T(4,128)}, f32[2,4,512]{2,1,0:T(4,128)}, f32[2,4,512]{2,1,0:T(4,128)}) custom-call(bf16[16,48,128]{2,1,0:T(8,128)(2,1)S(1)} %all-to-all-done.5.last_ref, f32[8,1024]{1,0:T(8,128)S(1)} %bitcast_add_fusion.2.frozen_ref, f32[8,128]{1,0:T(8,128)S(1)} %get-tuple-element.74.cosine_ref, ...), custom_call_target="tpu_custom_call" | custom-call | flops 2097152 | bytes 262144 | tf_op jit(solution)/shard_map/pallas_call | solution.py:457
  (40 shorter events, 0.3 us)
Async XLA Ops:
  0.6 0.7 copy-start.4
  1.4 0.7 copy-start.8
  2.8 25.9 %all-to-all-start = ((bf16[32,4,1152]{2,1,0:T(4,128)(2,1)}), bf16[32,4,1152]{2,1,0:T(4,128)(2,1)S(1)}, u32[]{:S(2)}, u32[]{:S(2)}) async-start(bf16[32,4,1152]{2,1,0:T(4,128)(2,1)} %shard_map.205), calls=%async_computation | async-start | bytes 589824 | tf_op jit(solution)/shard_map/all_to_all | solution.py:52
  18.9 4.8 %copy-start.9 = (f32[2,32,2]{1,2,0:T(2,128)S(1)}, f32[2,32,2]{1,2,0:T(2,128)}, u32[]{:S(2)}) copy-start(f32[2,32,2]{1,2,0:T(2,128)} %param.17) | copy-start | bytes 1540
  18.9 4.8 %copy-start.10 = (s32[2]{0:T(128)S(1)}, s32[2]{0:T(128)}, u32[]{:S(2)}) copy-start(s32[2]{0:T(128)} %lengths_ref.1) | copy-start | bytes 28
  18.9 5.0 %copy-start.12 = (f32[2,32,2]{1,2,0:T(2,128)S(1)}, f32[2,32,2]{1,2,0:T(2,128)}, u32[]{:S(2)}) copy-start(f32[2,32,2]{1,2,0:T(2,128)} %param.21) | copy-start | bytes 1540
  18.9 5.0 %copy-start.13 = (f32[2,32,2]{1,2,0:T(2,128)S(1)}, f32[2,32,2]{1,2,0:T(2,128)}, u32[]{:S(2)}) copy-start(f32[2,32,2]{1,2,0:T(2,128)} %param.20) | copy-start | bytes 1540
  18.9 9.9 %copy-start = (bf16[256,1024]{1,0:T(8,128)(2,1)S(1)}, bf16[256,1024]{1,0:T(8,128)(2,1)}, u32[]{:S(2)}) copy-start(bf16[256,1024]{1,0:T(8,128)(2,1)} %inputs_ref.3) | copy-start | bytes 1572868
  18.9 9.9 %copy-start.3 = (bf16[2,32,256]{2,1,0:T(8,128)(2,1)S(1)}, bf16[2,32,256]{2,1,0:T(8,128)(2,1)}, u32[]{:S(2)}) copy-start(bf16[2,32,256]{2,1,0:T(8,128)(2,1)} %param.15) | copy-start | bytes 98308
  20.6 41.4 %copy-start.11 = (bf16[2,4,8192]{2,1,0:T(4,128)(2,1)S(1)}, bf16[2,4,8192]{2,1,0:T(4,128)(2,1)}, u32[]{:S(2)}) copy-start(bf16[2,4,8192]{2,1,0:T(4,128)(2,1)} %param.24) | copy-start | bytes 393220
  20.6 41.6 %copy-start.1 = (bf16[2,4,256,128]{3,2,1,0:T(8,128)(2,1)S(1)}, bf16[2,4,256,128]{3,2,1,0:T(8,128)(2,1)}, u32[]{:S(2)}) copy-start(bf16[2,4,256,128]{3,2,1,0:T(8,128)(2,1)} %key_ref.1) | copy-start | bytes 1572868
  20.7 41.6 %copy-start.2 = (bf16[2,4,256,128]{3,2,1,0:T(8,128)(2,1)S(1)}, bf16[2,4,256,128]{3,2,1,0:T(8,128)(2,1)}, u32[]{:S(2)}) copy-start(bf16[2,4,256,128]{3,2,1,0:T(8,128)(2,1)} %value_ref.1) | copy-start | bytes 1572868
  20.7 21.9 %collective-permute-start = (f32[2,2,2,8,1024]{4,3,2,1,0:T(8,128)S(1)}, f32[2,2,2,8,1024]{4,3,2,1,0:T(8,128)S(1)}, u32[]{:S(2)}, u32[]{:S(2)}) collective-permute-start(f32[2,2,2,8,1024]{4,3,2,1,0:T(8,128)S(1)} %get-tuple-element.55), channel_id=1, source_target_pairs={{0,1},{1,0},{2,3},{3,2},{4,5},{5,4},{6,7},{7,6},{8,9},{9,8},{10,11... | collective-permute-start | bytes 786440 | tf_op jit(solution)/shard_map/ppermute | solution.py:70
  29.8 22.6 %all-to-all-start.1 = ((bf16[16,16,256]{2,1,0:T(8,128)(2,1)}), bf16[16,16,256]{2,1,0:T(8,128)(2,1)S(1)}, u32[]{:S(2)}, u32[]{:S(2)}) async-start(bf16[16,16,256]{2,1,0:T(8,128)(2,1)} %bitcast.2), calls=%async_computation.1 | async-start | bytes 262144 | tf_op jit(solution)/shard_map/all_to_all | solution.py:52
  53.0 14.1 %all-to-all-start.2 = ((bf16[16,16,256]{2,1,0:T(8,128)(2,1)}), bf16[16,16,256]{2,1,0:T(8,128)(2,1)S(1)}, u32[]{:S(2)}, u32[]{:S(2)}) async-start(bf16[16,16,256]{2,1,0:T(8,128)(2,1)} %shard_map.207), calls=%async_computation.2 | async-start | bytes 262144 | tf_op jit(solution)/shard_map/all_to_all | solution.py:52
  57.0 15.8 %collective-permute-start.1 = (f32[2,2,8,1024]{3,2,1,0:T(8,128)S(1)}, f32[2,2,8,1024]{3,2,1,0:T(8,128)S(1)}, u32[]{:S(2)}, u32[]{:S(2)}) collective-permute-start(f32[2,2,8,1024]{3,2,1,0:T(8,128)S(1)} %select_bitcast_fusion.2), channel_id=1, source_target_pairs={{0,8},{1,9},{2,10},{3,11},{4,12},{5,13},{6,14},{7,15},{8,0},{9,1},... | collective-permute-start | bytes 393224 | tf_op jit(solution)/shard_map/ppermute | solution.py:70
  62.0 23.7 %copy-start.5 = (f32[2,2,1024]{2,1,0:T(2,128)S(1)}, f32[2,2,1024]{2,1,0:T(2,128)}, u32[]{:S(2)}) copy-start(f32[2,2,1024]{2,1,0:T(2,128)} %down_ref.3) | copy-start | bytes 49156
  62.0 23.7 %copy-start.6 = (f32[2,2,1024]{2,1,0:T(2,128)S(1)}, f32[2,2,1024]{2,1,0:T(2,128)}, u32[]{:S(2)}) copy-start(f32[2,2,1024]{2,1,0:T(2,128)} %down_first_ref.1) | copy-start | bytes 49156
  62.0 23.7 %copy-start.7 = (f32[2,2,1024]{2,1,0:T(2,128)S(1)}, f32[2,2,1024]{2,1,0:T(2,128)}, u32[]{:S(2)}) copy-start(f32[2,2,1024]{2,1,0:T(2,128)} %down_second_ref.1) | copy-start | bytes 49156
  68.1 17.5 %all-to-all-start.3 = ((bf16[32,4,1152]{2,1,0:T(4,128)(2,1)}), bf16[32,4,1152]{2,1,0:T(4,128)(2,1)S(1)}, u32[]{:S(2)}, u32[]{:S(2)}) async-start(bf16[32,4,1152]{2,1,0:T(4,128)(2,1)} %shard_map.208), calls=%async_computation.3 | async-start | bytes 589824 | tf_op jit(solution)/shard_map/all_to_all | solution.py:52
  72.9 5.3 %collective-permute-start.2 = (f32[2,8,1024]{2,1,0:T(8,128)S(1)}, f32[2,8,1024]{2,1,0:T(8,128)S(1)}, u32[]{:S(2)}, u32[]{:S(2)}) collective-permute-start(f32[2,8,1024]{2,1,0:T(8,128)S(1)} %select_bitcast_fusion.3), channel_id=1, source_target_pairs={{0,4},{1,5},{2,6},{3,7},{4,0},{5,1},{6,2},{7,3},{8,12},{9,13},{10,... | collective-permute-start | bytes 196616 | tf_op jit(solution)/shard_map/ppermute | solution.py:70
  86.6 16.3 %all-to-all-start.4 = ((bf16[32,4,1152]{2,1,0:T(4,128)(2,1)}), bf16[32,4,1152]{2,1,0:T(4,128)(2,1)S(1)}, u32[]{:S(2)}, u32[]{:S(2)}) async-start(bf16[32,4,1152]{2,1,0:T(4,128)(2,1)} %get-tuple-element.36), calls=%async_computation.4 | async-start | bytes 589824 | tf_op jit(solution)/shard_map/all_to_all | solution.py:52
  91.0 9.2 %collective-permute-start.3 = (f32[8,1024]{1,0:T(8,128)S(1)}, f32[8,1024]{1,0:T(8,128)S(1)}, u32[]{:S(2)}, u32[]{:S(2)}) collective-permute-start(f32[8,1024]{1,0:T(8,128)S(1)} %select_bitcast_fusion.4), channel_id=1, source_target_pairs={{0,2},{1,3},{2,0},{3,1},{4,6},{5,7},{6,4},{7,5},{8,10},{9,11},{10,... | collective-permute-start | bytes 98312 | tf_op jit(solution)/shard_map/ppermute | solution.py:70
  103.9 17.3 %all-to-all-start.5 = ((bf16[16,48,128]{2,1,0:T(8,128)(2,1)}), bf16[16,48,128]{2,1,0:T(8,128)(2,1)S(1)}, u32[]{:S(2)}, u32[]{:S(2)}) async-start(bf16[16,48,128]{2,1,0:T(8,128)(2,1)} %shard_map.211), calls=%async_computation.5 | async-start | bytes 393216 | tf_op jit(solution)/shard_map/all_to_all | solution.py:52

commit v6 on v5

--- a/solution.py
+++ b/solution.py
@@ -369,9 +369,22 @@
 
     flat_inputs = decode_step_inputs.reshape(-1, own_width)
 
+    sent = out((groups, own_rows, wide))
+    masters = call(send_masters, sent, adapter_down_master, by_rank(adapter_up_master))
+    later_inputs = after(flat_inputs, masters)
+    frozen_part = jnp.concatenate(
+        [product("rd,dc->rc", later_inputs, frozen_weights[kind]) for kind in range(kinds)], axis=1
+    ).reshape(ranks, own_lines, kinds * columns)
+    bits = ranks.bit_length() - 1
+    frozen_part = frozen_part.reshape((2,) * bits + (own_lines, kinds * columns))
+    factors = exchange(masters, "grp").reshape(all_rows, wide)
+
+    frozen_part = half_sum(frozen_part, "tp", ranks, bits - 1, 0, earlier_sum=factors)
+    frozen_part = half_sum(frozen_part, "tp", ranks, 1, bits - 2)
+
     lines = query_width // (head_groups * head_size) * own_lines
     query_lines = (
-        queries.reshape(row_count, steps_count, head_groups, -1, head_size)
+        after(queries, factors).reshape(row_count, steps_count, head_groups, -1, head_size)
         .transpose(2, 3, 0, 1, 4)
         .reshape(head_groups, lines, head_size)
     )
@@ -393,24 +406,12 @@
         ),
     )(lengths, query_lines, rotated_key_cache, stored_value_cache)
 
-    sent = out((groups, own_rows, wide))
-    masters = call(send_masters, sent, adapter_down_master, by_rank(adapter_up_master))
-    later_inputs = after(flat_inputs, masters)
-    frozen_part = jnp.concatenate(
-        [product("rd,dc->rc", later_inputs, frozen_weights[kind]) for kind in range(kinds)], axis=1
-    ).reshape(ranks, own_lines, kinds * columns)
-    bits = ranks.bit_length() - 1
-    frozen_part = frozen_part.reshape((2,) * bits + (own_lines, kinds * columns))
-    factors = exchange(masters, "grp").reshape(all_rows, wide)
-
-    frozen_part = half_sum(frozen_part, "tp", ranks, bits - 1, 0, earlier_sum=factors)
-    frozen_part = half_sum(frozen_part, "tp", ranks, 0, bits - 1)
-
     cotangents = weighted_output_cotangents.reshape(-1, tokens)
     shares = call(
         project_tokens, out((tokens, 2 * all_rows)), factors, trainer_token_inputs, cotangents
     ).reshape(ranks, -1, 2 * all_rows)
     sums = call(sum_tokens, out(shares.shape), exchange(shares, "tp"))
+    sums, peak, total, cached = lax.optimization_barrier((sums, peak, total, cached))
     token_sums = exchange(sums, "tp").reshape(tokens, 2 * all_rows)
 
     gradients = call(
@@ -420,8 +421,7 @@
         trainer_token_inputs,
         cotangents,
     )
-    frozen_part = half_sum(frozen_part, "tp", ranks, 0, 2, earlier_send=gradients)
-    gradients, peak, total, cached = lax.optimization_barrier((gradients, peak, total, cached))
+    frozen_part = half_sum(frozen_part, "tp", ranks, 0, bits - 1, earlier_send=gradients)
     own = out(adapter_down_master.shape, jnp.float32)
     small = out((own_rows, wide - own_width), jnp.float32)
     *fresh, fresh_factors = call(

time: 124 us -> 124 us (level)
  starting transfers between devices: 58.9 us -> 56.7 us
    ppermute x4, waiting for transfers between devices: 8.38 us -> 10.8 us  [half_sum(): arrived = lax.ppermute(jnp.where(upper, low, high), axis, pairs)]
    ppermute x4, starting transfers between devices: 13.2 us -> 11.1 us  [half_sum(): arrived = lax.ppermute(jnp.where(upper, low, high), axis, pairs)]
  transfers between devices with their start and end apart: 10 -> 10, of which waited for: 8 -> 8; matrix products, arithmetic and copies ran while one was open for 6% -> 7% of each run, Pallas kernels for 3% -> 3%
where the time goes in v6:
time: 124 us; the launch traced here: 123 us
  starting transfers between devices  56.7 us (46%)
  waiting for transfers between devices  46.8 us (38%)
  Pallas kernels  8.54 us (7%)
  local copies, waits for them, and re-layouts  4.06 us (3%)
  matrix products  3.08 us (2%)
  other arithmetic  2.45 us (2%)
    all_to_all x6, starting transfers between devices, exchange(): return lax.all_to_all(pieces, axis, 0, 0, tiled=True)  45.5 us
    all_to_all x6, waiting for transfers between devices, exchange(): return lax.all_to_all(pieces, axis, 0, 0, tiled=True)  36 us
    ppermute x4, starting transfers between devices, half_sum(): arrived = lax.ppermute(jnp.where(upper, low, high), axis, pairs)  11.1 us
    ppermute x4, waiting for transfers between devices, half_sum(): arrived = lax.ppermute(jnp.where(upper, low, high), axis, pairs)  10.8 us
    pallas_call x6, Pallas kernels, call(): pl.pallas_call(kernel, out_shape=outs, in_specs=[pl.BlockSpec(memory_spac...  5.3 us
    dot_general x2, matrix products, product(): return jnp.einsum(spec, left, right, preferred_element_type=jnp.float32)  3.08 us
  transfers between devices with their start and end apart: 10, of which 8 were waited for; matrix products, arithmetic and copies ran while one was open for 7% of the time, Pallas kernels for 3%

profile of v6, /device:TPU:1, one launch (start us, length us, event | category | flops | bytes accessed | tf_op | source)
XLA Modules:
  0.0 122.7 jit_solution(16285556427757543856)
XLA Ops:
  0.6 0.0 copy-start.4
  0.7 0.7 copy-done.4
  1.4 0.7 copy-done.8
  2.0 0.8 shard_map.205
  2.8 13.5 %all-to-all-start = ((bf16[32,4,1152]{2,1,0:T(4,128)(2,1)}), bf16[32,4,1152]{2,1,0:T(4,128)(2,1)S(1)}, u32[]{:S(2)}, u32[]{:S(2)}) async-start(bf16[32,4,1152]{2,1,0:T(4,128)(2,1)} %shard_map.205), calls=%async_computation | async-start | bytes 589824 | tf_op jit(solution)/shard_map/all_to_all | solution.py:52
  16.3 1.0 reshape.104.inputs_ref
  17.3 1.5 %fusion = f32[128,512]{1,0:T(8,128)S(1)} fusion(bf16[128,1024]{1,0:T(8,128)(2,1)S(1)} %reshape.104.inputs_ref, bf16[2,1024,512]{2,1,0:T(8,128)(2,1)} %param.22), kind=kOutput, calls=%fused_computation | convolution fusion | flops 134217728 | bytes 1572864 | tf_op jit(solution)/shard_map/rd,dc->rc/dot_general | solution.py:56
  18.9 1.5 %fusion.2 = f32[128,512]{1,0:T(8,128)S(1)} fusion(bf16[128,1024]{1,0:T(8,128)(2,1)S(1)} %reshape.104.inputs_ref, bf16[2,1024,512]{2,1,0:T(8,128)(2,1)} %param.22), kind=kOutput, calls=%fused_computation.2 | convolution fusion | flops 134217728 | bytes 1572864 | tf_op jit(solution)/shard_map/rd,dc->rc/dot_general | solution.py:56
  20.7 3.0 %collective-permute-start = (f32[2,2,2,8,1024]{4,3,2,0,1:T(8,128)S(1)}, f32[2,2,2,8,1024]{4,3,2,0,1:T(8,128)S(1)}, u32[]{:S(2)}, u32[]{:S(2)}) collective-permute-start(f32[2,2,2,8,1024]{4,3,2,0,1:T(8,128)S(1)} %get-tuple-element.57), channel_id=1, source_target_pairs={{0,1},{1,0},{2,3},{3,2},{4,5},{5,4},{6,7},{7,6},{8,9},{9,8},{10,11... | collective-permute-start | bytes 786440 | tf_op jit(solution)/shard_map/ppermute | solution.py:70
  23.7 0.1 add_convert_fusion
  23.8 0.1 select_maximum_fusion.2.up_ref
  23.9 4.9 %all-to-all-done = bf16[32,4,1152]{2,1,0:T(4,128)(2,1)S(1)} async-done(((bf16[32,4,1152]{2,1,0:T(4,128)(2,1)}), bf16[32,4,1152]{2,1,0:T(4,128)(2,1)S(1)}, u32[]{:S(2)}, u32[]{:S(2)}) %all-to-all-start) | async-done | bytes 294944 | tf_op jit(solution)/shard_map/all_to_all | solution.py:52
  28.7 0.1 reshape.97.factors_ref
  28.8 1.0 shard_map.206
  29.8 12.5 %all-to-all-start.1 = ((bf16[16,16,256]{2,1,0:T(8,128)(2,1)}), bf16[16,16,256]{2,1,0:T(8,128)(2,1)S(1)}, u32[]{:S(2)}, u32[]{:S(2)}) async-start(bf16[16,16,256]{2,1,0:T(8,128)(2,1)} %bitcast.2), calls=%async_computation.1 | async-start | bytes 262144 | tf_op jit(solution)/shard_map/all_to_all | solution.py:52
  42.3 0.1 convert_element_type.19
  42.4 0.1 fusion.6
  42.5 1.1 reshape.100
  43.6 0.1 copy.24
  43.8 1.7 %shard_map.208 = (f32[4,128,1]{2,1,0:T(8,128)S(1)}, f32[4,128,1]{2,1,0:T(8,128)S(1)}, f32[4,128,128]{2,1,0:T(8,128)S(1)}) custom-call(s32[2]{0:T(128)S(1)} %copy-done.10, bf16[4,128,128]{2,1,0:T(8,128)(2,1)S(1)} %bitcast.64, bf16[2,4,256,128]{3,2,1,0:T(8,128)(2,1)S(1)} %copy-done.1, bf16[2,4,256,128]{3,2,1,0:T(8,128)(2,1)S(1)} %copy-done.2), custom_call_target="tpu_custom_call" | custom-call | flops 134217728 | bytes 1048576 | tf_op jit(solution)/shard_map/pallas_call | solution.py:392
  45.5 6.8 %all-to-all-done.1.parts_ref = bf16[16,16,256]{2,1,0:T(8,128)(2,1)S(1)} async-done(((bf16[16,16,256]{2,1,0:T(8,128)(2,1)}), bf16[16,16,256]{2,1,0:T(8,128)(2,1)S(1)}, u32[]{:S(2)}, u32[]{:S(2)}) %all-to-all-start.1) | async-done | bytes 131104 | tf_op jit(solution)/shard_map/all_to_all | solution.py:52
  52.4 0.7 shard_map.207
  53.0 4.0 %all-to-all-start.2 = ((bf16[16,16,256]{2,1,0:T(8,128)(2,1)}), bf16[16,16,256]{2,1,0:T(8,128)(2,1)S(1)}, u32[]{:S(2)}, u32[]{:S(2)}) async-start(bf16[16,16,256]{2,1,0:T(8,128)(2,1)} %shard_map.207), calls=%async_computation.2 | async-start | bytes 262144 | tf_op jit(solution)/shard_map/all_to_all | solution.py:52
  57.0 3.3 %collective-permute-start.1 = (f32[2,2,8,1024]{3,2,1,0:T(8,128)S(1)}, f32[2,2,8,1024]{3,2,1,0:T(8,128)S(1)}, u32[]{:S(2)}, u32[]{:S(2)}) collective-permute-start(f32[2,2,8,1024]{3,2,1,0:T(8,128)S(1)} %select_bitcast_fusion.2), channel_id=1, source_target_pairs={{0,4},{1,5},{2,6},{3,7},{4,0},{5,1},{6,2},{7,3},{8,12},{9,13},{10,... | collective-permute-start | bytes 393224 | tf_op jit(solution)/shard_map/ppermute | solution.py:70
  60.3 0.1 select_maximum_fusion.1.up_first_ref
  60.4 0.1 pad_maximum_fusion.1
  60.5 6.6 %all-to-all-done.2 = bf16[16,16,256]{2,1,0:T(8,128)(2,1)S(1)} async-done(((bf16[16,16,256]{2,1,0:T(8,128)(2,1)}), bf16[16,16,256]{2,1,0:T(8,128)(2,1)S(1)}, u32[]{:S(2)}, u32[]{:S(2)}) %all-to-all-start.2) | async-done | bytes 131104 | tf_op jit(solution)/shard_map/all_to_all | solution.py:52
  67.1 1.0 shard_map.209
  68.1 4.7 %all-to-all-start.3 = ((bf16[32,4,1152]{2,1,0:T(4,128)(2,1)}), bf16[32,4,1152]{2,1,0:T(4,128)(2,1)S(1)}, u32[]{:S(2)}, u32[]{:S(2)}) async-start(bf16[32,4,1152]{2,1,0:T(4,128)(2,1)} %shard_map.209), calls=%async_computation.3 | async-start | bytes 589824 | tf_op jit(solution)/shard_map/all_to_all | solution.py:52
  72.9 2.7 %collective-permute-start.2 = (f32[2,8,1024]{2,1,0:T(8,128)S(1)}, f32[2,8,1024]{2,1,0:T(8,128)S(1)}, u32[]{:S(2)}, u32[]{:S(2)}) collective-permute-start(f32[2,8,1024]{2,1,0:T(8,128)S(1)} %select_bitcast_fusion.3), channel_id=1, source_target_pairs={{0,8},{1,9},{2,10},{3,11},{4,12},{5,13},{6,14},{7,15},{8,0},{9,1},... | collective-permute-start | bytes 196616 | tf_op jit(solution)/shard_map/ppermute | solution.py:70
  75.6 0.1 select_maximum_fusion.up_second_ref
  75.7 4.0 %collective-permute-done.2 = f32[2,8,1024]{2,1,0:T(8,128)S(1)} collective-permute-done((f32[2,8,1024]{2,1,0:T(8,128)S(1)}, f32[2,8,1024]{2,1,0:T(8,128)S(1)}, u32[]{:S(2)}, u32[]{:S(2)}) %collective-permute-start.2) | collective-permute-done | bytes 65568 | tf_op jit(solution)/shard_map/ppermute | solution.py:70
  79.7 5.9 %all-to-all-done.3.parts_ref = bf16[32,4,1152]{2,1,0:T(4,128)(2,1)S(1)} async-done(((bf16[32,4,1152]{2,1,0:T(4,128)(2,1)}), bf16[32,4,1152]{2,1,0:T(4,128)(2,1)S(1)}, u32[]{:S(2)}, u32[]{:S(2)}) %all-to-all-start.3) | async-done | bytes 294944 | tf_op jit(solution)/shard_map/all_to_all | solution.py:52
  85.6 0.9 shard_map.210
  86.6 4.5 %all-to-all-start.4 = ((bf16[32,4,1152]{2,1,0:T(4,128)(2,1)}), bf16[32,4,1152]{2,1,0:T(4,128)(2,1)S(1)}, u32[]{:S(2)}, u32[]{:S(2)}) async-start(bf16[32,4,1152]{2,1,0:T(4,128)(2,1)} %get-tuple-element.38), calls=%async_computation.4 | async-start | bytes 589824 | tf_op jit(solution)/shard_map/all_to_all | solution.py:52
  91.1 2.1 %collective-permute-start.3 = (f32[8,1024]{1,0:T(8,128)S(1)}, f32[8,1024]{1,0:T(8,128)S(1)}, u32[]{:S(2)}, u32[]{:S(2)}) collective-permute-start(f32[8,1024]{1,0:T(8,128)S(1)} %select_bitcast_fusion.4), channel_id=1, source_target_pairs={{0,2},{1,3},{2,0},{3,1},{4,6},{5,7},{6,4},{7,5},{8,10},{9,11},{10,... | collective-permute-start | bytes 98312 | tf_op jit(solution)/shard_map/ppermute | solution.py:70
  93.2 0.1 slice_bitcast_fusion.7
  93.3 6.8 %collective-permute-done.3 = f32[8,1024]{1,0:T(8,128)S(1)} collective-permute-done((f32[8,1024]{1,0:T(8,128)S(1)}, f32[8,1024]{1,0:T(8,128)S(1)}, u32[]{:S(2)}, u32[]{:S(2)}) %collective-permute-start.3) | collective-permute-done | bytes 32800 | tf_op jit(solution)/shard_map/ppermute | solution.py:70
  100.1 2.8 %all-to-all-done.4 = bf16[32,4,1152]{2,1,0:T(4,128)(2,1)S(1)} async-done(((bf16[32,4,1152]{2,1,0:T(4,128)(2,1)}), bf16[32,4,1152]{2,1,0:T(4,128)(2,1)S(1)}, u32[]{:S(2)}, u32[]{:S(2)}) %all-to-all-start.4) | async-done | bytes 294944 | tf_op jit(solution)/shard_map/all_to_all | solution.py:52
  102.9 0.1 reshape.103.factors_ref
  103.0 0.9 shard_map.211
  103.9 6.4 %all-to-all-start.5 = ((bf16[16,48,128]{2,1,0:T(8,128)(2,1)}), bf16[16,48,128]{2,1,0:T(8,128)(2,1)S(1)}, u32[]{:S(2)}, u32[]{:S(2)}) async-start(bf16[16,48,128]{2,1,0:T(8,128)(2,1)} %shard_map.211), calls=%async_computation.5 | async-start | bytes 393216 | tf_op jit(solution)/shard_map/all_to_all | solution.py:52
  110.3 0.1 slice_bitcast_fusion.11
  110.4 0.6 maximum_bitcast_fusion
  111.0 0.6 maximum_bitcast_fusion.2
  111.6 0.6 maximum_bitcast_fusion.1
  112.2 9.0 %all-to-all-done.5.last_ref = bf16[16,48,128]{2,1,0:T(8,128)(2,1)S(1)} async-done(((bf16[16,48,128]{2,1,0:T(8,128)(2,1)}), bf16[16,48,128]{2,1,0:T(8,128)(2,1)S(1)}, u32[]{:S(2)}, u32[]{:S(2)}) %all-to-all-start.5) | async-done | bytes 196640 | tf_op jit(solution)/shard_map/all_to_all | solution.py:52
  121.1 1.5 %shard_map.212 = (f32[2,4,8192]{2,1,0:T(4,128)}, f32[2,4,512]{2,1,0:T(4,128)}, f32[2,4,512]{2,1,0:T(4,128)}) custom-call(bf16[16,48,128]{2,1,0:T(8,128)(2,1)S(1)} %all-to-all-done.5.last_ref, f32[8,1024]{1,0:T(8,128)S(1)} %bitcast_add_fusion.2.frozen_ref, f32[8,128]{1,0:T(8,128)S(1)} %get-tuple-element.78.cosine_ref, ...), custom_call_target="tpu_custom_call" | custom-call | flops 2097152 | bytes 262144 | tf_op jit(solution)/shard_map/pallas_call | solution.py:457
  (39 shorter events, 0.3 us)
Async XLA Ops:
  0.6 0.7 copy-start.4
  1.4 0.7 copy-start.8
  2.8 25.9 %all-to-all-start = ((bf16[32,4,1152]{2,1,0:T(4,128)(2,1)}), bf16[32,4,1152]{2,1,0:T(4,128)(2,1)S(1)}, u32[]{:S(2)}, u32[]{:S(2)}) async-start(bf16[32,4,1152]{2,1,0:T(4,128)(2,1)} %shard_map.205), calls=%async_computation | async-start | bytes 589824 | tf_op jit(solution)/shard_map/all_to_all | solution.py:52
  18.9 4.8 %copy-start.9 = (f32[2,32,2]{1,2,0:T(2,128)S(1)}, f32[2,32,2]{1,2,0:T(2,128)}, u32[]{:S(2)}) copy-start(f32[2,32,2]{1,2,0:T(2,128)} %param.17) | copy-start | bytes 1540
  18.9 4.8 %copy-start.10 = (s32[2]{0:T(128)S(1)}, s32[2]{0:T(128)}, u32[]{:S(2)}) copy-start(s32[2]{0:T(128)} %lengths_ref.1) | copy-start | bytes 28
  18.9 5.0 %copy-start.11 = (f32[2,32,2]{1,2,0:T(2,128)S(1)}, f32[2,32,2]{1,2,0:T(2,128)}, u32[]{:S(2)}) copy-start(f32[2,32,2]{1,2,0:T(2,128)} %param.20) | copy-start | bytes 1540
  18.9 5.0 %copy-start.12 = (f32[2,32,2]{1,2,0:T(2,128)S(1)}, f32[2,32,2]{1,2,0:T(2,128)}, u32[]{:S(2)}) copy-start(f32[2,32,2]{1,2,0:T(2,128)} %param.21) | copy-start | bytes 1540
  20.5 8.3 %copy-start = (bf16[256,1024]{1,0:T(8,128)(2,1)S(1)}, bf16[256,1024]{1,0:T(8,128)(2,1)}, u32[]{:S(2)}) copy-start(bf16[256,1024]{1,0:T(8,128)(2,1)} %inputs_ref.3) | copy-start | bytes 1572868
  20.5 8.3 %copy-start.3 = (bf16[2,32,256]{2,1,0:T(8,128)(2,1)S(1)}, bf16[2,32,256]{2,1,0:T(8,128)(2,1)}, u32[]{:S(2)}) copy-start(bf16[2,32,256]{2,1,0:T(8,128)(2,1)} %param.15) | copy-start | bytes 98308
  20.6 23.2 %copy-start.1 = (bf16[2,4,256,128]{3,2,1,0:T(8,128)(2,1)S(1)}, bf16[2,4,256,128]{3,2,1,0:T(8,128)(2,1)}, u32[]{:S(2)}) copy-start(bf16[2,4,256,128]{3,2,1,0:T(8,128)(2,1)} %key_ref.1) | copy-start | bytes 1572868
  20.6 23.2 %copy-start.2 = (bf16[2,4,256,128]{3,2,1,0:T(8,128)(2,1)S(1)}, bf16[2,4,256,128]{3,2,1,0:T(8,128)(2,1)}, u32[]{:S(2)}) copy-start(bf16[2,4,256,128]{3,2,1,0:T(8,128)(2,1)} %value_ref.1) | copy-start | bytes 1572868
  20.7 23.0 %collective-permute-start = (f32[2,2,2,8,1024]{4,3,2,0,1:T(8,128)S(1)}, f32[2,2,2,8,1024]{4,3,2,0,1:T(8,128)S(1)}, u32[]{:S(2)}, u32[]{:S(2)}) collective-permute-start(f32[2,2,2,8,1024]{4,3,2,0,1:T(8,128)S(1)} %get-tuple-element.57), channel_id=1, source_target_pairs={{0,1},{1,0},{2,3},{3,2},{4,5},{5,4},{6,7},{7,6},{8,9},{9,8},{10,11... | collective-permute-start | bytes 786440 | tf_op jit(solution)/shard_map/ppermute | solution.py:70
  29.8 22.6 %all-to-all-start.1 = ((bf16[16,16,256]{2,1,0:T(8,128)(2,1)}), bf16[16,16,256]{2,1,0:T(8,128)(2,1)S(1)}, u32[]{:S(2)}, u32[]{:S(2)}) async-start(bf16[16,16,256]{2,1,0:T(8,128)(2,1)} %bitcast.2), calls=%async_computation.1 | async-start | bytes 262144 | tf_op jit(solution)/shard_map/all_to_all | solution.py:52
  43.8 41.8 %copy-start.5 = (f32[2,2,1024]{2,1,0:T(2,128)S(1)}, f32[2,2,1024]{2,1,0:T(2,128)}, u32[]{:S(2)}) copy-start(f32[2,2,1024]{2,1,0:T(2,128)} %down_ref.3) | copy-start | bytes 49156
  43.8 41.8 %copy-start.6 = (f32[2,2,1024]{2,1,0:T(2,128)S(1)}, f32[2,2,1024]{2,1,0:T(2,128)}, u32[]{:S(2)}) copy-start(f32[2,2,1024]{2,1,0:T(2,128)} %down_first_ref.1) | copy-start | bytes 49156
  43.8 41.8 %copy-start.7 = (f32[2,2,1024]{2,1,0:T(2,128)S(1)}, f32[2,2,1024]{2,1,0:T(2,128)}, u32[]{:S(2)}) copy-start(f32[2,2,1024]{2,1,0:T(2,128)} %down_second_ref.1) | copy-start | bytes 49156
  53.0 14.1 %all-to-all-start.2 = ((bf16[16,16,256]{2,1,0:T(8,128)(2,1)}), bf16[16,16,256]{2,1,0:T(8,128)(2,1)S(1)}, u32[]{:S(2)}, u32[]{:S(2)}) async-start(bf16[16,16,256]{2,1,0:T(8,128)(2,1)} %shard_map.207), calls=%async_computation.2 | async-start | bytes 262144 | tf_op jit(solution)/shard_map/all_to_all | solution.py:52
  57.0 15.8 %collective-permute-start.1 = (f32[2,2,8,1024]{3,2,1,0:T(8,128)S(1)}, f32[2,2,8,1024]{3,2,1,0:T(8,128)S(1)}, u32[]{:S(2)}, u32[]{:S(2)}) collective-permute-start(f32[2,2,8,1024]{3,2,1,0:T(8,128)S(1)} %select_bitcast_fusion.2), channel_id=1, source_target_pairs={{0,4},{1,5},{2,6},{3,7},{4,0},{5,1},{6,2},{7,3},{8,12},{9,13},{10,... | collective-permute-start | bytes 393224 | tf_op jit(solution)/shard_map/ppermute | solution.py:70
  68.1 17.5 %all-to-all-start.3 = ((bf16[32,4,1152]{2,1,0:T(4,128)(2,1)}), bf16[32,4,1152]{2,1,0:T(4,128)(2,1)S(1)}, u32[]{:S(2)}, u32[]{:S(2)}) async-start(bf16[32,4,1152]{2,1,0:T(4,128)(2,1)} %shard_map.209), calls=%async_computation.3 | async-start | bytes 589824 | tf_op jit(solution)/shard_map/all_to_all | solution.py:52
  72.9 6.8 %collective-permute-start.2 = (f32[2,8,1024]{2,1,0:T(8,128)S(1)}, f32[2,8,1024]{2,1,0:T(8,128)S(1)}, u32[]{:S(2)}, u32[]{:S(2)}) collective-permute-start(f32[2,8,1024]{2,1,0:T(8,128)S(1)} %select_bitcast_fusion.3), channel_id=1, source_target_pairs={{0,8},{1,9},{2,10},{3,11},{4,12},{5,13},{6,14},{7,15},{8,0},{9,1},... | collective-permute-start | bytes 196616 | tf_op jit(solution)/shard_map/ppermute | solution.py:70
  86.6 16.4 %all-to-all-start.4 = ((bf16[32,4,1152]{2,1,0:T(4,128)(2,1)}), bf16[32,4,1152]{2,1,0:T(4,128)(2,1)S(1)}, u32[]{:S(2)}, u32[]{:S(2)}) async-start(bf16[32,4,1152]{2,1,0:T(4,128)(2,1)} %get-tuple-element.38), calls=%async_computation.4 | async-start | bytes 589824 | tf_op jit(solution)/shard_map/all_to_all | solution.py:52
  91.1 9.0 %collective-permute-start.3 = (f32[8,1024]{1,0:T(8,128)S(1)}, f32[8,1024]{1,0:T(8,128)S(1)}, u32[]{:S(2)}, u32[]{:S(2)}) collective-permute-start(f32[8,1024]{1,0:T(8,128)S(1)} %select_bitcast_fusion.4), channel_id=1, source_target_pairs={{0,2},{1,3},{2,0},{3,1},{4,6},{5,7},{6,4},{7,5},{8,10},{9,11},{10,... | collective-permute-start | bytes 98312 | tf_op jit(solution)/shard_map/ppermute | solution.py:70
  103.9 17.2 %all-to-all-start.5 = ((bf16[16,48,128]{2,1,0:T(8,128)(2,1)}), bf16[16,48,128]{2,1,0:T(8,128)(2,1)S(1)}, u32[]{:S(2)}, u32[]{:S(2)}) async-start(bf16[16,48,128]{2,1,0:T(8,128)(2,1)} %shard_map.211), calls=%async_computation.5 | async-start | bytes 393216 | tf_op jit(solution)/shard_map/all_to_all | solution.py:52

commit v7 on v6

--- a/solution.py
+++ b/solution.py
@@ -60,18 +60,18 @@
     return lax.optimization_barrier((values, earlier))[0]
 
 
-def half_sum(values, axis, count, at, bit, earlier_sum=None, earlier_send=None):
+def half_sum(values, axis, count, at, bit, earlier_sum=None, earlier_send=None, kind=jnp.float32):
     if earlier_send is not None:
         values = after(values, earlier_send)
     low = lax.index_in_dim(values, 0, at, keepdims=False)
     high = lax.index_in_dim(values, 1, at, keepdims=False)
     upper = (lax.axis_index(axis) >> bit) & 1 == 1
     pairs = [(place, place ^ (1 << bit)) for place in range(count)]
-    arrived = lax.ppermute(jnp.where(upper, low, high), axis, pairs)
+    arrived = lax.ppermute(jnp.where(upper, low, high).astype(kind), axis, pairs)
     kept = jnp.where(upper, high, low)
     if earlier_sum is not None:
         kept = after(kept, earlier_sum)
-    return kept + arrived
+    return kept + arrived.astype(jnp.float32)
 
 
 def dot_last(left, right):
@@ -352,13 +352,13 @@
         ]
         return by_rank(jnp.stack(blocks))
 
-    def call(kernel, outs, *operands):
+    def call(kernel, outs, *operands, limit=KERNEL_BYTES):
         flops = 4 * max(operand.size for operand in operands)
         return pl.pallas_call(
             kernel,
             out_shape=outs,
             in_specs=[pl.BlockSpec(memory_space=pltpu.VMEM)] * len(operands),
-            compiler_params=pltpu.CompilerParams(vmem_limit_bytes=KERNEL_BYTES),
+            compiler_params=pltpu.CompilerParams(vmem_limit_bytes=limit),
             cost_estimate=pl.CostEstimate(
                 flops=flops, bytes_accessed=flops, transcendentals=0
             ),
@@ -370,7 +370,9 @@
     flat_inputs = decode_step_inputs.reshape(-1, own_width)
 
     sent = out((groups, own_rows, wide))
-    masters = call(send_masters, sent, adapter_down_master, by_rank(adapter_up_master))
+    masters = call(
+        send_masters, sent, adapter_down_master, by_rank(adapter_up_master), limit=None
+    )
     later_inputs = after(flat_inputs, masters)
     frozen_part = jnp.concatenate(
         [product("rd,dc->rc", later_inputs, frozen_weights[kind]) for kind in range(kinds)], axis=1
@@ -421,7 +423,6 @@
         trainer_token_inputs,
         cotangents,
     )
-    frozen_part = half_sum(frozen_part, "tp", ranks, 0, bits - 1, earlier_send=gradients)
     own = out(adapter_down_master.shape, jnp.float32)
     small = out((own_rows, wide - own_width), jnp.float32)
     *fresh, fresh_factors = call(
@@ -435,7 +436,17 @@
         placed(up_first_moment),
         placed(up_second_moment),
     )
-    frozen_sum = half_sum(frozen_part, "tp", ranks, 0, 1, earlier_send=fresh_factors)
+    frozen_part = half_sum(
+        frozen_part,
+        "tp",
+        ranks,
+        1,
+        1,
+        earlier_sum=fresh_factors,
+        earlier_send=gradients,
+        kind=jnp.bfloat16,
+    )
+    frozen_sum = half_sum(frozen_part, "tp", ranks, 0, bits - 1)
     factors = exchange(fresh_factors, "grp").reshape(all_rows, wide)
 
     rank_space = call(

time: 124 us -> 124 us (level)
  local copies, waits for them, and re-layouts: 4.06 us -> 1.77 us
  other arithmetic: 2.45 us -> 4.11 us
    ppermute x4, waiting for transfers between devices: 10.8 us -> 3.35 us  [half_sum(): lax.ppermute(jnp.where(upper, low, high).astype(kind), axis, pairs)]
    all_to_all x6, waiting for transfers between devices: 36 us -> 42.9 us  [exchange(): return lax.all_to_all(pieces, axis, 0, 0, tiled=True)]
    unnamed x26 -> x24, local copies, waits for them, and re-layouts: 1.46 us -> 0.08 us
  transfers between devices with their start and end apart: 10 -> 10, of which waited for: 8 -> 7; matrix products, arithmetic and copies ran while one was open for 7% -> 7% of each run, Pallas kernels for 3% -> 4%
where the time goes in v7:
time: 124 us; the launch traced here: 123 us
  starting transfers between devices  57.1 us (46%)
  waiting for transfers between devices  46.2 us (37%)
  Pallas kernels  9.27 us (7%)
  other arithmetic  4.11 us (3%)
  matrix products  3.08 us (2%)
  local copies, waits for them, and re-layouts  1.77 us (1%)
    all_to_all x6, starting transfers between devices, exchange(): return lax.all_to_all(pieces, axis, 0, 0, tiled=True)  46.1 us
    all_to_all x6, waiting for transfers between devices, exchange(): return lax.all_to_all(pieces, axis, 0, 0, tiled=True)  42.9 us
    ppermute x4, starting transfers between devices, half_sum(): lax.ppermute(jnp.where(upper, low, high).astype(kind), axis, pairs)  11 us
    pallas_call x6, Pallas kernels, call(): pl.pallas_call(kernel, out_shape=outs, in_specs=[pl.BlockSpec(memory_spac...  6.03 us
    ppermute x4, waiting for transfers between devices, half_sum(): lax.ppermute(jnp.where(upper, low, high).astype(kind), axis, pairs)  3.35 us
    dot_general x2, matrix products, product(): return jnp.einsum(spec, left, right, preferred_element_type=jnp.float32)  3.08 us
  transfers between devices with their start and end apart: 10, of which 7 were waited for; matrix products, arithmetic and copies ran while one was open for 7% of the time, Pallas kernels for 4%

profile of v7, /device:TPU:1, one launch (start us, length us, event | category | flops | bytes accessed | tf_op | source)
XLA Modules:
  0.0 122.6 jit_solution(1898713780985272261)
XLA Ops:
  0.6 1.5 %shard_map.205 = bf16[32,4,1152]{2,1,0:T(4,128)(2,1)} custom-call(f32[2,2,1024]{2,1,0:T(2,128)} %down_ref.3, f32[2,2,32]{2,1,0:T(2,128)} %bitcast.70), custom_call_target="tpu_custom_call" | custom-call | flops 16384 | bytes 16384 | tf_op jit(solution)/shard_map/pallas_call | solution.py:357
  2.2 13.5 %all-to-all-start = ((bf16[32,4,1152]{2,1,0:T(4,128)(2,1)}), bf16[32,4,1152]{2,1,0:T(4,128)(2,1)S(1)}, u32[]{:S(2)}, u32[]{:S(2)}) async-start(bf16[32,4,1152]{2,1,0:T(4,128)(2,1)} %shard_map.205), calls=%async_computation | async-start | bytes 589824 | tf_op jit(solution)/shard_map/all_to_all | solution.py:52
  15.6 1.0 reshape.105.inputs_ref
  16.7 1.5 %fusion = f32[128,512]{1,0:T(8,128)S(1)} fusion(bf16[128,1024]{1,0:T(8,128)(2,1)S(1)} %reshape.105.inputs_ref, bf16[2,1024,512]{2,1,0:T(8,128)(2,1)} %param.22), kind=kOutput, calls=%fused_computation | convolution fusion | flops 134217728 | bytes 1572864 | tf_op jit(solution)/shard_map/rd,dc->rc/dot_general | solution.py:56
  18.2 0.0 copy-start.9
  18.2 0.0 copy-start.10
  18.2 1.5 %fusion.2 = f32[128,512]{1,0:T(8,128)S(1)} fusion(bf16[128,1024]{1,0:T(8,128)(2,1)S(1)} %reshape.105.inputs_ref, bf16[2,1024,512]{2,1,0:T(8,128)(2,1)} %param.22), kind=kOutput, calls=%fused_computation.2 | convolution fusion | flops 134217728 | bytes 1572864 | tf_op jit(solution)/shard_map/rd,dc->rc/dot_general | solution.py:56
  20.0 0.8 select_bitcast_fusion
  20.7 2.9 %collective-permute-start = (f32[2,2,2,8,1024]{4,3,0,2,1:T(8,128)}, f32[2,2,2,8,1024]{4,3,0,2,1:T(8,128)}, u32[]{:S(2)}, u32[]{:S(2)}) collective-permute-start(f32[2,2,2,8,1024]{4,3,0,2,1:T(8,128)} %get-tuple-element.57), channel_id=1, source_target_pairs={{0,1},{1,0},{2,3},{3,2},{4,5},{5,4},{6,7},{7,6},{8,9},{9,8},{10,11... | collective-permute-start | bytes 786440 | tf_op jit(solution)/shard_map/ppermute | solution.py:70
  23.6 0.1 select_maximum_fusion.2.up_ref
  23.7 0.1 select_maximum_fusion.1.up_first_ref
  23.8 0.1 add_convert_fusion
  23.9 4.2 %all-to-all-done = bf16[32,4,1152]{2,1,0:T(4,128)(2,1)S(1)} async-done(((bf16[32,4,1152]{2,1,0:T(4,128)(2,1)}), bf16[32,4,1152]{2,1,0:T(4,128)(2,1)S(1)}, u32[]{:S(2)}, u32[]{:S(2)}) %all-to-all-start) | async-done | bytes 294944 | tf_op jit(solution)/shard_map/all_to_all | solution.py:52
  28.0 0.1 reshape.98.factors_ref
  28.1 1.0 shard_map.206
  29.1 12.5 %all-to-all-start.1 = ((bf16[16,16,256]{2,1,0:T(8,128)(2,1)}), bf16[16,16,256]{2,1,0:T(8,128)(2,1)S(1)}, u32[]{:S(2)}, u32[]{:S(2)}) async-start(bf16[16,16,256]{2,1,0:T(8,128)(2,1)} %bitcast.2), calls=%async_computation.1 | async-start | bytes 262144 | tf_op jit(solution)/shard_map/all_to_all | solution.py:52
  41.7 0.1 convert_element_type.31
  41.7 0.1 fusion.7
  41.9 0.2 reshape.101
  42.0 0.1 copy.24
  42.1 1.0 add.54
  43.2 1.7 %shard_map.208 = (f32[4,128,1]{2,1,0:T(8,128)S(1)}, f32[4,128,1]{2,1,0:T(8,128)S(1)}, f32[4,128,128]{2,1,0:T(8,128)S(1)}) custom-call(s32[2]{0:T(128)S(1)} %copy-done.7, bf16[4,128,128]{2,1,0:T(8,128)(2,1)S(1)} %bitcast.64, bf16[2,4,256,128]{3,2,1,0:T(8,128)(2,1)S(1)} %copy-done.1, bf16[2,4,256,128]{3,2,1,0:T(8,128)(2,1)S(1)} %copy-done.2), custom_call_target="tpu_custom_call" | custom-call | flops 134217728 | bytes 1048576 | tf_op jit(solution)/shard_map/pallas_call | solution.py:394
  44.9 6.8 %all-to-all-done.1.parts_ref = bf16[16,16,256]{2,1,0:T(8,128)(2,1)S(1)} async-done(((bf16[16,16,256]{2,1,0:T(8,128)(2,1)}), bf16[16,16,256]{2,1,0:T(8,128)(2,1)S(1)}, u32[]{:S(2)}, u32[]{:S(2)}) %all-to-all-start.1) | async-done | bytes 131104 | tf_op jit(solution)/shard_map/all_to_all | solution.py:52
  51.7 0.7 shard_map.207
  52.4 4.0 %all-to-all-start.2 = ((bf16[16,16,256]{2,1,0:T(8,128)(2,1)}), bf16[16,16,256]{2,1,0:T(8,128)(2,1)S(1)}, u32[]{:S(2)}, u32[]{:S(2)}) async-start(bf16[16,16,256]{2,1,0:T(8,128)(2,1)} %shard_map.207), calls=%async_computation.2 | async-start | bytes 262144 | tf_op jit(solution)/shard_map/all_to_all | solution.py:52
  56.3 3.3 %collective-permute-start.1 = (f32[2,2,8,1024]{3,2,0,1:T(8,128)S(1)}, f32[2,2,8,1024]{3,2,0,1:T(8,128)S(1)}, u32[]{:S(2)}, u32[]{:S(2)}) collective-permute-start(f32[2,2,8,1024]{3,2,0,1:T(8,128)S(1)} %select_bitcast_fusion.2), channel_id=1, source_target_pairs={{0,4},{1,5},{2,6},{3,7},{4,0},{5,1},{6,2},{7,3},{8,12},{9,13},{10,... | collective-permute-start | bytes 393224 | tf_op jit(solution)/shard_map/ppermute | solution.py:70
  59.7 0.1 select_maximum_fusion.up_second_ref
  59.7 0.1 pad_maximum_fusion.1
  59.8 6.6 %all-to-all-done.2 = bf16[16,16,256]{2,1,0:T(8,128)(2,1)S(1)} async-done(((bf16[16,16,256]{2,1,0:T(8,128)(2,1)}), bf16[16,16,256]{2,1,0:T(8,128)(2,1)S(1)}, u32[]{:S(2)}, u32[]{:S(2)}) %all-to-all-start.2) | async-done | bytes 131104 | tf_op jit(solution)/shard_map/all_to_all | solution.py:52
  66.5 1.0 shard_map.209
  67.4 4.9 %all-to-all-start.3 = ((bf16[32,4,1152]{2,1,0:T(4,128)(2,1)}), bf16[32,4,1152]{2,1,0:T(4,128)(2,1)S(1)}, u32[]{:S(2)}, u32[]{:S(2)}) async-start(bf16[32,4,1152]{2,1,0:T(4,128)(2,1)} %shard_map.209), calls=%async_computation.3 | async-start | bytes 589824 | tf_op jit(solution)/shard_map/all_to_all | solution.py:52
  72.4 2.1 %collective-permute-start.2 = (bf16[2,8,1024]{2,1,0:T(8,128)(2,1)S(1)}, bf16[2,8,1024]{2,1,0:T(8,128)(2,1)S(1)}, u32[]{:S(2)}, u32[]{:S(2)}) collective-permute-start(bf16[2,8,1024]{2,1,0:T(8,128)(2,1)S(1)} %fusion.6), channel_id=1, source_target_pairs={{0,2},{1,3},{2,0},{3,1},{4,6},{5,7},{6,4},{7,5},{8,10},{9,11},{10,... | collective-permute-start | bytes 98312 | tf_op jit(solution)/shard_map/ppermute | solution.py:70
  74.6 10.6 %all-to-all-done.3.parts_ref = bf16[32,4,1152]{2,1,0:T(4,128)(2,1)S(1)} async-done(((bf16[32,4,1152]{2,1,0:T(4,128)(2,1)}), bf16[32,4,1152]{2,1,0:T(4,128)(2,1)S(1)}, u32[]{:S(2)}, u32[]{:S(2)}) %all-to-all-start.3) | async-done | bytes 294944 | tf_op jit(solution)/shard_map/all_to_all | solution.py:52
  85.2 0.9 shard_map.210
  86.1 4.9 %all-to-all-start.4 = ((bf16[32,4,1152]{2,1,0:T(4,128)(2,1)}), bf16[32,4,1152]{2,1,0:T(4,128)(2,1)S(1)}, u32[]{:S(2)}, u32[]{:S(2)}) async-start(bf16[32,4,1152]{2,1,0:T(4,128)(2,1)} %get-tuple-element.38), calls=%async_computation.4 | async-start | bytes 589824 | tf_op jit(solution)/shard_map/all_to_all | solution.py:52
  91.1 2.7 %collective-permute-start.3 = (f32[8,1024]{1,0:T(8,128)S(1)}, f32[8,1024]{1,0:T(8,128)S(1)}, u32[]{:S(2)}, u32[]{:S(2)}) collective-permute-start(f32[8,1024]{1,0:T(8,128)S(1)} %select_bitcast_fusion.4), channel_id=1, source_target_pairs={{0,8},{1,9},{2,10},{3,11},{4,12},{5,13},{6,14},{7,15},{8,0},{9,1},... | collective-permute-start | bytes 98312 | tf_op jit(solution)/shard_map/ppermute | solution.py:70
  93.9 0.1 slice_bitcast_fusion.7
  94.0 3.3 %collective-permute-done.3 = f32[8,1024]{1,0:T(8,128)S(1)} collective-permute-done((f32[8,1024]{1,0:T(8,128)S(1)}, f32[8,1024]{1,0:T(8,128)S(1)}, u32[]{:S(2)}, u32[]{:S(2)}) %collective-permute-start.3) | collective-permute-done | bytes 32800 | tf_op jit(solution)/shard_map/ppermute | solution.py:70
  97.3 5.7 %all-to-all-done.4 = bf16[32,4,1152]{2,1,0:T(4,128)(2,1)S(1)} async-done(((bf16[32,4,1152]{2,1,0:T(4,128)(2,1)}), bf16[32,4,1152]{2,1,0:T(4,128)(2,1)S(1)}, u32[]{:S(2)}, u32[]{:S(2)}) %all-to-all-start.4) | async-done | bytes 294944 | tf_op jit(solution)/shard_map/all_to_all | solution.py:52
  103.0 0.1 reshape.104.factors_ref
  103.1 0.9 shard_map.211
  104.0 6.3 %all-to-all-start.5 = ((bf16[16,48,128]{2,1,0:T(8,128)(2,1)}), bf16[16,48,128]{2,1,0:T(8,128)(2,1)S(1)}, u32[]{:S(2)}, u32[]{:S(2)}) async-start(bf16[16,48,128]{2,1,0:T(8,128)(2,1)} %shard_map.211), calls=%async_computation.5 | async-start | bytes 393216 | tf_op jit(solution)/shard_map/all_to_all | solution.py:52
  110.3 0.1 slice_bitcast_fusion.11
  110.4 0.6 maximum_bitcast_fusion
  110.9 0.6 maximum_bitcast_fusion.2
  111.5 0.6 maximum_bitcast_fusion.1
  112.1 9.0 %all-to-all-done.5.last_ref = bf16[16,48,128]{2,1,0:T(8,128)(2,1)S(1)} async-done(((bf16[16,48,128]{2,1,0:T(8,128)(2,1)}), bf16[16,48,128]{2,1,0:T(8,128)(2,1)S(1)}, u32[]{:S(2)}, u32[]{:S(2)}) %all-to-all-start.5) | async-done | bytes 196640 | tf_op jit(solution)/shard_map/all_to_all | solution.py:52
  121.1 1.5 %shard_map.212 = (f32[2,4,8192]{2,1,0:T(4,128)}, f32[2,4,512]{2,1,0:T(4,128)}, f32[2,4,512]{2,1,0:T(4,128)}) custom-call(bf16[16,48,128]{2,1,0:T(8,128)(2,1)S(1)} %all-to-all-done.5.last_ref, f32[8,1024]{1,0:T(8,128)S(1)} %bitcast_add_fusion.1.frozen_ref, f32[8,128]{1,0:T(8,128)S(1)} %get-tuple-element.78.cosine_ref, ...), custom_call_target="tpu_custom_call" | custom-call | flops 2097152 | bytes 262144 | tf_op jit(solution)/shard_map/pallas_call | solution.py:468
  (38 shorter events, 0.3 us)
Async XLA Ops:
  2.2 25.9 %all-to-all-start = ((bf16[32,4,1152]{2,1,0:T(4,128)(2,1)}), bf16[32,4,1152]{2,1,0:T(4,128)(2,1)S(1)}, u32[]{:S(2)}, u32[]{:S(2)}) async-start(bf16[32,4,1152]{2,1,0:T(4,128)(2,1)} %shard_map.205), calls=%async_computation | async-start | bytes 589824 | tf_op jit(solution)/shard_map/all_to_all | solution.py:52
  18.2 5.4 %copy-start.9 = (f32[2,32,2]{1,2,0:T(2,128)S(1)}, f32[2,32,2]{1,2,0:T(2,128)}, u32[]{:S(2)}) copy-start(f32[2,32,2]{1,2,0:T(2,128)} %param.17) | copy-start | bytes 1540
  18.2 5.4 %copy-start.10 = (f32[2,32,2]{1,2,0:T(2,128)S(1)}, f32[2,32,2]{1,2,0:T(2,128)}, u32[]{:S(2)}) copy-start(f32[2,32,2]{1,2,0:T(2,128)} %param.20) | copy-start | bytes 1540
  18.2 5.6 %copy-start.7 = (s32[2]{0:T(128)S(1)}, s32[2]{0:T(128)}, u32[]{:S(2)}) copy-start(s32[2]{0:T(128)} %lengths_ref.1) | copy-start | bytes 28
  18.2 5.6 %copy-start.11 = (f32[2,32,2]{1,2,0:T(2,128)S(1)}, f32[2,32,2]{1,2,0:T(2,128)}, u32[]{:S(2)}) copy-start(f32[2,32,2]{1,2,0:T(2,128)} %param.21) | copy-start | bytes 1540
  19.8 8.3 %copy-start = (bf16[256,1024]{1,0:T(8,128)(2,1)S(1)}, bf16[256,1024]{1,0:T(8,128)(2,1)}, u32[]{:S(2)}) copy-start(bf16[256,1024]{1,0:T(8,128)(2,1)} %inputs_ref.3) | copy-start | bytes 1572868
  19.8 8.3 %copy-start.3 = (bf16[2,32,256]{2,1,0:T(8,128)(2,1)S(1)}, bf16[2,32,256]{2,1,0:T(8,128)(2,1)}, u32[]{:S(2)}) copy-start(bf16[2,32,256]{2,1,0:T(8,128)(2,1)} %param.15) | copy-start | bytes 98308
  19.9 22.0 %copy-start.8 = (bf16[2,4,8192]{2,1,0:T(4,128)(2,1)S(1)}, bf16[2,4,8192]{2,1,0:T(4,128)(2,1)}, u32[]{:S(2)}) copy-start(bf16[2,4,8192]{2,1,0:T(4,128)(2,1)} %param.24) | copy-start | bytes 393220
  19.9 23.2 %copy-start.1 = (bf16[2,4,256,128]{3,2,1,0:T(8,128)(2,1)S(1)}, bf16[2,4,256,128]{3,2,1,0:T(8,128)(2,1)}, u32[]{:S(2)}) copy-start(bf16[2,4,256,128]{3,2,1,0:T(8,128)(2,1)} %key_ref.1) | copy-start | bytes 1572868
  19.9 23.2 %copy-start.2 = (bf16[2,4,256,128]{3,2,1,0:T(8,128)(2,1)S(1)}, bf16[2,4,256,128]{3,2,1,0:T(8,128)(2,1)}, u32[]{:S(2)}) copy-start(bf16[2,4,256,128]{3,2,1,0:T(8,128)(2,1)} %value_ref.1) | copy-start | bytes 1572868
  20.7 21.4 %collective-permute-start = (f32[2,2,2,8,1024]{4,3,0,2,1:T(8,128)}, f32[2,2,2,8,1024]{4,3,0,2,1:T(8,128)}, u32[]{:S(2)}, u32[]{:S(2)}) collective-permute-start(f32[2,2,2,8,1024]{4,3,0,2,1:T(8,128)} %get-tuple-element.57), channel_id=1, source_target_pairs={{0,1},{1,0},{2,3},{3,2},{4,5},{5,4},{6,7},{7,6},{8,9},{9,8},{10,11... | collective-permute-start | bytes 786440 | tf_op jit(solution)/shard_map/ppermute | solution.py:70
  29.1 22.6 %all-to-all-start.1 = ((bf16[16,16,256]{2,1,0:T(8,128)(2,1)}), bf16[16,16,256]{2,1,0:T(8,128)(2,1)S(1)}, u32[]{:S(2)}, u32[]{:S(2)}) async-start(bf16[16,16,256]{2,1,0:T(8,128)(2,1)} %bitcast.2), calls=%async_computation.1 | async-start | bytes 262144 | tf_op jit(solution)/shard_map/all_to_all | solution.py:52
  43.1 42.0 %copy-start.4 = (f32[2,2,1024]{2,1,0:T(2,128)S(1)}, f32[2,2,1024]{2,1,0:T(2,128)}, u32[]{:S(2)}) copy-start(f32[2,2,1024]{2,1,0:T(2,128)} %down_ref.3) | copy-start | bytes 49156
  43.2 42.0 %copy-start.5 = (f32[2,2,1024]{2,1,0:T(2,128)S(1)}, f32[2,2,1024]{2,1,0:T(2,128)}, u32[]{:S(2)}) copy-start(f32[2,2,1024]{2,1,0:T(2,128)} %down_first_ref.1) | copy-start | bytes 49156
  43.2 42.0 %copy-start.6 = (f32[2,2,1024]{2,1,0:T(2,128)S(1)}, f32[2,2,1024]{2,1,0:T(2,128)}, u32[]{:S(2)}) copy-start(f32[2,2,1024]{2,1,0:T(2,128)} %down_second_ref.1) | copy-start | bytes 49156
  52.4 14.1 %all-to-all-start.2 = ((bf16[16,16,256]{2,1,0:T(8,128)(2,1)}), bf16[16,16,256]{2,1,0:T(8,128)(2,1)S(1)}, u32[]{:S(2)}, u32[]{:S(2)}) async-start(bf16[16,16,256]{2,1,0:T(8,128)(2,1)} %shard_map.207), calls=%async_computation.2 | async-start | bytes 262144 | tf_op jit(solution)/shard_map/all_to_all | solution.py:52
  56.3 16.0 %collective-permute-start.1 = (f32[2,2,8,1024]{3,2,0,1:T(8,128)S(1)}, f32[2,2,8,1024]{3,2,0,1:T(8,128)S(1)}, u32[]{:S(2)}, u32[]{:S(2)}) collective-permute-start(f32[2,2,8,1024]{3,2,0,1:T(8,128)S(1)} %select_bitcast_fusion.2), channel_id=1, source_target_pairs={{0,4},{1,5},{2,6},{3,7},{4,0},{5,1},{6,2},{7,3},{8,12},{9,13},{10,... | collective-permute-start | bytes 393224 | tf_op jit(solution)/shard_map/ppermute | solution.py:70
  67.4 17.7 %all-to-all-start.3 = ((bf16[32,4,1152]{2,1,0:T(4,128)(2,1)}), bf16[32,4,1152]{2,1,0:T(4,128)(2,1)S(1)}, u32[]{:S(2)}, u32[]{:S(2)}) async-start(bf16[32,4,1152]{2,1,0:T(4,128)(2,1)} %shard_map.209), calls=%async_computation.3 | async-start | bytes 589824 | tf_op jit(solution)/shard_map/all_to_all | solution.py:52
  72.4 18.7 %collective-permute-start.2 = (bf16[2,8,1024]{2,1,0:T(8,128)(2,1)S(1)}, bf16[2,8,1024]{2,1,0:T(8,128)(2,1)S(1)}, u32[]{:S(2)}, u32[]{:S(2)}) collective-permute-start(bf16[2,8,1024]{2,1,0:T(8,128)(2,1)S(1)} %fusion.6), channel_id=1, source_target_pairs={{0,2},{1,3},{2,0},{3,1},{4,6},{5,7},{6,4},{7,5},{8,10},{9,11},{10,... | collective-permute-start | bytes 98312 | tf_op jit(solution)/shard_map/ppermute | solution.py:70
  86.1 16.9 %all-to-all-start.4 = ((bf16[32,4,1152]{2,1,0:T(4,128)(2,1)}), bf16[32,4,1152]{2,1,0:T(4,128)(2,1)S(1)}, u32[]{:S(2)}, u32[]{:S(2)}) async-start(bf16[32,4,1152]{2,1,0:T(4,128)(2,1)} %get-tuple-element.38), calls=%async_computation.4 | async-start | bytes 589824 | tf_op jit(solution)/shard_map/all_to_all | solution.py:52
  91.1 6.2 %collective-permute-start.3 = (f32[8,1024]{1,0:T(8,128)S(1)}, f32[8,1024]{1,0:T(8,128)S(1)}, u32[]{:S(2)}, u32[]{:S(2)}) collective-permute-start(f32[8,1024]{1,0:T(8,128)S(1)} %select_bitcast_fusion.4), channel_id=1, source_target_pairs={{0,8},{1,9},{2,10},{3,11},{4,12},{5,13},{6,14},{7,15},{8,0},{9,1},... | collective-permute-start | bytes 98312 | tf_op jit(solution)/shard_map/ppermute | solution.py:70
  104.0 17.1 %all-to-all-start.5 = ((bf16[16,48,128]{2,1,0:T(8,128)(2,1)}), bf16[16,48,128]{2,1,0:T(8,128)(2,1)S(1)}, u32[]{:S(2)}, u32[]{:S(2)}) async-start(bf16[16,48,128]{2,1,0:T(8,128)(2,1)} %shard_map.211), calls=%async_computation.5 | async-start | bytes 393216 | tf_op jit(solution)/shard_map/all_to_all | solution.py:52

commit v8 on v7

--- a/solution.py
+++ b/solution.py
@@ -112,6 +112,14 @@
         out_ref[group] = block
 
 
+def project_decode(inputs_ref, weights_ref, out_ref):
+    columns = weights_ref.shape[2]
+    for kind in range(weights_ref.shape[0]):
+        out_ref[:, kind * columns : (kind + 1) * columns] = jnp.dot(
+            inputs_ref[...], weights_ref[kind], preferred_element_type=jnp.float32
+        )
+
+
 def project_tokens(factors_ref, inputs_ref, cotangents_ref, out_ref):
     all_rows = factors_ref.shape[0]
     own_width = inputs_ref.shape[1]
@@ -151,12 +159,10 @@
     )
     lane_kind = lax.broadcasted_iota(jnp.int32, up.shape, 1) // (both // 2)
     up = jnp.where(lane_kind == kind_of_row(up.shape, own_rank), ADAPTER_SCALE * up, 0.0)
-    down = down.astype(jnp.bfloat16)
-    up = up.astype(jnp.bfloat16)
     for group in range(groups):
         rows = slice(group * own_rows, (group + 1) * own_rows)
-        out_ref[group, :, :own_width] = down[rows]
-        out_ref[group, :, own_width:] = up[rows]
+        out_ref[group, :, :own_width] = down[rows].astype(jnp.bfloat16)
+        out_ref[group, :, own_width:] = up[rows].astype(jnp.bfloat16)
 
 
 def update_factors(
@@ -374,9 +380,12 @@
         send_masters, sent, adapter_down_master, by_rank(adapter_up_master), limit=None
     )
     later_inputs = after(flat_inputs, masters)
-    frozen_part = jnp.concatenate(
-        [product("rd,dc->rc", later_inputs, frozen_weights[kind]) for kind in range(kinds)], axis=1
-    ).reshape(ranks, own_lines, kinds * columns)
+    frozen_part = call(
+        project_decode,
+        out((ranks * own_lines, kinds * columns), jnp.float32),
+        later_inputs,
+        frozen_weights,
+    )
     bits = ranks.bit_length() - 1
     frozen_part = frozen_part.reshape((2,) * bits + (own_lines, kinds * columns))
     factors = exchange(masters, "grp").reshape(all_rows, wide)

time: 124 us -> 123 us (level)
  matrix products: 3.08 us -> 0 us
  local copies, waits for them, and re-layouts: 1.77 us -> 4.24 us
    dot_general x2 -> x0, matrix products: 3.08 us -> none  [product(): return jnp.einsum(spec, left, right, preferred_element_type=jnp.float32)]
    unnamed x24, local copies, waits for them, and re-layouts: 0.08 us -> 1.65 us
    pallas_call x6 -> x7, Pallas kernels: 6.03 us -> 6.46 us  [call(): pl.pallas_call(kernel, out_shape=outs, in_specs=[pl.BlockSpec(memory_spac...]
  transfers between devices with their start and end apart: 10 -> 10, of which waited for: 7 -> 7; matrix products, arithmetic and copies ran while one was open for 7% -> 5% of each run, Pallas kernels for 4% -> 4%
where the time goes in v8:
time: 123 us; the launch traced here: 122 us
  starting transfers between devices  56.9 us (46%)
  waiting for transfers between devices  47.4 us (39%)
  Pallas kernels  9.7 us (8%)
  local copies, waits for them, and re-layouts  4.24 us (3%)
  other arithmetic  3.14 us (3%)
    all_to_all x6, starting transfers between devices, exchange(): return lax.all_to_all(pieces, axis, 0, 0, tiled=True)  45.9 us
    all_to_all x6, waiting for transfers between devices, exchange(): return lax.all_to_all(pieces, axis, 0, 0, tiled=True)  44.1 us
    ppermute x4, starting transfers between devices, half_sum(): lax.ppermute(jnp.where(upper, low, high).astype(kind), axis, pairs)  11 us
    pallas_call x7, Pallas kernels, call(): pl.pallas_call(kernel, out_shape=outs, in_specs=[pl.BlockSpec(memory_spac...  6.46 us
    ppermute x4, waiting for transfers between devices, half_sum(): lax.ppermute(jnp.where(upper, low, high).astype(kind), axis, pairs)  3.35 us
  transfers between devices with their start and end apart: 10, of which 7 were waited for; matrix products, arithmetic and copies ran while one was open for 5% of the time, Pallas kernels for 4%

profile of v8, /device:TPU:1, one launch (start us, length us, event | category | flops | bytes accessed | tf_op | source)
XLA Modules:
  0.0 122.4 jit_solution(2482375760201790024)
XLA Ops:
  0.6 1.5 %shard_map.205 = bf16[32,4,1152]{2,1,0:T(4,128)(2,1)} custom-call(f32[2,2,1024]{2,1,0:T(2,128)} %down_ref.3, f32[2,2,32]{2,1,0:T(2,128)} %bitcast.62), custom_call_target="tpu_custom_call" | custom-call | flops 16384 | bytes 16384 | tf_op jit(solution)/shard_map/pallas_call | solution.py:363
  2.2 13.5 %all-to-all-start = ((bf16[32,4,1152]{2,1,0:T(4,128)(2,1)}), bf16[32,4,1152]{2,1,0:T(4,128)(2,1)S(1)}, u32[]{:S(2)}, u32[]{:S(2)}) async-start(bf16[32,4,1152]{2,1,0:T(4,128)(2,1)} %shard_map.205), calls=%async_computation | async-start | bytes 589824 | tf_op jit(solution)/shard_map/all_to_all | solution.py:52
  15.6 1.0 reshape.108.inputs_ref
  16.7 0.0 copy-start
  16.7 1.6 %copy-done = bf16[2,1024,512]{2,1,0:T(8,128)(2,1)S(1)} copy-done((bf16[2,1024,512]{2,1,0:T(8,128)(2,1)S(1)}, bf16[2,1024,512]{2,1,0:T(8,128)(2,1)}, u32[]{:S(2)}) %copy-start) | copy-done | bytes 2097176
  18.3 0.4 shard_map.212
  18.8 0.0 copy-start.2
  18.8 0.8 select_bitcast_fusion
  19.6 2.9 %collective-permute-start = (f32[2,2,2,8,1024]{4,3,0,2,1:T(8,128)}, f32[2,2,2,8,1024]{4,3,0,2,1:T(8,128)S(1)}, u32[]{:S(2)}, u32[]{:S(2)}) collective-permute-start(f32[2,2,2,8,1024]{4,3,0,2,1:T(8,128)} %get-tuple-element.57), channel_id=1, source_target_pairs={{0,1},{1,0},{2,3},{3,2},{4,5},{5,4},{6,7},{7,6},{8,9},{9,8},{10,11... | collective-permute-start | bytes 786440 | tf_op jit(solution)/shard_map/ppermute | solution.py:70
  22.5 0.1 select_maximum_fusion.2.up_ref
  22.6 0.1 select_maximum_fusion.1.up_first_ref
  22.6 0.1 add_convert_fusion
  22.7 5.3 %all-to-all-done = bf16[32,4,1152]{2,1,0:T(4,128)(2,1)S(1)} async-done(((bf16[32,4,1152]{2,1,0:T(4,128)(2,1)}), bf16[32,4,1152]{2,1,0:T(4,128)(2,1)S(1)}, u32[]{:S(2)}, u32[]{:S(2)}) %all-to-all-start) | async-done | bytes 294944 | tf_op jit(solution)/shard_map/all_to_all | solution.py:52
  28.0 0.1 reshape.101.factors_ref
  28.1 1.0 shard_map.206
  29.1 12.5 %all-to-all-start.1 = ((bf16[16,16,256]{2,1,0:T(8,128)(2,1)}), bf16[16,16,256]{2,1,0:T(8,128)(2,1)S(1)}, u32[]{:S(2)}, u32[]{:S(2)}) async-start(bf16[16,16,256]{2,1,0:T(8,128)(2,1)} %bitcast.2), calls=%async_computation.1 | async-start | bytes 262144 | tf_op jit(solution)/shard_map/all_to_all | solution.py:52
  41.6 0.1 convert_element_type.31
  41.7 0.1 fusion.1
  41.8 1.1 reshape.104
  42.9 0.1 copy.24
  43.1 0.0 copy-start.5
  43.1 1.7 %shard_map.208 = (f32[4,128,1]{2,1,0:T(8,128)S(1)}, f32[4,128,1]{2,1,0:T(8,128)S(1)}, f32[4,128,128]{2,1,0:T(8,128)S(1)}) custom-call(s32[2]{0:T(128)S(1)} %copy-done.8, bf16[4,128,128]{2,1,0:T(8,128)(2,1)S(1)} %bitcast.57, bf16[2,4,256,128]{3,2,1,0:T(8,128)(2,1)S(1)} %copy-done.2, bf16[2,4,256,128]{3,2,1,0:T(8,128)(2,1)S(1)} %copy-done.3), custom_call_target="tpu_custom_call" | custom-call | flops 134217728 | bytes 1048576 | tf_op jit(solution)/shard_map/pallas_call | solution.py:403
  44.8 6.8 %all-to-all-done.1.parts_ref = bf16[16,16,256]{2,1,0:T(8,128)(2,1)S(1)} async-done(((bf16[16,16,256]{2,1,0:T(8,128)(2,1)}), bf16[16,16,256]{2,1,0:T(8,128)(2,1)S(1)}, u32[]{:S(2)}, u32[]{:S(2)}) %all-to-all-start.1) | async-done | bytes 131104 | tf_op jit(solution)/shard_map/all_to_all | solution.py:52
  51.7 0.7 shard_map.207
  52.3 4.0 %all-to-all-start.2 = ((bf16[16,16,256]{2,1,0:T(8,128)(2,1)}), bf16[16,16,256]{2,1,0:T(8,128)(2,1)S(1)}, u32[]{:S(2)}, u32[]{:S(2)}) async-start(bf16[16,16,256]{2,1,0:T(8,128)(2,1)} %shard_map.207), calls=%async_computation.2 | async-start | bytes 262144 | tf_op jit(solution)/shard_map/all_to_all | solution.py:52
  56.3 3.3 %collective-permute-start.1 = (f32[2,2,8,1024]{3,2,0,1:T(8,128)S(1)}, f32[2,2,8,1024]{3,2,0,1:T(8,128)S(1)}, u32[]{:S(2)}, u32[]{:S(2)}) collective-permute-start(f32[2,2,8,1024]{3,2,0,1:T(8,128)S(1)} %select_bitcast_fusion.2), channel_id=1, source_target_pairs={{0,4},{1,5},{2,6},{3,7},{4,0},{5,1},{6,2},{7,3},{8,12},{9,13},{10,... | collective-permute-start | bytes 393224 | tf_op jit(solution)/shard_map/ppermute | solution.py:70
  59.6 0.1 select_maximum_fusion.up_second_ref
  59.7 0.1 pad_maximum_fusion
  59.8 6.6 %all-to-all-done.2 = bf16[16,16,256]{2,1,0:T(8,128)(2,1)S(1)} async-done(((bf16[16,16,256]{2,1,0:T(8,128)(2,1)}), bf16[16,16,256]{2,1,0:T(8,128)(2,1)S(1)}, u32[]{:S(2)}, u32[]{:S(2)}) %all-to-all-start.2) | async-done | bytes 131104 | tf_op jit(solution)/shard_map/all_to_all | solution.py:52
  66.4 1.0 shard_map.209
  67.4 4.7 %all-to-all-start.3 = ((bf16[32,4,1152]{2,1,0:T(4,128)(2,1)}), bf16[32,4,1152]{2,1,0:T(4,128)(2,1)S(1)}, u32[]{:S(2)}, u32[]{:S(2)}) async-start(bf16[32,4,1152]{2,1,0:T(4,128)(2,1)} %shard_map.209), calls=%async_computation.3 | async-start | bytes 589824 | tf_op jit(solution)/shard_map/all_to_all | solution.py:52
  72.2 2.1 %collective-permute-start.2 = (bf16[2,8,1024]{2,1,0:T(8,128)(2,1)S(1)}, bf16[2,8,1024]{2,1,0:T(8,128)(2,1)S(1)}, u32[]{:S(2)}, u32[]{:S(2)}) collective-permute-start(bf16[2,8,1024]{2,1,0:T(8,128)(2,1)S(1)} %fusion), channel_id=1, source_target_pairs={{0,2},{1,3},{2,0},{3,1},{4,6},{5,7},{6,4},{7,5},{8,10},{9,11},{10,... | collective-permute-start | bytes 98312 | tf_op jit(solution)/shard_map/ppermute | solution.py:70
  74.3 10.6 %all-to-all-done.3.parts_ref = bf16[32,4,1152]{2,1,0:T(4,128)(2,1)S(1)} async-done(((bf16[32,4,1152]{2,1,0:T(4,128)(2,1)}), bf16[32,4,1152]{2,1,0:T(4,128)(2,1)S(1)}, u32[]{:S(2)}, u32[]{:S(2)}) %all-to-all-start.3) | async-done | bytes 294944 | tf_op jit(solution)/shard_map/all_to_all | solution.py:52
  84.9 0.9 shard_map.210
  85.9 4.9 %all-to-all-start.4 = ((bf16[32,4,1152]{2,1,0:T(4,128)(2,1)}), bf16[32,4,1152]{2,1,0:T(4,128)(2,1)S(1)}, u32[]{:S(2)}, u32[]{:S(2)}) async-start(bf16[32,4,1152]{2,1,0:T(4,128)(2,1)} %get-tuple-element.38), calls=%async_computation.4 | async-start | bytes 589824 | tf_op jit(solution)/shard_map/all_to_all | solution.py:52
  90.9 2.7 %collective-permute-start.3 = (f32[8,1024]{1,0:T(8,128)S(1)}, f32[8,1024]{1,0:T(8,128)S(1)}, u32[]{:S(2)}, u32[]{:S(2)}) collective-permute-start(f32[8,1024]{1,0:T(8,128)S(1)} %select_bitcast_fusion.4), channel_id=1, source_target_pairs={{0,8},{1,9},{2,10},{3,11},{4,12},{5,13},{6,14},{7,15},{8,0},{9,1},... | collective-permute-start | bytes 98312 | tf_op jit(solution)/shard_map/ppermute | solution.py:70
  93.6 0.1 slice_bitcast_fusion.7
  93.7 3.3 %collective-permute-done.3 = f32[8,1024]{1,0:T(8,128)S(1)} collective-permute-done((f32[8,1024]{1,0:T(8,128)S(1)}, f32[8,1024]{1,0:T(8,128)S(1)}, u32[]{:S(2)}, u32[]{:S(2)}) %collective-permute-start.3) | collective-permute-done | bytes 32800 | tf_op jit(solution)/shard_map/ppermute | solution.py:70
  97.0 5.7 %all-to-all-done.4 = bf16[32,4,1152]{2,1,0:T(4,128)(2,1)S(1)} async-done(((bf16[32,4,1152]{2,1,0:T(4,128)(2,1)}), bf16[32,4,1152]{2,1,0:T(4,128)(2,1)S(1)}, u32[]{:S(2)}, u32[]{:S(2)}) %all-to-all-start.4) | async-done | bytes 294944 | tf_op jit(solution)/shard_map/all_to_all | solution.py:52
  102.7 0.1 reshape.107.factors_ref
  102.8 0.9 shard_map.211
  103.7 6.3 %all-to-all-start.5 = ((bf16[16,48,128]{2,1,0:T(8,128)(2,1)}), bf16[16,48,128]{2,1,0:T(8,128)(2,1)S(1)}, u32[]{:S(2)}, u32[]{:S(2)}) async-start(bf16[16,48,128]{2,1,0:T(8,128)(2,1)} %shard_map.211), calls=%async_computation.5 | async-start | bytes 393216 | tf_op jit(solution)/shard_map/all_to_all | solution.py:52
  110.0 0.1 slice_bitcast_fusion.11
  110.1 0.6 maximum_bitcast_fusion
  110.7 0.6 maximum_bitcast_fusion.2
  111.3 0.6 maximum_bitcast_fusion.1
  111.9 9.0 %all-to-all-done.5.last_ref = bf16[16,48,128]{2,1,0:T(8,128)(2,1)S(1)} async-done(((bf16[16,48,128]{2,1,0:T(8,128)(2,1)}), bf16[16,48,128]{2,1,0:T(8,128)(2,1)S(1)}, u32[]{:S(2)}, u32[]{:S(2)}) %all-to-all-start.5) | async-done | bytes 196640 | tf_op jit(solution)/shard_map/all_to_all | solution.py:52
  120.8 1.5 %shard_map.213 = (f32[2,4,8192]{2,1,0:T(4,128)}, f32[2,4,512]{2,1,0:T(4,128)}, f32[2,4,512]{2,1,0:T(4,128)}) custom-call(bf16[16,48,128]{2,1,0:T(8,128)(2,1)S(1)} %all-to-all-done.5.last_ref, f32[8,1024]{1,0:T(8,128)S(1)} %bitcast_add_fusion.1.frozen_ref, f32[8,128]{1,0:T(8,128)S(1)} %get-tuple-element.78.cosine_ref, ...), custom_call_target="tpu_custom_call" | custom-call | flops 2097152 | bytes 262144 | tf_op jit(solution)/shard_map/pallas_call | solution.py:477
  (36 shorter events, 0.2 us)
Async XLA Ops:
  2.2 25.9 %all-to-all-start = ((bf16[32,4,1152]{2,1,0:T(4,128)(2,1)}), bf16[32,4,1152]{2,1,0:T(4,128)(2,1)S(1)}, u32[]{:S(2)}, u32[]{:S(2)}) async-start(bf16[32,4,1152]{2,1,0:T(4,128)(2,1)} %shard_map.205), calls=%async_computation | async-start | bytes 589824 | tf_op jit(solution)/shard_map/all_to_all | solution.py:52
  16.7 1.6 %copy-start = (bf16[2,1024,512]{2,1,0:T(8,128)(2,1)S(1)}, bf16[2,1024,512]{2,1,0:T(8,128)(2,1)}, u32[]{:S(2)}) copy-start(bf16[2,1024,512]{2,1,0:T(8,128)(2,1)} %weights_ref.1) | copy-start | bytes 6291460
  18.3 4.2 %copy-start.9 = (f32[2,32,2]{1,2,0:T(2,128)S(1)}, f32[2,32,2]{1,2,0:T(2,128)}, u32[]{:S(2)}) copy-start(f32[2,32,2]{1,2,0:T(2,128)} %param.17) | copy-start | bytes 1540
  18.3 4.2 %copy-start.10 = (f32[2,32,2]{1,2,0:T(2,128)S(1)}, f32[2,32,2]{1,2,0:T(2,128)}, u32[]{:S(2)}) copy-start(f32[2,32,2]{1,2,0:T(2,128)} %param.20) | copy-start | bytes 1540
  18.3 4.4 %copy-start.8 = (s32[2]{0:T(128)S(1)}, s32[2]{0:T(128)}, u32[]{:S(2)}) copy-start(s32[2]{0:T(128)} %lengths_ref.1) | copy-start | bytes 28
  18.3 4.4 %copy-start.11 = (f32[2,32,2]{1,2,0:T(2,128)S(1)}, f32[2,32,2]{1,2,0:T(2,128)}, u32[]{:S(2)}) copy-start(f32[2,32,2]{1,2,0:T(2,128)} %param.21) | copy-start | bytes 1540
  18.3 9.9 %copy-start.1 = (bf16[256,1024]{1,0:T(8,128)(2,1)S(1)}, bf16[256,1024]{1,0:T(8,128)(2,1)}, u32[]{:S(2)}) copy-start(bf16[256,1024]{1,0:T(8,128)(2,1)} %inputs_ref.3) | copy-start | bytes 1572868
  18.3 9.9 %copy-start.4 = (bf16[2,32,256]{2,1,0:T(8,128)(2,1)S(1)}, bf16[2,32,256]{2,1,0:T(8,128)(2,1)}, u32[]{:S(2)}) copy-start(bf16[2,32,256]{2,1,0:T(8,128)(2,1)} %param.15) | copy-start | bytes 98308
  18.8 24.3 %copy-start.2 = (bf16[2,4,256,128]{3,2,1,0:T(8,128)(2,1)S(1)}, bf16[2,4,256,128]{3,2,1,0:T(8,128)(2,1)}, u32[]{:S(2)}) copy-start(bf16[2,4,256,128]{3,2,1,0:T(8,128)(2,1)} %key_ref.1) | copy-start | bytes 1572868
  18.8 24.3 %copy-start.3 = (bf16[2,4,256,128]{3,2,1,0:T(8,128)(2,1)S(1)}, bf16[2,4,256,128]{3,2,1,0:T(8,128)(2,1)}, u32[]{:S(2)}) copy-start(bf16[2,4,256,128]{3,2,1,0:T(8,128)(2,1)} %value_ref.1) | copy-start | bytes 1572868
  19.6 23.5 %collective-permute-start = (f32[2,2,2,8,1024]{4,3,0,2,1:T(8,128)}, f32[2,2,2,8,1024]{4,3,0,2,1:T(8,128)S(1)}, u32[]{:S(2)}, u32[]{:S(2)}) collective-permute-start(f32[2,2,2,8,1024]{4,3,0,2,1:T(8,128)} %get-tuple-element.57), channel_id=1, source_target_pairs={{0,1},{1,0},{2,3},{3,2},{4,5},{5,4},{6,7},{7,6},{8,9},{9,8},{10,11... | collective-permute-start | bytes 786440 | tf_op jit(solution)/shard_map/ppermute | solution.py:70
  29.1 22.6 %all-to-all-start.1 = ((bf16[16,16,256]{2,1,0:T(8,128)(2,1)}), bf16[16,16,256]{2,1,0:T(8,128)(2,1)S(1)}, u32[]{:S(2)}, u32[]{:S(2)}) async-start(bf16[16,16,256]{2,1,0:T(8,128)(2,1)} %bitcast.2), calls=%async_computation.1 | async-start | bytes 262144 | tf_op jit(solution)/shard_map/all_to_all | solution.py:52
  43.1 41.8 %copy-start.5 = (f32[2,2,1024]{2,1,0:T(2,128)S(1)}, f32[2,2,1024]{2,1,0:T(2,128)}, u32[]{:S(2)}) copy-start(f32[2,2,1024]{2,1,0:T(2,128)} %down_ref.3) | copy-start | bytes 49156
  43.1 41.8 %copy-start.6 = (f32[2,2,1024]{2,1,0:T(2,128)S(1)}, f32[2,2,1024]{2,1,0:T(2,128)}, u32[]{:S(2)}) copy-start(f32[2,2,1024]{2,1,0:T(2,128)} %down_first_ref.1) | copy-start | bytes 49156
  43.1 41.8 %copy-start.7 = (f32[2,2,1024]{2,1,0:T(2,128)S(1)}, f32[2,2,1024]{2,1,0:T(2,128)}, u32[]{:S(2)}) copy-start(f32[2,2,1024]{2,1,0:T(2,128)} %down_second_ref.1) | copy-start | bytes 49156
  52.3 14.1 %all-to-all-start.2 = ((bf16[16,16,256]{2,1,0:T(8,128)(2,1)}), bf16[16,16,256]{2,1,0:T(8,128)(2,1)S(1)}, u32[]{:S(2)}, u32[]{:S(2)}) async-start(bf16[16,16,256]{2,1,0:T(8,128)(2,1)} %shard_map.207), calls=%async_computation.2 | async-start | bytes 262144 | tf_op jit(solution)/shard_map/all_to_all | solution.py:52
  56.3 15.8 %collective-permute-start.1 = (f32[2,2,8,1024]{3,2,0,1:T(8,128)S(1)}, f32[2,2,8,1024]{3,2,0,1:T(8,128)S(1)}, u32[]{:S(2)}, u32[]{:S(2)}) collective-permute-start(f32[2,2,8,1024]{3,2,0,1:T(8,128)S(1)} %select_bitcast_fusion.2), channel_id=1, source_target_pairs={{0,4},{1,5},{2,6},{3,7},{4,0},{5,1},{6,2},{7,3},{8,12},{9,13},{10,... | collective-permute-start | bytes 393224 | tf_op jit(solution)/shard_map/ppermute | solution.py:70
  67.4 17.5 %all-to-all-start.3 = ((bf16[32,4,1152]{2,1,0:T(4,128)(2,1)}), bf16[32,4,1152]{2,1,0:T(4,128)(2,1)S(1)}, u32[]{:S(2)}, u32[]{:S(2)}) async-start(bf16[32,4,1152]{2,1,0:T(4,128)(2,1)} %shard_map.209), calls=%async_computation.3 | async-start | bytes 589824 | tf_op jit(solution)/shard_map/all_to_all | solution.py:52
  72.2 18.6 %collective-permute-start.2 = (bf16[2,8,1024]{2,1,0:T(8,128)(2,1)S(1)}, bf16[2,8,1024]{2,1,0:T(8,128)(2,1)S(1)}, u32[]{:S(2)}, u32[]{:S(2)}) collective-permute-start(bf16[2,8,1024]{2,1,0:T(8,128)(2,1)S(1)} %fusion), channel_id=1, source_target_pairs={{0,2},{1,3},{2,0},{3,1},{4,6},{5,7},{6,4},{7,5},{8,10},{9,11},{10,... | collective-permute-start | bytes 98312 | tf_op jit(solution)/shard_map/ppermute | solution.py:70
  85.9 16.9 %all-to-all-start.4 = ((bf16[32,4,1152]{2,1,0:T(4,128)(2,1)}), bf16[32,4,1152]{2,1,0:T(4,128)(2,1)S(1)}, u32[]{:S(2)}, u32[]{:S(2)}) async-start(bf16[32,4,1152]{2,1,0:T(4,128)(2,1)} %get-tuple-element.38), calls=%async_computation.4 | async-start | bytes 589824 | tf_op jit(solution)/shard_map/all_to_all | solution.py:52
  90.9 6.2 %collective-permute-start.3 = (f32[8,1024]{1,0:T(8,128)S(1)}, f32[8,1024]{1,0:T(8,128)S(1)}, u32[]{:S(2)}, u32[]{:S(2)}) collective-permute-start(f32[8,1024]{1,0:T(8,128)S(1)} %select_bitcast_fusion.4), channel_id=1, source_target_pairs={{0,8},{1,9},{2,10},{3,11},{4,12},{5,13},{6,14},{7,15},{8,0},{9,1},... | collective-permute-start | bytes 98312 | tf_op jit(solution)/shard_map/ppermute | solution.py:70
  103.7 17.1 %all-to-all-start.5 = ((bf16[16,48,128]{2,1,0:T(8,128)(2,1)}), bf16[16,48,128]{2,1,0:T(8,128)(2,1)S(1)}, u32[]{:S(2)}, u32[]{:S(2)}) async-start(bf16[16,48,128]{2,1,0:T(8,128)(2,1)} %shard_map.211), calls=%async_computation.5 | async-start | bytes 393216 | tf_op jit(solution)/shard_map/all_to_all | solution.py:52

commit v9 on v8

--- a/solution.py
+++ b/solution.py
@@ -391,7 +391,7 @@
     factors = exchange(masters, "grp").reshape(all_rows, wide)
 
     frozen_part = half_sum(frozen_part, "tp", ranks, bits - 1, 0, earlier_sum=factors)
-    frozen_part = half_sum(frozen_part, "tp", ranks, 1, bits - 2)
+    frozen_part = half_sum(frozen_part, "tp", ranks, 1, bits - 2, kind=jnp.bfloat16)
 
     lines = query_width // (head_groups * head_size) * own_lines
     query_lines = (

time: 123 us -> 123 us (level)
  no operation moved by 1% of the time
where the time goes in v9:
time: 123 us; the launch traced here: 122 us
  starting transfers between devices  56.9 us (46%)
  waiting for transfers between devices  47.3 us (38%)
  Pallas kernels  9.75 us (8%)
  other arithmetic  4.09 us (3%)
  local copies, waits for them, and re-layouts  3.35 us (3%)
    all_to_all x6, starting transfers between devices, exchange(): return lax.all_to_all(pieces, axis, 0, 0, tiled=True)  45.8 us
    all_to_all x6, waiting for transfers between devices, exchange(): return lax.all_to_all(pieces, axis, 0, 0, tiled=True)  43.9 us
    ppermute x4, starting transfers between devices, half_sum(): lax.ppermute(jnp.where(upper, low, high).astype(kind), axis, pairs)  11 us
    pallas_call x7, Pallas kernels, call(): pl.pallas_call(kernel, out_shape=outs, in_specs=[pl.BlockSpec(memory_spac...  6.48 us
    ppermute x4, waiting for transfers between devices, half_sum(): lax.ppermute(jnp.where(upper, low, high).astype(kind), axis, pairs)  3.35 us
  transfers between devices with their start and end apart: 10, of which 7 were waited for; matrix products, arithmetic and copies ran while one was open for 5% of the time, Pallas kernels for 4%

profile of v9, /device:TPU:1, one launch (start us, length us, event | category | flops | bytes accessed | tf_op | source)
XLA Modules:
  0.0 122.3 jit_solution(2576856047621806603)
XLA Ops:
  0.6 1.5 %shard_map.205 = bf16[32,4,1152]{2,1,0:T(4,128)(2,1)} custom-call(f32[2,2,1024]{2,1,0:T(2,128)} %down_ref.3, f32[2,2,32]{2,1,0:T(2,128)} %bitcast.62), custom_call_target="tpu_custom_call" | custom-call | flops 16384 | bytes 16384 | tf_op jit(solution)/shard_map/pallas_call | solution.py:363
  2.2 13.5 %all-to-all-start = ((bf16[32,4,1152]{2,1,0:T(4,128)(2,1)}), bf16[32,4,1152]{2,1,0:T(4,128)(2,1)S(1)}, u32[]{:S(2)}, u32[]{:S(2)}) async-start(bf16[32,4,1152]{2,1,0:T(4,128)(2,1)} %shard_map.205), calls=%async_computation | async-start | bytes 589824 | tf_op jit(solution)/shard_map/all_to_all | solution.py:52
  15.6 1.0 reshape.109.inputs_ref
  16.7 0.0 copy-start
  16.7 1.6 %copy-done = bf16[2,1024,512]{2,1,0:T(8,128)(2,1)S(1)} copy-done((bf16[2,1024,512]{2,1,0:T(8,128)(2,1)S(1)}, bf16[2,1024,512]{2,1,0:T(8,128)(2,1)}, u32[]{:S(2)}) %copy-start) | copy-done | bytes 2097176
  18.3 0.4 shard_map.212
  18.7 0.0 copy-start.12
  18.8 0.8 select_bitcast_fusion
  19.6 2.9 %collective-permute-start = (f32[2,2,2,8,1024]{4,3,0,2,1:T(8,128)}, f32[2,2,2,8,1024]{4,3,0,2,1:T(8,128)}, u32[]{:S(2)}, u32[]{:S(2)}) collective-permute-start(f32[2,2,2,8,1024]{4,3,0,2,1:T(8,128)} %get-tuple-element.57), channel_id=1, source_target_pairs={{0,1},{1,0},{2,3},{3,2},{4,5},{5,4},{6,7},{7,6},{8,9},{9,8},{10,11... | collective-permute-start | bytes 786440 | tf_op jit(solution)/shard_map/ppermute | solution.py:70
  22.5 0.1 add_convert_fusion
  22.6 0.1 select_maximum_fusion.2.up_ref
  22.7 0.1 convert_element_type.43
  22.7 0.1 fusion.2
  22.9 0.1 pad_maximum_fusion
  22.9 5.1 %all-to-all-done = bf16[32,4,1152]{2,1,0:T(4,128)(2,1)S(1)} async-done(((bf16[32,4,1152]{2,1,0:T(4,128)(2,1)}), bf16[32,4,1152]{2,1,0:T(4,128)(2,1)S(1)}, u32[]{:S(2)}, u32[]{:S(2)}) %all-to-all-start) | async-done | bytes 294944 | tf_op jit(solution)/shard_map/all_to_all | solution.py:52
  28.0 0.1 reshape.102.factors_ref
  28.1 1.0 shard_map.206
  29.1 12.5 %all-to-all-start.1 = ((bf16[16,16,256]{2,1,0:T(8,128)(2,1)}), bf16[16,16,256]{2,1,0:T(8,128)(2,1)S(1)}, u32[]{:S(2)}, u32[]{:S(2)}) async-start(bf16[16,16,256]{2,1,0:T(8,128)(2,1)} %bitcast.2), calls=%async_computation.1 | async-start | bytes 262144 | tf_op jit(solution)/shard_map/all_to_all | solution.py:52
  41.6 0.1 select_maximum_fusion.1.up_first_ref
  41.7 0.2 reshape.105
  41.9 0.1 copy.24
  42.0 1.0 add.54
  43.0 1.7 %shard_map.208 = (f32[4,128,1]{2,1,0:T(8,128)S(1)}, f32[4,128,1]{2,1,0:T(8,128)S(1)}, f32[4,128,128]{2,1,0:T(8,128)S(1)}) custom-call(s32[2]{0:T(128)S(1)} %copy-done.8, bf16[4,128,128]{2,1,0:T(8,128)(2,1)S(1)} %bitcast.57, bf16[2,4,256,128]{3,2,1,0:T(8,128)(2,1)S(1)} %copy-done.2, bf16[2,4,256,128]{3,2,1,0:T(8,128)(2,1)S(1)} %copy-done.3), custom_call_target="tpu_custom_call" | custom-call | flops 134217728 | bytes 1048576 | tf_op jit(solution)/shard_map/pallas_call | solution.py:403
  44.8 6.9 %all-to-all-done.1.parts_ref = bf16[16,16,256]{2,1,0:T(8,128)(2,1)S(1)} async-done(((bf16[16,16,256]{2,1,0:T(8,128)(2,1)}), bf16[16,16,256]{2,1,0:T(8,128)(2,1)S(1)}, u32[]{:S(2)}, u32[]{:S(2)}) %all-to-all-start.1) | async-done | bytes 131104 | tf_op jit(solution)/shard_map/all_to_all | solution.py:52
  51.7 0.7 shard_map.207
  52.4 4.0 %all-to-all-start.2 = ((bf16[16,16,256]{2,1,0:T(8,128)(2,1)}), bf16[16,16,256]{2,1,0:T(8,128)(2,1)S(1)}, u32[]{:S(2)}, u32[]{:S(2)}) async-start(bf16[16,16,256]{2,1,0:T(8,128)(2,1)} %shard_map.207), calls=%async_computation.2 | async-start | bytes 262144 | tf_op jit(solution)/shard_map/all_to_all | solution.py:52
  56.3 3.3 %collective-permute-start.1 = (bf16[2,2,8,1024]{3,2,0,1:T(8,128)(2,1)S(1)}, bf16[2,2,8,1024]{3,2,0,1:T(8,128)(2,1)S(1)}, u32[]{:S(2)}, u32[]{:S(2)}) collective-permute-start(bf16[2,2,8,1024]{3,2,0,1:T(8,128)(2,1)S(1)} %fusion), channel_id=1, source_target_pairs={{0,4},{1,5},{2,6},{3,7},{4,0},{5,1},{6,2},{7,3},{8,12},{9,13},{10,... | collective-permute-start | bytes 196616 | tf_op jit(solution)/shard_map/ppermute | solution.py:70
  59.7 0.1 select_maximum_fusion.up_second_ref
  59.7 6.7 %all-to-all-done.2 = bf16[16,16,256]{2,1,0:T(8,128)(2,1)S(1)} async-done(((bf16[16,16,256]{2,1,0:T(8,128)(2,1)}), bf16[16,16,256]{2,1,0:T(8,128)(2,1)S(1)}, u32[]{:S(2)}, u32[]{:S(2)}) %all-to-all-start.2) | async-done | bytes 131104 | tf_op jit(solution)/shard_map/all_to_all | solution.py:52
  66.5 1.0 shard_map.209
  67.5 4.7 %all-to-all-start.3 = ((bf16[32,4,1152]{2,1,0:T(4,128)(2,1)}), bf16[32,4,1152]{2,1,0:T(4,128)(2,1)S(1)}, u32[]{:S(2)}, u32[]{:S(2)}) async-start(bf16[32,4,1152]{2,1,0:T(4,128)(2,1)} %shard_map.209), calls=%async_computation.3 | async-start | bytes 589824 | tf_op jit(solution)/shard_map/all_to_all | solution.py:52
  72.2 2.1 %collective-permute-start.2 = (bf16[2,8,1024]{2,1,0:T(8,128)(2,1)S(1)}, bf16[2,8,1024]{2,1,0:T(8,128)(2,1)S(1)}, u32[]{:S(2)}, u32[]{:S(2)}) collective-permute-start(bf16[2,8,1024]{2,1,0:T(8,128)(2,1)S(1)} %fusion.1), channel_id=1, source_target_pairs={{0,2},{1,3},{2,0},{3,1},{4,6},{5,7},{6,4},{7,5},{8,10},{9,11},{10,... | collective-permute-start | bytes 98312 | tf_op jit(solution)/shard_map/ppermute | solution.py:70
  74.3 10.6 %all-to-all-done.3.parts_ref = bf16[32,4,1152]{2,1,0:T(4,128)(2,1)S(1)} async-done(((bf16[32,4,1152]{2,1,0:T(4,128)(2,1)}), bf16[32,4,1152]{2,1,0:T(4,128)(2,1)S(1)}, u32[]{:S(2)}, u32[]{:S(2)}) %all-to-all-start.3) | async-done | bytes 294944 | tf_op jit(solution)/shard_map/all_to_all | solution.py:52
  85.0 0.9 shard_map.210
  85.9 4.9 %all-to-all-start.4 = ((bf16[32,4,1152]{2,1,0:T(4,128)(2,1)}), bf16[32,4,1152]{2,1,0:T(4,128)(2,1)S(1)}, u32[]{:S(2)}, u32[]{:S(2)}) async-start(bf16[32,4,1152]{2,1,0:T(4,128)(2,1)} %get-tuple-element.38), calls=%async_computation.4 | async-start | bytes 589824 | tf_op jit(solution)/shard_map/all_to_all | solution.py:52
  90.9 2.7 %collective-permute-start.3 = (f32[8,1024]{1,0:T(8,128)S(1)}, f32[8,1024]{1,0:T(8,128)S(1)}, u32[]{:S(2)}, u32[]{:S(2)}) collective-permute-start(f32[8,1024]{1,0:T(8,128)S(1)} %select_bitcast_fusion.3), channel_id=1, source_target_pairs={{0,8},{1,9},{2,10},{3,11},{4,12},{5,13},{6,14},{7,15},{8,0},{9,1},... | collective-permute-start | bytes 98312 | tf_op jit(solution)/shard_map/ppermute | solution.py:70
  93.6 0.1 slice_bitcast_fusion.7
  93.7 3.3 %collective-permute-done.3 = f32[8,1024]{1,0:T(8,128)S(1)} collective-permute-done((f32[8,1024]{1,0:T(8,128)S(1)}, f32[8,1024]{1,0:T(8,128)S(1)}, u32[]{:S(2)}, u32[]{:S(2)}) %collective-permute-start.3) | collective-permute-done | bytes 32800 | tf_op jit(solution)/shard_map/ppermute | solution.py:70
  97.1 5.7 %all-to-all-done.4 = bf16[32,4,1152]{2,1,0:T(4,128)(2,1)S(1)} async-done(((bf16[32,4,1152]{2,1,0:T(4,128)(2,1)}), bf16[32,4,1152]{2,1,0:T(4,128)(2,1)S(1)}, u32[]{:S(2)}, u32[]{:S(2)}) %all-to-all-start.4) | async-done | bytes 294944 | tf_op jit(solution)/shard_map/all_to_all | solution.py:52
  102.7 0.1 reshape.108.factors_ref
  102.8 0.9 shard_map.211
  103.8 6.3 %all-to-all-start.5 = ((bf16[16,48,128]{2,1,0:T(8,128)(2,1)}), bf16[16,48,128]{2,1,0:T(8,128)(2,1)S(1)}, u32[]{:S(2)}, u32[]{:S(2)}) async-start(bf16[16,48,128]{2,1,0:T(8,128)(2,1)} %shard_map.211), calls=%async_computation.5 | async-start | bytes 393216 | tf_op jit(solution)/shard_map/all_to_all | solution.py:52
  110.1 0.1 slice_bitcast_fusion.11
  110.1 0.6 maximum_bitcast_fusion
  110.7 0.6 maximum_bitcast_fusion.2
  111.3 0.6 maximum_bitcast_fusion.1
  111.9 8.9 %all-to-all-done.5.last_ref = bf16[16,48,128]{2,1,0:T(8,128)(2,1)S(1)} async-done(((bf16[16,48,128]{2,1,0:T(8,128)(2,1)}), bf16[16,48,128]{2,1,0:T(8,128)(2,1)S(1)}, u32[]{:S(2)}, u32[]{:S(2)}) %all-to-all-start.5) | async-done | bytes 196640 | tf_op jit(solution)/shard_map/all_to_all | solution.py:52
  120.8 1.5 %shard_map.213 = (f32[2,4,8192]{2,1,0:T(4,128)}, f32[2,4,512]{2,1,0:T(4,128)}, f32[2,4,512]{2,1,0:T(4,128)}) custom-call(bf16[16,48,128]{2,1,0:T(8,128)(2,1)S(1)} %all-to-all-done.5.last_ref, f32[8,1024]{1,0:T(8,128)S(1)} %bitcast_add_fusion.1.frozen_ref, f32[8,128]{1,0:T(8,128)S(1)} %get-tuple-element.78.cosine_ref, ...), custom_call_target="tpu_custom_call" | custom-call | flops 2097152 | bytes 262144 | tf_op jit(solution)/shard_map/pallas_call | solution.py:477
  (38 shorter events, 0.2 us)
Async XLA Ops:
  2.2 25.9 %all-to-all-start = ((bf16[32,4,1152]{2,1,0:T(4,128)(2,1)}), bf16[32,4,1152]{2,1,0:T(4,128)(2,1)S(1)}, u32[]{:S(2)}, u32[]{:S(2)}) async-start(bf16[32,4,1152]{2,1,0:T(4,128)(2,1)} %shard_map.205), calls=%async_computation | async-start | bytes 589824 | tf_op jit(solution)/shard_map/all_to_all | solution.py:52
  16.7 1.6 %copy-start = (bf16[2,1024,512]{2,1,0:T(8,128)(2,1)S(1)}, bf16[2,1024,512]{2,1,0:T(8,128)(2,1)}, u32[]{:S(2)}) copy-start(bf16[2,1024,512]{2,1,0:T(8,128)(2,1)} %weights_ref.1) | copy-start | bytes 6291460
  18.2 4.2 %copy-start.10 = (f32[2,32,2]{1,2,0:T(2,128)S(1)}, f32[2,32,2]{1,2,0:T(2,128)}, u32[]{:S(2)}) copy-start(f32[2,32,2]{1,2,0:T(2,128)} %param.17) | copy-start | bytes 1540
  18.3 4.2 %copy-start.8 = (s32[2]{0:T(128)S(1)}, s32[2]{0:T(128)}, u32[]{:S(2)}) copy-start(s32[2]{0:T(128)} %lengths_ref.1) | copy-start | bytes 28
  18.3 4.7 %copy-start.11 = (f32[2,32,2]{1,2,0:T(2,128)S(1)}, f32[2,32,2]{1,2,0:T(2,128)}, u32[]{:S(2)}) copy-start(f32[2,32,2]{1,2,0:T(2,128)} %param.20) | copy-start | bytes 1540
  18.7 9.4 %copy-start.1 = (bf16[256,1024]{1,0:T(8,128)(2,1)S(1)}, bf16[256,1024]{1,0:T(8,128)(2,1)}, u32[]{:S(2)}) copy-start(bf16[256,1024]{1,0:T(8,128)(2,1)} %inputs_ref.3) | copy-start | bytes 1572868
  18.7 9.4 %copy-start.4 = (bf16[2,32,256]{2,1,0:T(8,128)(2,1)S(1)}, bf16[2,32,256]{2,1,0:T(8,128)(2,1)}, u32[]{:S(2)}) copy-start(bf16[2,32,256]{2,1,0:T(8,128)(2,1)} %param.15) | copy-start | bytes 98308
  18.7 23.0 %copy-start.12 = (f32[2,32,2]{1,2,0:T(2,128)S(1)}, f32[2,32,2]{1,2,0:T(2,128)}, u32[]{:S(2)}) copy-start(f32[2,32,2]{1,2,0:T(2,128)} %param.21) | copy-start | bytes 1540
  18.7 23.0 %copy-start.9 = (bf16[2,4,8192]{2,1,0:T(4,128)(2,1)S(1)}, bf16[2,4,8192]{2,1,0:T(4,128)(2,1)}, u32[]{:S(2)}) copy-start(bf16[2,4,8192]{2,1,0:T(4,128)(2,1)} %param.24) | copy-start | bytes 393220
  18.8 24.2 %copy-start.2 = (bf16[2,4,256,128]{3,2,1,0:T(8,128)(2,1)S(1)}, bf16[2,4,256,128]{3,2,1,0:T(8,128)(2,1)}, u32[]{:S(2)}) copy-start(bf16[2,4,256,128]{3,2,1,0:T(8,128)(2,1)} %key_ref.1) | copy-start | bytes 1572868
  18.8 24.2 %copy-start.3 = (bf16[2,4,256,128]{3,2,1,0:T(8,128)(2,1)S(1)}, bf16[2,4,256,128]{3,2,1,0:T(8,128)(2,1)}, u32[]{:S(2)}) copy-start(bf16[2,4,256,128]{3,2,1,0:T(8,128)(2,1)} %value_ref.1) | copy-start | bytes 1572868
  19.6 22.4 %collective-permute-start = (f32[2,2,2,8,1024]{4,3,0,2,1:T(8,128)}, f32[2,2,2,8,1024]{4,3,0,2,1:T(8,128)}, u32[]{:S(2)}, u32[]{:S(2)}) collective-permute-start(f32[2,2,2,8,1024]{4,3,0,2,1:T(8,128)} %get-tuple-element.57), channel_id=1, source_target_pairs={{0,1},{1,0},{2,3},{3,2},{4,5},{5,4},{6,7},{7,6},{8,9},{9,8},{10,11... | collective-permute-start | bytes 786440 | tf_op jit(solution)/shard_map/ppermute | solution.py:70
  29.1 22.6 %all-to-all-start.1 = ((bf16[16,16,256]{2,1,0:T(8,128)(2,1)}), bf16[16,16,256]{2,1,0:T(8,128)(2,1)S(1)}, u32[]{:S(2)}, u32[]{:S(2)}) async-start(bf16[16,16,256]{2,1,0:T(8,128)(2,1)} %bitcast.2), calls=%async_computation.1 | async-start | bytes 262144 | tf_op jit(solution)/shard_map/all_to_all | solution.py:52
  43.0 41.9 %copy-start.5 = (f32[2,2,1024]{2,1,0:T(2,128)S(1)}, f32[2,2,1024]{2,1,0:T(2,128)}, u32[]{:S(2)}) copy-start(f32[2,2,1024]{2,1,0:T(2,128)} %down_ref.3) | copy-start | bytes 49156
  43.0 41.9 %copy-start.6 = (f32[2,2,1024]{2,1,0:T(2,128)S(1)}, f32[2,2,1024]{2,1,0:T(2,128)}, u32[]{:S(2)}) copy-start(f32[2,2,1024]{2,1,0:T(2,128)} %down_first_ref.1) | copy-start | bytes 49156
  43.0 41.9 %copy-start.7 = (f32[2,2,1024]{2,1,0:T(2,128)S(1)}, f32[2,2,1024]{2,1,0:T(2,128)}, u32[]{:S(2)}) copy-start(f32[2,2,1024]{2,1,0:T(2,128)} %down_second_ref.1) | copy-start | bytes 49156
  52.4 14.1 %all-to-all-start.2 = ((bf16[16,16,256]{2,1,0:T(8,128)(2,1)}), bf16[16,16,256]{2,1,0:T(8,128)(2,1)S(1)}, u32[]{:S(2)}, u32[]{:S(2)}) async-start(bf16[16,16,256]{2,1,0:T(8,128)(2,1)} %shard_map.207), calls=%async_computation.2 | async-start | bytes 262144 | tf_op jit(solution)/shard_map/all_to_all | solution.py:52
  56.3 15.8 %collective-permute-start.1 = (bf16[2,2,8,1024]{3,2,0,1:T(8,128)(2,1)S(1)}, bf16[2,2,8,1024]{3,2,0,1:T(8,128)(2,1)S(1)}, u32[]{:S(2)}, u32[]{:S(2)}) collective-permute-start(bf16[2,2,8,1024]{3,2,0,1:T(8,128)(2,1)S(1)} %fusion), channel_id=1, source_target_pairs={{0,4},{1,5},{2,6},{3,7},{4,0},{5,1},{6,2},{7,3},{8,12},{9,13},{10,... | collective-permute-start | bytes 196616 | tf_op jit(solution)/shard_map/ppermute | solution.py:70
  67.5 17.5 %all-to-all-start.3 = ((bf16[32,4,1152]{2,1,0:T(4,128)(2,1)}), bf16[32,4,1152]{2,1,0:T(4,128)(2,1)S(1)}, u32[]{:S(2)}, u32[]{:S(2)}) async-start(bf16[32,4,1152]{2,1,0:T(4,128)(2,1)} %shard_map.209), calls=%async_computation.3 | async-start | bytes 589824 | tf_op jit(solution)/shard_map/all_to_all | solution.py:52
  72.2 18.7 %collective-permute-start.2 = (bf16[2,8,1024]{2,1,0:T(8,128)(2,1)S(1)}, bf16[2,8,1024]{2,1,0:T(8,128)(2,1)S(1)}, u32[]{:S(2)}, u32[]{:S(2)}) collective-permute-start(bf16[2,8,1024]{2,1,0:T(8,128)(2,1)S(1)} %fusion.1), channel_id=1, source_target_pairs={{0,2},{1,3},{2,0},{3,1},{4,6},{5,7},{6,4},{7,5},{8,10},{9,11},{10,... | collective-permute-start | bytes 98312 | tf_op jit(solution)/shard_map/ppermute | solution.py:70
  85.9 16.9 %all-to-all-start.4 = ((bf16[32,4,1152]{2,1,0:T(4,128)(2,1)}), bf16[32,4,1152]{2,1,0:T(4,128)(2,1)S(1)}, u32[]{:S(2)}, u32[]{:S(2)}) async-start(bf16[32,4,1152]{2,1,0:T(4,128)(2,1)} %get-tuple-element.38), calls=%async_computation.4 | async-start | bytes 589824 | tf_op jit(solution)/shard_map/all_to_all | solution.py:52
  90.9 6.2 %collective-permute-start.3 = (f32[8,1024]{1,0:T(8,128)S(1)}, f32[8,1024]{1,0:T(8,128)S(1)}, u32[]{:S(2)}, u32[]{:S(2)}) collective-permute-start(f32[8,1024]{1,0:T(8,128)S(1)} %select_bitcast_fusion.3), channel_id=1, source_target_pairs={{0,8},{1,9},{2,10},{3,11},{4,12},{5,13},{6,14},{7,15},{8,0},{9,1},... | collective-permute-start | bytes 98312 | tf_op jit(solution)/shard_map/ppermute | solution.py:70
  103.8 17.0 %all-to-all-start.5 = ((bf16[16,48,128]{2,1,0:T(8,128)(2,1)}), bf16[16,48,128]{2,1,0:T(8,128)(2,1)S(1)}, u32[]{:S(2)}, u32[]{:S(2)}) async-start(bf16[16,48,128]{2,1,0:T(8,128)(2,1)} %shard_map.211), calls=%async_computation.5 | async-start | bytes 393216 | tf_op jit(solution)/shard_map/all_to_all | solution.py:52
